TPU v7x, 32 devices: a whole 2x2x4 slice. The times are simulated.
32 devices in a mesh: dp: 8 (over z, x), seq: 4 (over y, core).
Axes of the slice: x: 2, y: 2, z: 4, core: 2. Of those that a mesh axis runs over, the one named last changes fastest.
Arguments:
- inputs: bfloat16 [16, 1024, 1152], P('dp', 'seq'), may hold values from -6 to 6
- segments: int32 [16, 1024], P('dp', 'seq'), may hold values from 0 to 4, as said below
- query_weight: bfloat16 [1152, 1024], P(None, ('dp', 'seq')), may hold values from -0.1875 to 0.1875
- key_weight: bfloat16 [1152, 256], P(None, ('dp', 'seq')), may hold values from -0.1875 to 0.1875
- value_weight: bfloat16 [1152, 256], P(None, ('dp', 'seq')), may hold values from -0.1875 to 0.1875
- out_weight: bfloat16 [1024, 1152], P(('dp', 'seq')), may hold values from -0.1875 to 0.1875
- gate_weight: bfloat16 [1152, 6912], P(None, ('dp', 'seq')), may hold values from -0.1875 to 0.1875
- up_weight: bfloat16 [1152, 6912], P(None, ('dp', 'seq')), may hold values from -0.1875 to 0.1875
- down_weight: bfloat16 [6912, 1152], P(('dp', 'seq')), may hold values from -0.078125 to 0.078125
- input_gain: float32 [1152], replicated, may hold values from -0.9 to 0.9
- attention_gain: float32 [1152], replicated, may hold values from -0.9 to 0.9
- feed_gain: float32 [1152], replicated, may hold values from -0.9 to 0.9
- output_gain: float32 [1152], replicated, may hold values from -0.9 to 0.9
- query_gain: float32 [256], replicated, may hold values from -0.9 to 0.9
- key_gain: float32 [256], replicated, may hold values from -0.9 to 0.9
- cotangent: bfloat16 [16, 1024, 1152], P('dp', 'seq'), may hold values from -6 to 6
Outputs:
- output: bfloat16 [16, 1024, 1152], P('dp', 'seq')
- grad_inputs: float32 [16, 1024, 1152], P('dp', 'seq')
- grad_query_weight: float32 [1152, 1024], P(None, ('dp', 'seq'))
- grad_key_weight: float32 [1152, 256], P(None, ('dp', 'seq'))
- grad_value_weight: float32 [1152, 256], P(None, ('dp', 'seq'))
- grad_out_weight: float32 [1024, 1152], P(('dp', 'seq'))
- grad_gate_weight: float32 [1152, 6912], P(None, ('dp', 'seq'))
- grad_up_weight: float32 [1152, 6912], P(None, ('dp', 'seq'))
- grad_down_weight: float32 [6912, 1152], P(('dp', 'seq'))
- grad_input_gain: float32 [1152], replicated
- grad_attention_gain: float32 [1152], replicated
- grad_feed_gain: float32 [1152], replicated
- grad_output_gain: float32 [1152], replicated
- grad_query_gain: float32 [256], replicated
- grad_key_gain: float32 [256], replicated
Inputs may be any that keep to these rules, and one draw needn't show every extreme that they name: `segments`: in each sequence the ids start at 0 at the first token and rise by 0 or 1 from one token to the next, never above 4, which every draw reaches. Of the 2 sequences of each index of dp, one keeps a single id from token 128 to token 895.
All inputs are finite; a program needn't handle non-finite values.
Results may differ from a plain program's by a relative error of at most 0.017.
Values may be sent and summed in bfloat16 or wider, within the bound.
No kernel may reach another device: no remote copies, remote signals or barrier semaphores. Data moves between devices by JAX's collectives and lax.ppermute only.
A program may use at most 512 MiB of HBM per device.

v0:
```python
import jax
import jax.numpy as jnp
from jax import lax
from jax.sharding import PartitionSpec as P

HEADS = 4
FF = 6912
WINDOW = 512


epsilon = 1e-06


def passed_along(value, axis, steps):
    count = lax.axis_size(axis)
    leading, last = (max(0, -steps), min(count, count - steps))
    return lax.ppermute(value, axis, [(source, source + steps) for source in range(leading, last)])


def rms_scale(values, gain):
    mean_square = jnp.mean(values * values, axis=-1, keepdims=True)
    return values * lax.rsqrt(mean_square + epsilon) * (1.0 + gain)


def rope_tables(positions, width):
    steps = jnp.arange(width // 2, dtype=jnp.float32)
    inverse = 10000.0 ** (-2.0 * steps / width)
    angles = positions.astype(jnp.float32)[:, None] * inverse[None, :]
    doubled = jnp.concatenate([angles, angles], axis=-1)
    return (jnp.cos(doubled), jnp.sin(doubled))


def rotate(values, cosine, sine):
    half = values.shape[-1] // 2
    turned = jnp.concatenate([-values[..., half:], values[..., :half]], axis=-1)
    return values * cosine + turned * sine


def geglu(gate, upward):
    return jax.nn.gelu(gate, approximate=True) * upward


def matmul(left, right):
    return jnp.dot(left, right, preferred_element_type=jnp.float32)


def left_product(left, right):
    return lax.dot_general(
        left, right, (((0,), (0,)), ((), ())), preferred_element_type=jnp.float32
    )


def right_product(left, right):
    return lax.dot_general(
        left, right, (((1,), (1,)), ((), ())), preferred_element_type=jnp.float32
    )


def on_device(
    inputs,
    segments,
    query_weight,
    key_weight,
    value_weight,
    out_weight,
    gate_weight,
    up_weight,
    down_weight,
    input_gain,
    attention_gain,
    feed_gain,
    output_gain,
    query_gain,
    key_gain,
    cotangent,
):
    micro, length, width = inputs.shape
    head_size = query_gain.shape[0]
    heads = HEADS
    scale = 1.0 / jnp.sqrt(jnp.float32(head_size))
    seq_count = lax.axis_size("seq")
    hops = min((WINDOW + length - 2) // length, seq_count - 1)
    seq_index = lax.axis_index("seq")
    shards = (
        query_weight,
        key_weight,
        value_weight,
        out_weight,
        gate_weight,
        up_weight,
        down_weight,
    )
    positions = seq_index * length + jnp.arange(length, dtype=jnp.int32)
    cosine, sine = rope_tables(positions, head_size)

    def shape_query(projected, gain):
        return rotate(
            rms_scale(projected.reshape(length, heads, head_size), gain),
            cosine[:, None, :],
            sine[:, None, :],
        )

    def shape_key(projected, gain):
        return rotate(rms_scale(projected, gain), cosine, sine)

    key_count = (hops + 1) * length
    key_pos = seq_index * length - hops * length + jnp.arange(key_count, dtype=jnp.int32)
    query_pos = jnp.broadcast_to(positions[:, None], (length, heads)).reshape(length * heads)

    def block_scores(query, keys, row_seg, column_seg):
        scores = right_product(query, keys) * scale
        allowed = (key_pos[None, :] >= 0) & (key_pos[None, :] <= query_pos[:, None])
        allowed = allowed & (query_pos[:, None] - key_pos[None, :] < WINDOW)
        allowed = allowed & (column_seg[None, :] == row_seg[:, None])
        return (scores, allowed)

    def one_micro(totals, item):
        seq_inputs, seq_segment, seq_cot = item
        weights = (
            lax.all_gather(shards[0], ("dp", "seq"), axis=1, tiled=True),
            lax.all_gather(shards[1], ("dp", "seq"), axis=1, tiled=True),
            lax.all_gather(shards[2], ("dp", "seq"), axis=1, tiled=True),
            lax.all_gather(shards[3], ("dp", "seq"), axis=0, tiled=True),
            lax.all_gather(shards[4], ("dp", "seq"), axis=1, tiled=True),
            lax.all_gather(shards[5], ("dp", "seq"), axis=1, tiled=True),
            lax.all_gather(shards[6], ("dp", "seq"), axis=0, tiled=True),
        )
        full_query, full_key, full_value, full_out, full_gate, full_up, full_down = weights
        source = seq_inputs.astype(jnp.float32)
        normed = rms_scale(source, input_gain).astype(jnp.bfloat16)
        query_proj = matmul(normed, full_query)
        key_proj = matmul(normed, full_key)
        value_low = matmul(normed, full_value).astype(jnp.bfloat16)
        query_low = (
            shape_query(query_proj, query_gain)
            .astype(jnp.bfloat16)
            .reshape(length * heads, head_size)
        )
        key_low = shape_key(key_proj, key_gain).astype(jnp.bfloat16)
        own_block = jnp.concatenate([key_low, value_low], axis=-1)
        key_blocks = [own_block]
        seg_blocks = [seq_segment]
        carried = (own_block, seq_segment)
        for hop in range(hops):
            carried = passed_along((carried[0], carried[1]), "seq", 1)
            key_blocks.insert(0, carried[0])
            seg_blocks.insert(0, carried[1])
        all_keys = jnp.concatenate(key_blocks, axis=0)
        key_seg = jnp.concatenate(seg_blocks, axis=0)
        keys_only = all_keys[:, :head_size]
        values_only = all_keys[:, head_size:]
        query_seg = jnp.broadcast_to(seq_segment[:, None], (length, heads)).reshape(length * heads)
        scores, allowed = block_scores(query_low, keys_only, query_seg, key_seg)
        masked = jnp.where(allowed, scores, -1e30)
        highest = jnp.max(masked, axis=-1, keepdims=True)
        expo = jnp.exp(masked - highest)
        total = jnp.sum(expo, axis=-1, keepdims=True)
        probs_low = (expo / total).astype(jnp.bfloat16)
        mixed_rows = matmul(probs_low, values_only).astype(jnp.bfloat16)
        log_total = (highest + jnp.log(total))[:, 0]
        mixed_flat = mixed_rows.reshape(length, heads * head_size)
        attended = matmul(mixed_flat, full_out)
        hidden = source + rms_scale(attended, attention_gain)
        prenorm = rms_scale(hidden, feed_gain).astype(jnp.bfloat16)
        gate = matmul(prenorm, full_gate)
        upward = matmul(prenorm, full_up)
        product = geglu(gate, upward).astype(jnp.bfloat16)
        down = matmul(product, full_down)
        result = hidden + rms_scale(down, output_gain)
        output = result.astype(jnp.bfloat16)
        full_query, full_key, full_value, full_out, full_gate, full_up, full_down = (
            lax.all_gather(shards[0], ("dp", "seq"), axis=1, tiled=True),
            lax.all_gather(shards[1], ("dp", "seq"), axis=1, tiled=True),
            lax.all_gather(shards[2], ("dp", "seq"), axis=1, tiled=True),
            lax.all_gather(shards[3], ("dp", "seq"), axis=0, tiled=True),
            lax.all_gather(shards[4], ("dp", "seq"), axis=1, tiled=True),
            lax.all_gather(shards[5], ("dp", "seq"), axis=1, tiled=True),
            lax.all_gather(shards[6], ("dp", "seq"), axis=0, tiled=True),
        )
        grad_result = seq_cot.astype(jnp.float32)
        _, pull_output = jax.vjp(rms_scale, down, output_gain)
        grad_down, grad_output_gain = pull_output(grad_result)
        grad_down_low = grad_down.astype(jnp.bfloat16)
        grad_down_weight = left_product(product, grad_down_low)
        grad_product = right_product(grad_down_low, full_down)
        _, pull_geglu = jax.vjp(geglu, gate, upward)
        grad_gate, grad_upward = pull_geglu(grad_product)
        grad_gate_low = grad_gate.astype(jnp.bfloat16)
        grad_up_low = grad_upward.astype(jnp.bfloat16)
        grad_gate_weight = left_product(prenorm, grad_gate_low)
        grad_up_weight = left_product(prenorm, grad_up_low)
        grad_prenorm = right_product(grad_gate_low, full_gate) + right_product(grad_up_low, full_up)
        _, pull_feed = jax.vjp(rms_scale, hidden, feed_gain)
        grad_hidden_part, grad_feed_gain = pull_feed(grad_prenorm)
        grad_hidden = grad_result + grad_hidden_part
        _, pull_mixer = jax.vjp(rms_scale, attended, attention_gain)
        grad_attended, grad_attention_gain = pull_mixer(grad_hidden)
        grad_attended_low = grad_attended.astype(jnp.bfloat16)
        grad_out_weight = left_product(mixed_flat, grad_attended_low)
        grad_mixed = right_product(grad_attended_low, full_out).astype(jnp.bfloat16)
        grad_mixed = grad_mixed.reshape(length * heads, head_size)
        scores, allowed = block_scores(query_low, keys_only, query_seg, key_seg)
        probs = jnp.where(allowed, jnp.exp(scores - log_total[:, None]), 0.0)
        grad_probs = right_product(grad_mixed, values_only)
        delta = jnp.sum(probs * grad_probs, axis=-1, keepdims=True)
        grad_scores = (probs * (grad_probs - delta)).astype(jnp.bfloat16)
        grad_query_rows = matmul(grad_scores, keys_only) * scale
        grad_keys = left_product(grad_scores, query_low) * scale
        grad_values = left_product(probs.astype(jnp.bfloat16), grad_mixed)
        key_grads = jnp.concatenate([grad_keys, grad_values], axis=-1)
        returning = key_grads[0:length]
        for hop in range(hops):
            returning = passed_along(returning.astype(jnp.bfloat16), "seq", -1).astype(
                returning.dtype
            )
            returning = returning + key_grads[(hop + 1) * length : (hop + 2) * length]
        _, pull_query = jax.vjp(shape_query, query_proj, query_gain)
        grad_query_proj, grad_query_gain = pull_query(
            grad_query_rows.reshape(length, heads, head_size)
        )
        _, pull_key = jax.vjp(shape_key, key_proj, key_gain)
        grad_key_proj, grad_key_gain = pull_key(returning[:, :head_size])
        grad_query_low = grad_query_proj.astype(jnp.bfloat16)
        grad_key_low = grad_key_proj.astype(jnp.bfloat16)
        grad_value_low = returning[:, head_size:].astype(jnp.bfloat16)
        grad_query_weight = left_product(normed, grad_query_low)
        grad_key_weight = left_product(normed, grad_key_low)
        grad_value_weight = left_product(normed, grad_value_low)
        grad_normed = right_product(grad_query_low, full_query) + right_product(
            grad_key_low, full_key
        )
        grad_normed = grad_normed + right_product(grad_value_low, full_value)
        _, pull_input = jax.vjp(rms_scale, source, input_gain)
        grad_source, grad_input_gain = pull_input(grad_normed)
        grad_inputs = grad_hidden + grad_source
        terms = (
            grad_query_weight,
            grad_key_weight,
            grad_value_weight,
            grad_out_weight,
            grad_gate_weight,
            grad_up_weight,
            grad_down_weight,
            grad_input_gain,
            grad_attention_gain,
            grad_feed_gain,
            grad_output_gain,
            grad_query_gain,
            grad_key_gain,
        )
        totals = tuple((running + term for running, term in zip(totals, terms)))
        return (totals, (output, grad_inputs))

    start = (
        jnp.zeros((width, heads * head_size), jnp.float32),
        jnp.zeros((width, head_size), jnp.float32),
        jnp.zeros((width, head_size), jnp.float32),
        jnp.zeros((heads * head_size, width), jnp.float32),
        jnp.zeros((width, FF), jnp.float32),
        jnp.zeros((width, FF), jnp.float32),
        jnp.zeros((FF, width), jnp.float32),
        jnp.zeros_like(input_gain),
        jnp.zeros_like(attention_gain),
        jnp.zeros_like(feed_gain),
        jnp.zeros_like(output_gain),
        jnp.zeros_like(query_gain),
        jnp.zeros_like(key_gain),
    )
    totals, (output, grad_inputs) = lax.scan(one_micro, start, (inputs, segments, cotangent))
    shard_query, shard_key, shard_value, shard_gate, shard_up = (
        lax.psum_scatter(totals[0], ("dp", "seq"), scatter_dimension=1, tiled=True),
        lax.psum_scatter(totals[1], ("dp", "seq"), scatter_dimension=1, tiled=True),
        lax.psum_scatter(totals[2], ("dp", "seq"), scatter_dimension=1, tiled=True),
        lax.psum_scatter(totals[4], ("dp", "seq"), scatter_dimension=1, tiled=True),
        lax.psum_scatter(totals[5], ("dp", "seq"), scatter_dimension=1, tiled=True),
    )
    shard_out, shard_down = (
        lax.psum_scatter(totals[3], ("dp", "seq"), scatter_dimension=0, tiled=True),
        lax.psum_scatter(totals[6], ("dp", "seq"), scatter_dimension=0, tiled=True),
    )
    sum_input, sum_attention, sum_feed, sum_output, sum_query, sum_key = lax.psum(
        (totals[7], totals[8], totals[9], totals[10], totals[11], totals[12]), ("dp", "seq")
    )
    return (
        output,
        grad_inputs,
        shard_query,
        shard_key,
        shard_value,
        shard_out,
        shard_gate,
        shard_up,
        shard_down,
        sum_input,
        sum_attention,
        sum_feed,
        sum_output,
        sum_query,
        sum_key,
    )


def solution(mesh):
    in_specs = (
        P("dp", "seq", None),
        P("dp", "seq"),
        P(None, ("dp", "seq")),
        P(None, ("dp", "seq")),
        P(None, ("dp", "seq")),
        P(("dp", "seq"), None),
        P(None, ("dp", "seq")),
        P(None, ("dp", "seq")),
        P(("dp", "seq"), None),
        P(),
        P(),
        P(),
        P(),
        P(),
        P(),
        P("dp", "seq", None),
    )
    out_specs = (
        P("dp", "seq", None),
        P("dp", "seq", None),
        P(None, ("dp", "seq")),
        P(None, ("dp", "seq")),
        P(None, ("dp", "seq")),
        P(("dp", "seq"), None),
        P(None, ("dp", "seq")),
        P(None, ("dp", "seq")),
        P(("dp", "seq"), None),
        P(),
        P(),
        P(),
        P(),
        P(),
        P(),
    )
    return jax.shard_map(
        on_device, mesh=mesh, in_specs=in_specs, out_specs=out_specs, check_vma=False
    )
```

profile of v0, /device:TPU:0, one launch (start us, length us, event | category | flops | bytes accessed | tf_op | source)
XLA Modules:
  0.0 2584.8 jit_solution(7106296971022459902)
XLA Ops:
  9.2 1243.0 %while.41 = (s32[]{:T(128)}, f32[1152,1024]{1,0:T(8,128)}, f32[1152,256]{1,0:T(8,128)}, f32[1152,256]{1,0:T(8,128)}, f32[1024,1152]{1,0:T(8,128)}, /*index=5*/f3...) while((s32[]{:T(128)}, f32[1152,1024]{1,0:T(8,128)}, ...), condition=%wide.region_22.23_spmd.clone, body=%wide.region_0.22_spmd.clone.sunk | while | flops 43852558336 | bytes 916269120 | solution.py:269
  15.2 45.6 %all_gather.65 = bf16[1152,256]{0,1:T(8,128)(2,1)S(1)} all-gather(bf16[1152,8]{0,1:T(8,128)(2,1)} %get-tuple-element.1139), channel_id=1, replica_groups=mesh['dp'=8,'seq'=4] {'dp','seq'}, dimensions={1}, use_global_device_ids=true | all-gather | bytes 608256 | tf_op jit(solution)/shard_map/while/body/eval_jaxpr/all_gather | solution.py:121
  61.6 39.0 %all_gather.64 = bf16[1152,256]{0,1:T(8,128)(2,1)S(1)} all-gather(bf16[1152,8]{0,1:T(8,128)(2,1)S(1)} %copy-done.63), channel_id=1, replica_groups=mesh['dp'=8,'seq'=4] {'dp','seq'}, dimensions={1}, use_global_device_ids=true | all-gather | bytes 608256 | tf_op jit(solution)/shard_map/while/body/eval_jaxpr/all_gather | solution.py:122
  111.2 3.5 collective-permute-start.1
  129.2 4.4 all-gather.8.cloned.1.call-done
  138.7 107.6 %all-gather.10.cloned.1.call-done = bf16[1152,6912]{0,1:T(8,128)(2,1)} async-done(((bf16[1152,216]{0,1:T(8,128)(2,1)}), bf16[1152,6912]{0,1:T(8,128)(2,1)}) %all-gather.10.cloned.1.call-update) | async-done | bytes 15925264 | tf_op jit(solution)/shard_map/while/body/eval_jaxpr/all_gather | solution.py:124
  246.3 13.4 fusion.267
  259.7 98.5 %all-gather.12.cloned.1.call-done = bf16[1152,6912]{0,1:T(8,128)(2,1)} async-done(((bf16[1152,216]{0,1:T(8,128)(2,1)}), bf16[1152,6912]{0,1:T(8,128)(2,1)}) %all-gather.12.cloned.1.call-update) | async-done | bytes 15925264 | tf_op jit(solution)/shard_map/while/body/eval_jaxpr/all_gather | solution.py:125
  358.2 12.7 multiply_convert_fusion.9
  370.9 99.2 %all-gather.14.cloned.1.call-done = bf16[6912,1152]{1,0:T(8,128)(2,1)} async-done(((bf16[216,1152]{1,0:T(8,128)(2,1)}), bf16[6912,1152]{1,0:T(8,128)(2,1)}) %all-gather.14.cloned.1.call-update) | async-done | bytes 15925264 | tf_op jit(solution)/shard_map/while/body/eval_jaxpr/all_gather | solution.py:126
  470.1 10.7 multiply_reduce_fusion.28
  482.8 17.6 multiply_convert_fusion.10
  500.4 10.3 fusion.270
  510.8 10.5 multiply_reduce_fusion.29
  526.3 3.9 fusion.274
  546.7 14.8 convolution_add_fusion.24
  561.5 13.9 convolution_add_fusion.22
  575.4 14.1 convolution_add_fusion.23
  590.7 3.0 convolution_add_fusion.21
  618.1 44.9 %all_gather.65 = bf16[1152,256]{0,1:T(8,128)(2,1)S(1)} all-gather(bf16[1152,8]{0,1:T(8,128)(2,1)} %get-tuple-element.1139), channel_id=1, replica_groups=mesh['dp'=8,'seq'=4] {'dp','seq'}, dimensions={1}, use_global_device_ids=true | all-gather | bytes 608256 | tf_op jit(solution)/shard_map/while/body/eval_jaxpr/all_gather | solution.py:121
  663.7 38.6 %all_gather.64 = bf16[1152,256]{0,1:T(8,128)(2,1)S(1)} all-gather(bf16[1152,8]{0,1:T(8,128)(2,1)S(1)} %copy-done.63), channel_id=1, replica_groups=mesh['dp'=8,'seq'=4] {'dp','seq'}, dimensions={1}, use_global_device_ids=true | all-gather | bytes 608256 | tf_op jit(solution)/shard_map/while/body/eval_jaxpr/all_gather | solution.py:122
  705.3 3.4 collective-permute-start
  713.4 3.5 collective-permute-start.1
  731.7 4.1 all-gather.8.cloned.1.call-done
  740.9 107.6 %all-gather.10.cloned.1.call-done = bf16[1152,6912]{0,1:T(8,128)(2,1)} async-done(((bf16[1152,216]{0,1:T(8,128)(2,1)}), bf16[1152,6912]{0,1:T(8,128)(2,1)}) %all-gather.10.cloned.1.call-update) | async-done | bytes 15925264 | tf_op jit(solution)/shard_map/while/body/eval_jaxpr/all_gather | solution.py:124
  848.5 13.4 fusion.267
  861.9 98.6 %all-gather.12.cloned.1.call-done = bf16[1152,6912]{0,1:T(8,128)(2,1)} async-done(((bf16[1152,216]{0,1:T(8,128)(2,1)}), bf16[1152,6912]{0,1:T(8,128)(2,1)}) %all-gather.12.cloned.1.call-update) | async-done | bytes 15925264 | tf_op jit(solution)/shard_map/while/body/eval_jaxpr/all_gather | solution.py:125
  960.5 12.7 multiply_convert_fusion.9
  973.2 99.2 %all-gather.14.cloned.1.call-done = bf16[6912,1152]{1,0:T(8,128)(2,1)} async-done(((bf16[216,1152]{1,0:T(8,128)(2,1)}), bf16[6912,1152]{1,0:T(8,128)(2,1)}) %all-gather.14.cloned.1.call-update) | async-done | bytes 15925264 | tf_op jit(solution)/shard_map/while/body/eval_jaxpr/all_gather | solution.py:126
  1072.4 10.6 multiply_reduce_fusion.28
  1085.1 17.6 multiply_convert_fusion.10
  1102.7 10.3 fusion.270
  1113.0 10.3 multiply_reduce_fusion.29
  1128.3 3.9 fusion.274
  1148.7 25.3 convolution_add_fusion.24
  1174.0 24.5 convolution_add_fusion.22
  1198.5 24.7 convolution_add_fusion.23
  1224.5 6.1 convolution_add_fusion.21
  1256.5 6.1 copy.47
  1263.3 32.6 %copy.50 = f32[1152,6912]{0,1:T(8,128)} copy(f32[1152,6912]{1,0:T(8,128)} %get-tuple-element.472) | data formatting | bytes 63700992 | tf_op jit(solution)/shard_map/while | solution.py:269
  1296.0 32.4 %copy.51 = f32[1152,6912]{0,1:T(8,128)} copy(f32[1152,6912]{1,0:T(8,128)} %get-tuple-element.473) | data formatting | bytes 63700992 | tf_op jit(solution)/shard_map/while | solution.py:269
  1329.2 43.6 %all-reduce.9 = (f32[1152]{0:T(1024)}, f32[1152]{0:T(1024)}, f32[1152]{0:T(1024)}, f32[1152]{0:T(1024)}, f32[256]{0:T(256)}, /*index=5*/f32[256]{0:T(256)}) all-reduce(f32[1152]{0:T(1024)S(1)} %copy-done.77, f32[1152]{0:T(1024)S(1)} %copy-done.80, f32[1152]{0:T(1024)S(1)} %copy-done.83, ...), channel_id=1, replica_groups=mesh['dp'=8,'seq'=4] {'dp','seq'}, use_global_device_ids=true, to_apply=%region_30.31 | all-reduce | flops 5120 | bytes 40960 | tf_op jit(solution)/shard_map/psum | solution.py:281
  1372.8 23.1 all-reduce.13.cloned.1.call-done
  1398.7 109.7 %reduce-scatter.12.cloned.1.call-done = f32[1152,32]{0,1:T(8,128)} async-done(((f32[1152,1024]{0,1:T(8,128)}), f32[1152,32]{0,1:T(8,128)}) %reduce-scatter.12.cloned.1.call-update) | async-done | bytes 147472 | tf_op jit(solution)/shard_map/reduce_scatter | solution.py:271
  1508.3 111.9 %reduce-scatter.14.cloned.1.call-done = f32[32,1152]{1,0:T(8,128)} async-done(((f32[1024,1152]{1,0:T(8,128)}), f32[32,1152]{1,0:T(8,128)}) %reduce-scatter.14.cloned.1.call-update) | async-done | bytes 147472 | tf_op jit(solution)/shard_map/reduce_scatter | solution.py:278
  1620.2 318.9 %reduce-scatter.16.cloned.1.call-done = f32[1152,216]{0,1:T(8,128)} async-done(((f32[1152,6912]{0,1:T(8,128)}), f32[1152,216]{0,1:T(8,128)}) %reduce-scatter.16.cloned.1.call-update) | async-done | bytes 995344
  1939.1 318.4 %reduce-scatter.18.cloned.1.call-done = f32[1152,216]{0,1:T(8,128)} async-done(((f32[1152,6912]{0,1:T(8,128)}), f32[1152,216]{0,1:T(8,128)}) %reduce-scatter.18.cloned.1.call-update) | async-done | bytes 995344
  2257.5 319.6 %reduce-scatter.20.cloned.1.call-done = f32[216,1152]{1,0:T(8,128)} async-done(((f32[6912,1152]{1,0:T(8,128)}), f32[216,1152]{1,0:T(8,128)}) %reduce-scatter.20.cloned.1.call-update) | async-done | bytes 995344
  (682 shorter events, 163.4 us)
Async XLA Ops:
  9.8 106.4 %copy-start.96 = (s32[256]{0:T(256)}, s32[256]{0:T(256)S(1)}, u32[]{:S(2)}) copy-start(s32[256]{0:T(256)S(1)} %get-tuple-element.1151) | copy-start | bytes 3076 | tf_op jit(solution)/shard_map/while
  9.8 111.4 %copy-start.15 = (f32[256,256]{0,1:T(8,128)}, f32[256,256]{0,1:T(8,128)S(1)}, u32[]{:S(2)}) copy-start(f32[256,256]{0,1:T(8,128)S(1)} %get-tuple-element.1138) | copy-start | bytes 786436 | tf_op jit(solution)/shard_map/while
  9.8 111.4 %copy-start.17 = (f32[256,256]{0,1:T(8,128)}, f32[256,256]{0,1:T(8,128)S(1)}, u32[]{:S(2)}) copy-start(f32[256,256]{0,1:T(8,128)S(1)} %get-tuple-element.1137) | copy-start | bytes 786436 | tf_op jit(solution)/shard_map/while
  9.8 51.0 %copy-start = (bf16[2,256,1152]{2,1,0:T(8,128)(2,1)S(1)}, bf16[2,256,1152]{2,1,0:T(8,128)(2,1)}, u32[]{:S(2)}) copy-start(bf16[2,256,1152]{2,1,0:T(8,128)(2,1)} %get-tuple-element.1132) | copy-start | bytes 3538948 | tf_op jit(solution)/shard_map/while
  9.8 107.8 %all-gather.6.cloned.1.call-start = ((), (), s32[]{:S(2)}) async-start(), calls=%async_computation.11 | async-start | bytes 2433024 | tf_op jit(solution)/shard_map/while/body/eval_jaxpr/all_gather | solution.py:120
  10.6 50.8 %copy-start.105 = (f32[256]{0:T(256)S(1)}, f32[256]{0:T(256)}, u32[]{:S(2)}) copy-start(f32[256]{0:T(256)} %get-tuple-element.1140) | copy-start | bytes 3076 | tf_op jit(solution)/shard_map/while
  10.6 123.0 %all-gather.8.cloned.1.call-start = ((), (), s32[]{:S(2)}) async-start(), calls=%async_computation.12 | async-start | bytes 2433024 | tf_op jit(solution)/shard_map/while/body/eval_jaxpr/all_gather | solution.py:123
  11.3 235.0 %all-gather.10.cloned.1.call-start = ((), (), s32[]{:S(2)}) async-start(), calls=%async_computation.13 | async-start | bytes 16422912 | tf_op jit(solution)/shard_map/while/body/eval_jaxpr/all_gather | solution.py:124
  12.1 346.1 %all-gather.12.cloned.1.call-start = ((), (), s32[]{:S(2)}) async-start(), calls=%async_computation.14 | async-start | bytes 16422912 | tf_op jit(solution)/shard_map/while/body/eval_jaxpr/all_gather | solution.py:125
  12.6 49.0 %copy-start.63 = (bf16[1152,8]{0,1:T(8,128)(2,1)S(1)}, bf16[1152,8]{0,1:T(8,128)(2,1)}, u32[]{:S(2)}) copy-start(bf16[1152,8]{0,1:T(8,128)(2,1)} %get-tuple-element.1141) | copy-start | bytes 55300 | tf_op jit(solution)/shard_map/while
  12.6 457.4 %all-gather.14.cloned.1.call-start = ((), (), s32[]{:S(2)}) async-start(), calls=%async_computation.15 | async-start | bytes 16422912 | tf_op jit(solution)/shard_map/while/body/eval_jaxpr/all_gather | solution.py:126
  14.5 86.6 %copy-start.84 = (f32[256]{0:T(256)}, f32[256]{0:T(256)S(1)}, u32[]{:S(2)}) copy-start(f32[256]{0:T(256)S(1)} %fusion.256) | copy-start | bytes 3076 | tf_op jit(solution)/shard_map/while
  14.5 86.6 %copy-start.53 = (f32[256]{0:T(256)}, f32[256]{0:T(256)S(1)}, u32[]{:S(2)}) copy-start(f32[256]{0:T(256)S(1)} %fusion.257) | copy-start | bytes 3076 | tf_op jit(solution)/shard_map/while
  15.2 102.4 %copy-start.42 = (f32[1152]{0:T(1024)}, f32[1152]{0:T(1024)S(1)}, u32[]{:S(2)}) copy-start(f32[1152]{0:T(1024)S(1)} %broadcast_add_fusion.12) | copy-start | bytes 13828 | tf_op jit(solution)/shard_map/while
  61.5 46.8 %copy-start.87 = (f32[1152]{0:T(1024)S(1)}, f32[1152]{0:T(1024)}, u32[]{:S(2)}) copy-start(f32[1152]{0:T(1024)} %get-tuple-element.1143) | copy-start | bytes 13828 | tf_op jit(solution)/shard_map/while
  101.3 7.1 collective-permute-start.2
  103.6 7.6 collective-permute-start
  108.4 9.2 collective-permute-start.3
  111.2 5.7 collective-permute-start.1
  537.0 61.3 %collective-permute-start.4 = (bf16[256,512]{0,1:T(8,128)(2,1)S(1)}, bf16[256,512]{0,1:T(8,128)(2,1)S(1)}, u32[]{:S(2)}, u32[]{:S(2)}) collective-permute-start(bf16[256,512]{0,1:T(8,128)(2,1)S(1)} %fusion.275), channel_id=1, source_target_pairs={{1,0},{2,1},{3,2},{5,4},{6,5},{7,6},{9,8},{10,9},{11,10},{13,12},{... | collective-permute-start | bytes 786440 | tf_op jit(solution)/shard_map/while/body/eval_jaxpr/ppermute | solution.py:17
  599.4 4.2 collective-permute-start.5
  612.6 105.8 %copy-start.96 = (s32[256]{0:T(256)}, s32[256]{0:T(256)S(1)}, u32[]{:S(2)}) copy-start(s32[256]{0:T(256)S(1)} %get-tuple-element.1151) | copy-start | bytes 3076 | tf_op jit(solution)/shard_map/while
  612.6 110.8 %copy-start.15 = (f32[256,256]{0,1:T(8,128)}, f32[256,256]{0,1:T(8,128)S(1)}, u32[]{:S(2)}) copy-start(f32[256,256]{0,1:T(8,128)S(1)} %get-tuple-element.1138) | copy-start | bytes 786436 | tf_op jit(solution)/shard_map/while
  612.6 110.8 %copy-start.17 = (f32[256,256]{0,1:T(8,128)}, f32[256,256]{0,1:T(8,128)S(1)}, u32[]{:S(2)}) copy-start(f32[256,256]{0,1:T(8,128)S(1)} %get-tuple-element.1137) | copy-start | bytes 786436 | tf_op jit(solution)/shard_map/while
  612.6 50.3 %copy-start = (bf16[2,256,1152]{2,1,0:T(8,128)(2,1)S(1)}, bf16[2,256,1152]{2,1,0:T(8,128)(2,1)}, u32[]{:S(2)}) copy-start(bf16[2,256,1152]{2,1,0:T(8,128)(2,1)} %get-tuple-element.1132) | copy-start | bytes 3538948 | tf_op jit(solution)/shard_map/while
  612.6 107.2 %all-gather.6.cloned.1.call-start = ((), (), s32[]{:S(2)}) async-start(), calls=%async_computation.11 | async-start | bytes 2433024 | tf_op jit(solution)/shard_map/while/body/eval_jaxpr/all_gather | solution.py:120
  613.2 50.2 %copy-start.105 = (f32[256]{0:T(256)S(1)}, f32[256]{0:T(256)}, u32[]{:S(2)}) copy-start(f32[256]{0:T(256)} %get-tuple-element.1140) | copy-start | bytes 3076 | tf_op jit(solution)/shard_map/while
  613.2 122.5 %all-gather.8.cloned.1.call-start = ((), (), s32[]{:S(2)}) async-start(), calls=%async_computation.12 | async-start | bytes 2433024 | tf_op jit(solution)/shard_map/while/body/eval_jaxpr/all_gather | solution.py:123
  614.0 234.5 %all-gather.10.cloned.1.call-start = ((), (), s32[]{:S(2)}) async-start(), calls=%async_computation.13 | async-start | bytes 16422912 | tf_op jit(solution)/shard_map/while/body/eval_jaxpr/all_gather | solution.py:124
  614.7 345.8 %all-gather.12.cloned.1.call-start = ((), (), s32[]{:S(2)}) async-start(), calls=%async_computation.14 | async-start | bytes 16422912 | tf_op jit(solution)/shard_map/while/body/eval_jaxpr/all_gather | solution.py:125
  615.5 48.3 %copy-start.63 = (bf16[1152,8]{0,1:T(8,128)(2,1)S(1)}, bf16[1152,8]{0,1:T(8,128)(2,1)}, u32[]{:S(2)}) copy-start(bf16[1152,8]{0,1:T(8,128)(2,1)} %get-tuple-element.1141) | copy-start | bytes 55300 | tf_op jit(solution)/shard_map/while
  615.5 456.9 %all-gather.14.cloned.1.call-start = ((), (), s32[]{:S(2)}) async-start(), calls=%async_computation.15 | async-start | bytes 16422912 | tf_op jit(solution)/shard_map/while/body/eval_jaxpr/all_gather | solution.py:126
  617.3 85.5 %copy-start.84 = (f32[256]{0:T(256)}, f32[256]{0:T(256)S(1)}, u32[]{:S(2)}) copy-start(f32[256]{0:T(256)S(1)} %fusion.256) | copy-start | bytes 3076 | tf_op jit(solution)/shard_map/while
  617.3 85.5 %copy-start.53 = (f32[256]{0:T(256)}, f32[256]{0:T(256)S(1)}, u32[]{:S(2)}) copy-start(f32[256]{0:T(256)S(1)} %fusion.257) | copy-start | bytes 3076 | tf_op jit(solution)/shard_map/while
  618.1 101.8 %copy-start.42 = (f32[1152]{0:T(1024)}, f32[1152]{0:T(1024)S(1)}, u32[]{:S(2)}) copy-start(f32[1152]{0:T(1024)S(1)} %broadcast_add_fusion.12) | copy-start | bytes 13828 | tf_op jit(solution)/shard_map/while
  663.6 46.9 %copy-start.87 = (f32[1152]{0:T(1024)S(1)}, f32[1152]{0:T(1024)}, u32[]{:S(2)}) copy-start(f32[1152]{0:T(1024)} %get-tuple-element.1143) | copy-start | bytes 13828 | tf_op jit(solution)/shard_map/while
  703.0 7.5 collective-permute-start.2
  705.3 8.1 collective-permute-start
  710.6 9.2 collective-permute-start.3
  713.4 5.7 collective-permute-start.1
  1139.0 96.1 %collective-permute-start.4 = (bf16[256,512]{0,1:T(8,128)(2,1)S(1)}, bf16[256,512]{0,1:T(8,128)(2,1)S(1)}, u32[]{:S(2)}, u32[]{:S(2)}) collective-permute-start(bf16[256,512]{0,1:T(8,128)(2,1)S(1)} %fusion.275), channel_id=1, source_target_pairs={{1,0},{2,1},{3,2},{5,4},{6,5},{7,6},{9,8},{10,9},{11,10},{13,12},{... | collective-permute-start | bytes 786440 | tf_op jit(solution)/shard_map/while/body/eval_jaxpr/ppermute | solution.py:17
  1236.2 4.2 collective-permute-start.5
  1252.3 143.6 %all-reduce.13.cloned.1.call-start = ((), (), s32[]{:S(2)}) async-start(), calls=%async_computation.10 | async-start | bytes 4718592
  1256.5 251.8 %reduce-scatter.12.cloned.1.call-start = ((), (), s32[]{:S(2)}) async-start(), calls=%async_computation.5 | async-start | bytes 4866048 | tf_op jit(solution)/shard_map/reduce_scatter | solution.py:271
  1262.6 357.5 %reduce-scatter.14.cloned.1.call-start = ((), (), s32[]{:S(2)}) async-start(), calls=%async_computation.6 | async-start | bytes 4866048 | tf_op jit(solution)/shard_map/reduce_scatter | solution.py:278
  1263.2 675.9 %reduce-scatter.16.cloned.1.call-start = ((), (), s32[]{:S(2)}) async-start(), calls=%async_computation.7 | async-start | bytes 32845824
  1295.9 961.6 %reduce-scatter.18.cloned.1.call-start = ((), (), s32[]{:S(2)}) async-start(), calls=%async_computation.8 | async-start | bytes 32845824
  1328.4 1248.7 %reduce-scatter.20.cloned.1.call-start = ((), (), s32[]{:S(2)}) async-start(), calls=%async_computation.9 | async-start | bytes 32845824
  (199 other events, 1324.6 us)
Sparse Core Ops, SparseCore 0:
  13.6 60.9 all-gather.5
  77.5 56.0 all-gather.7
  136.4 109.8 all-gather.9
  249.0 109.1 all-gather.11
  360.9 109.1 all-gather.13
  616.1 60.9 all-gather.5
  680.0 55.6 all-gather.7
  738.6 109.8 all-gather.9
  851.3 109.1 all-gather.11
  963.2 109.1 all-gather.13
Sparse Core Ops, SparseCore 1:
  1258.4 137.4 all-reduce.12
  1402.7 105.6 reduce-scatter.11
  1514.2 105.9 reduce-scatter.13
  1628.4 310.7 reduce-scatter.15
  1946.1 311.3 reduce-scatter.17
  2265.7 311.4 reduce-scatter.19
where the time goes:
time: 2590 us; the launch traced here: 2580 us
  waiting for transfers between devices  1830 us (71%)
  matrix products  327 us (13%)
  blocking collectives  212 us (8%)
  local copies, waits for them, and re-layouts  115 us (4%)
  other arithmetic  46.3 us (2%)
  starting transfers between devices  29.2 us (1%)
    unnamed x10, waiting for transfers between devices  981 us
    all_gather x2, waiting for transfers between devices, one_micro(): lax.all_gather(shards[4], ('dp', 'seq'), axis=1, tiled=True)  215 us
    all_gather x2, waiting for transfers between devices, one_micro(): lax.all_gather(shards[6], ('dp', 'seq'), axis=0, tiled=True)  198 us
    all_gather x2, waiting for transfers between devices, one_micro(): lax.all_gather(shards[5], ('dp', 'seq'), axis=1, tiled=True)  197 us
    dot_general x18, matrix products, left_product(): lax.dot_general(left, right, (((0,), (0,)), ((), ())), preferred_element_...  143 us
    reduce_scatter x1, waiting for transfers between devices, on_device(): lax.psum_scatter(totals[3], ('dp', 'seq'), scatter_dimension=0, tiled=True)  112 us
    reduce_scatter x1, waiting for transfers between devices, on_device(): lax.psum_scatter(totals[0], ('dp', 'seq'), scatter_dimension=1, tiled=True)  110 us
    dot_general x18, matrix products, matmul(): return jnp.dot(left, right, preferred_element_type=jnp.float32)  94.1 us
  transfers between devices with their start and end apart: 28, of which 16 were waited for; matrix products, arithmetic and copies ran while one was open for 13% of the time, Pallas kernels for 0%

commit v1 on v0

v1 whole, which is shorter than its diff:
```python
import jax
import jax.numpy as jnp
from jax import lax
from jax.sharding import PartitionSpec as P

HEADS = 4
WINDOW = 512

epsilon = 1e-06
both = ("dp", "seq")
low = jnp.bfloat16
wide = jnp.float32


def flipped(value, bits):
    count = lax.axis_size("seq")
    return lax.ppermute(value, "seq", [(index, index ^ bits) for index in range(count)])


def passed_along(value, axis, steps):
    count = lax.axis_size(axis)
    leading, last = (max(0, -steps), min(count, count - steps))
    return lax.ppermute(value, axis, [(source, source + steps) for source in range(leading, last)])


def seq_gather(rows):
    across = flipped(rows, 2)
    return jnp.concatenate([flipped(rows, 1), flipped(across, 1), rows, across], axis=0)


def seq_reduce(partner, own):
    rows = own.shape[0] // 2
    summed = own + flipped(partner, 1).astype(wide)
    return summed[:rows] + flipped(summed[rows:].astype(low), 2).astype(wide)


def rms_parts(values):
    scale = lax.rsqrt(jnp.mean(values * values, axis=-1, keepdims=True) + epsilon)
    return values * scale, scale


def rms_back(unit, scale, gain, grad):
    weighted = grad * (1.0 + gain)
    inner = jnp.mean(unit * weighted, axis=-1, keepdims=True)
    axes = tuple(range(grad.ndim - 1))
    return scale * (weighted - unit * inner), jnp.sum(unit * grad, axis=axes)


def rope_tables(positions, width):
    steps = jnp.arange(width // 2, dtype=wide)
    inverse = 10000.0 ** (-2.0 * steps / width)
    angles = positions.astype(wide)[:, None] * inverse[None, :]
    doubled = jnp.concatenate([angles, angles], axis=-1)
    return (jnp.cos(doubled), jnp.sin(doubled))


def rotate(values, cosine, sine):
    half = values.shape[-1] // 2
    turned = jnp.concatenate([-values[..., half:], values[..., :half]], axis=-1)
    return values * cosine + turned * sine


def rotate_back(grad, cosine, sine):
    half = grad.shape[-1] // 2
    swung = grad * sine
    turned = jnp.concatenate([swung[..., half:], -swung[..., :half]], axis=-1)
    return grad * cosine + turned


def product_of(left, right, left_axis, right_axis):
    return lax.dot_general(
        left, right, (((left_axis,), (right_axis,)), ((), ())), preferred_element_type=wide
    )


def gelu_parts(gate):
    inner = 0.7978845608028654 * (gate + 0.044715 * gate * gate * gate)
    bend = jnp.tanh(inner)
    value = 0.5 * gate * (1.0 + bend)
    slope = 0.5 * (1.0 + bend) + 0.5 * gate * (1.0 - bend * bend) * 0.7978845608028654 * (
        1.0 + 3.0 * 0.044715 * gate * gate
    )
    return value, slope


def on_device(
    inputs,
    segments,
    query_weight,
    key_weight,
    value_weight,
    out_weight,
    gate_weight,
    up_weight,
    down_weight,
    input_gain,
    attention_gain,
    feed_gain,
    output_gain,
    query_gain,
    key_gain,
    cotangent,
):
    micro, length, width = inputs.shape
    rows = micro * length
    size = query_gain.shape[0]
    heads = HEADS
    scale = 1.0 / jnp.sqrt(wide(size))
    seq_count = lax.axis_size("seq")
    hops = min((WINDOW + length - 2) // length, seq_count - 1)
    seq_index = lax.axis_index("seq")
    nq, nk, nv = query_weight.shape[1], key_weight.shape[1], value_weight.shape[1]

    attn_shard = jnp.concatenate([query_weight.T, key_weight.T, value_weight.T, out_weight], axis=0)
    attn_all = lax.all_gather(attn_shard, both, axis=0, tiled=False)
    ends = (nq, nq + nk, nq + nk + nv)
    full_qkv = jnp.concatenate(
        [
            attn_all[:, : ends[0]].reshape(-1, width),
            attn_all[:, ends[0] : ends[1]].reshape(-1, width),
            attn_all[:, ends[1] : ends[2]].reshape(-1, width),
        ],
        axis=0,
    )
    full_out = attn_all[:, ends[2] :].reshape(-1, width)
    gate_all = lax.all_gather(gate_weight.T, "dp", axis=0, tiled=True)
    up_all = lax.all_gather(up_weight.T, "dp", axis=0, tiled=True)
    down_all = lax.all_gather(down_weight, "dp", axis=0, tiled=True)

    positions = seq_index * length + jnp.arange(length, dtype=jnp.int32)
    cosine, sine = rope_tables(positions, size)
    source = inputs.reshape(rows, width).astype(wide)
    source_unit, source_scale = rms_parts(source)
    normed = (source_unit * (1.0 + input_gain)).astype(low)
    projected = product_of(normed, full_qkv, 1, 1)
    hq = heads * size
    query_proj = projected[:, :hq].reshape(micro, length, heads, size)
    key_proj = projected[:, hq : hq + size].reshape(micro, length, size)
    value_low = projected[:, hq + size :].astype(low).reshape(micro, length, size)
    query_unit, query_scale = rms_parts(query_proj)
    key_unit, key_scale = rms_parts(key_proj)
    query_low = rotate(
        query_unit * (1.0 + query_gain), cosine[:, None, :], sine[:, None, :]
    ).astype(low)
    query_low = query_low.reshape(micro, length * heads, size)
    key_low = rotate(key_unit * (1.0 + key_gain), cosine, sine).astype(low)
    own_block = jnp.concatenate([key_low, value_low], axis=-1)
    blocks = [own_block]
    seg_blocks = [segments]
    for hop in range(1, hops + 1):
        blocks.insert(0, passed_along(own_block, "seq", hop))
        seg_blocks.insert(0, passed_along(segments, "seq", hop))
    all_keys = jnp.concatenate(blocks, axis=1)
    key_seg = jnp.concatenate(seg_blocks, axis=1)
    keys_only = all_keys[..., :size]
    values_only = all_keys[..., size:]
    key_count = (hops + 1) * length
    key_pos = seq_index * length - hops * length + jnp.arange(key_count, dtype=jnp.int32)
    query_pos = jnp.broadcast_to(positions[:, None], (length, heads)).reshape(length * heads)
    window = (key_pos[None, :] >= 0) & (key_pos[None, :] <= query_pos[:, None])
    window = window & (query_pos[:, None] - key_pos[None, :] < WINDOW)
    mixed, kept = [], []
    for item in range(micro):
        row_seg = jnp.broadcast_to(segments[item][:, None], (length, heads)).reshape(-1)
        allowed = window & (key_seg[item][None, :] == row_seg[:, None])
        scores = product_of(query_low[item], keys_only[item], 1, 1) * scale
        masked = jnp.where(allowed, scores, -1e30)
        highest = jnp.max(masked, axis=-1, keepdims=True)
        expo = jnp.exp(masked - highest)
        total = jnp.sum(expo, axis=-1, keepdims=True)
        probs = (expo / total).astype(low)
        mixed.append(product_of(probs, values_only[item], 1, 0).astype(low))
        kept.append((allowed, highest + jnp.log(total)))
    mixed_flat = jnp.stack(mixed).reshape(rows, hq)
    attended = product_of(mixed_flat, full_out, 1, 0)
    attended_unit, attended_scale = rms_parts(attended)
    hidden = source + attended_unit * (1.0 + attention_gain)
    hidden_unit, hidden_scale = rms_parts(hidden)
    prenorm = (hidden_unit * (1.0 + feed_gain)).astype(low)

    group = seq_gather(prenorm)
    half = 2 * rows
    gate = product_of(group, gate_all, 1, 1)
    upward = product_of(group, up_all, 1, 1)
    product = (gelu_parts(gate)[0] * upward).astype(low)
    down = seq_reduce(
        product_of(product[:half], down_all, 1, 0).astype(low),
        product_of(product[half:], down_all, 1, 0),
    )
    down_unit, down_scale = rms_parts(down)
    output = (hidden + down_unit * (1.0 + output_gain)).astype(low)

    grad_result = cotangent.reshape(rows, width).astype(wide)
    grad_down, grad_output_gain = rms_back(down_unit, down_scale, output_gain, grad_result)
    grad_group = seq_gather(grad_down.astype(low))
    grad_down_weight = product_of(product, grad_group, 0, 0).astype(low)
    shard_down = lax.psum_scatter(grad_down_weight, "dp", scatter_dimension=0, tiled=True)
    grad_product = product_of(grad_group, down_all, 1, 1)
    value, slope = gelu_parts(gate)
    grad_gate = (grad_product * upward * slope).astype(low)
    grad_up = (grad_product * value).astype(low)
    grad_prenorm = seq_reduce(
        (product_of(grad_gate[:half], gate_all, 1, 0) + product_of(grad_up[:half], up_all, 1, 0)).astype(low),
        product_of(grad_gate[half:], gate_all, 1, 0) + product_of(grad_up[half:], up_all, 1, 0),
    )
    grad_gate_weight = product_of(grad_gate, group, 0, 0).astype(low)
    shard_gate = lax.psum_scatter(grad_gate_weight, "dp", scatter_dimension=0, tiled=True)
    grad_up_weight = product_of(grad_up, group, 0, 0).astype(low)
    shard_up = lax.psum_scatter(grad_up_weight, "dp", scatter_dimension=0, tiled=True)

    grad_part, grad_feed_gain = rms_back(hidden_unit, hidden_scale, feed_gain, grad_prenorm)
    grad_hidden = grad_result + grad_part
    grad_attended, grad_attention_gain = rms_back(
        attended_unit, attended_scale, attention_gain, grad_hidden
    )
    grad_attended = grad_attended.astype(low)
    grad_out = product_of(mixed_flat, grad_attended, 0, 0).astype(low)
    grad_mixed = product_of(grad_attended, full_out, 1, 1).astype(low)
    grad_mixed = grad_mixed.reshape(micro, length * heads, size)
    grad_query_rows, key_grads = [], []
    for item in range(micro):
        allowed, log_total = kept[item]
        scores = product_of(query_low[item], keys_only[item], 1, 1) * scale
        probs = jnp.where(allowed, jnp.exp(scores - log_total), 0.0)
        grad_probs = product_of(grad_mixed[item], values_only[item], 1, 1)
        delta = jnp.sum(probs * grad_probs, axis=-1, keepdims=True)
        grad_scores = (probs * (grad_probs - delta)).astype(low)
        grad_query_rows.append(product_of(grad_scores, keys_only[item], 1, 0) * scale)
        grad_keys = product_of(grad_scores, query_low[item], 0, 0) * scale
        grad_values = product_of(probs.astype(low), grad_mixed[item], 0, 0)
        key_grads.append(jnp.concatenate([grad_keys, grad_values], axis=-1))
    key_grads = jnp.stack(key_grads)
    returning = key_grads[:, hops * length :]
    for hop in range(1, hops + 1):
        block = key_grads[:, (hops - hop) * length : (hops - hop + 1) * length]
        returning = returning + passed_along(block.astype(low), "seq", -hop).astype(wide)
    grad_query_rows = jnp.stack(grad_query_rows).reshape(micro, length, heads, size)
    grad_query_proj, grad_query_gain = rms_back(
        query_unit,
        query_scale,
        query_gain,
        rotate_back(grad_query_rows, cosine[:, None, :], sine[:, None, :]),
    )
    grad_key_proj, grad_key_gain = rms_back(
        key_unit, key_scale, key_gain, rotate_back(returning[..., :size], cosine, sine)
    )
    grad_projected = jnp.concatenate(
        [
            grad_query_proj.astype(low).reshape(rows, hq),
            grad_key_proj.astype(low).reshape(rows, size),
            returning[..., size:].astype(low).reshape(rows, size),
        ],
        axis=-1,
    )
    grad_qkv = product_of(grad_projected, normed, 0, 0).astype(low)
    grad_normed = product_of(grad_projected, full_qkv, 1, 0)
    grad_source, grad_input_gain = rms_back(source_unit, source_scale, input_gain, grad_normed)
    grad_inputs = grad_hidden + grad_source

    count = attn_all.shape[0]
    grad_attn = jnp.concatenate(
        [
            grad_qkv[:hq].reshape(count, nq, width),
            grad_qkv[hq : hq + size].reshape(count, nk, width),
            grad_qkv[hq + size :].reshape(count, nv, width),
            grad_out.reshape(count, -1, width),
        ],
        axis=1,
    )
    shard_attn = lax.psum_scatter(grad_attn, both, scatter_dimension=0, tiled=False).astype(wide)
    gains = lax.psum(
        jnp.concatenate(
            [
                grad_input_gain,
                grad_attention_gain,
                grad_feed_gain,
                grad_output_gain,
                grad_query_gain,
                grad_key_gain,
            ]
        ),
        both,
    )
    return (
        output.reshape(micro, length, width),
        grad_inputs.reshape(micro, length, width),
        shard_attn[: ends[0]].T,
        shard_attn[ends[0] : ends[1]].T,
        shard_attn[ends[1] : ends[2]].T,
        shard_attn[ends[2] :],
        shard_gate.astype(wide).T,
        shard_up.astype(wide).T,
        shard_down.astype(wide),
        gains[:width],
        gains[width : 2 * width],
        gains[2 * width : 3 * width],
        gains[3 * width : 4 * width],
        gains[4 * width : 4 * width + size],
        gains[4 * width + size :],
    )


def solution(mesh):
    in_specs = (
        P("dp", "seq", None),
        P("dp", "seq"),
        P(None, ("dp", "seq")),
        P(None, ("dp", "seq")),
        P(None, ("dp", "seq")),
        P(("dp", "seq"), None),
        P(None, ("dp", "seq")),
        P(None, ("dp", "seq")),
        P(("dp", "seq"), None),
        P(),
        P(),
        P(),
        P(),
        P(),
        P(),
        P("dp", "seq", None),
    )
    out_specs = (
        P("dp", "seq", None),
        P("dp", "seq", None),
        P(None, ("dp", "seq")),
        P(None, ("dp", "seq")),
        P(None, ("dp", "seq")),
        P(("dp", "seq"), None),
        P(None, ("dp", "seq")),
        P(None, ("dp", "seq")),
        P(("dp", "seq"), None),
        P(),
        P(),
        P(),
        P(),
        P(),
        P(),
    )
    return jax.shard_map(
        on_device, mesh=mesh, in_specs=in_specs, out_specs=out_specs, check_vma=False
    )
```

time: 2590 us -> 782 us (0.30)
  waiting for transfers between devices: 1830 us -> 364 us
  blocking collectives: 212 us -> 42.8 us
  matrix products: 327 us -> 198 us
  local copies, waits for them, and re-layouts: 115 us -> 62.7 us
    unnamed x10 -> x11, waiting for transfers between devices: 981 us -> 3.44 us
    all_gather x10 -> x4, waiting for transfers between devices: 619 us -> 143 us  [the longest x1 52.4 us: on_device(): attn_all = lax.all_gather(attn_shard, both, axis=0, tiled=False)]
    all_gather x4 -> x0, blocking collectives: 168 us -> none  [the longest x2 90.4 us: one_micro(): lax.all_gather(shards[1], ('dp', 'seq'), axis=1, tiled=True)]
    dot_general x54 -> x30, matrix products: 327 us -> 198 us  [product_of(): lax.dot_general(left, right, (((left_axis,), (right_axis,)), ((), ())), p...]
    reduce_scatter x2 -> x1, waiting for transfers between devices: 222 us -> 116 us  [on_device(): lax.psum_scatter(grad_attn, both, scatter_dimension=0, tiled=False)]
    ppermute x0 -> x10, waiting for transfers between devices: none -> 97 us  [flipped(): lax.ppermute(value, 'seq', [(index, index ^ bits) for index in range(coun...]
    while x429 -> x0, local copies, waits for them, and re-layouts: 96.7 us -> none  [the longest x5 75.2 us: on_device(): lax.scan(one_micro, start, (inputs, segments, cotangent))]
  transfers between devices with their start and end apart: 28 -> 24, of which waited for: 16 -> 13; matrix products, arithmetic and copies ran while one was open for 13% -> 35% of each run, Pallas kernels for 0% -> 0%
where the time goes in v1:
time: 782 us; the launch traced here: 776 us
  waiting for transfers between devices  364 us (47%)
  matrix products  198 us (25%)
  other arithmetic  63.8 us (8%)
  local copies, waits for them, and re-layouts  62.7 us (8%)
  blocking collectives  42.8 us (5%)
  starting transfers between devices  27.9 us (4%)
  between operations  16.2 us (2%)
    dot_general x30, matrix products, product_of(): lax.dot_general(left, right, (((left_axis,), (right_axis,)), ((), ())), p...  198 us
    reduce_scatter x1, waiting for transfers between devices, on_device(): lax.psum_scatter(grad_attn, both, scatter_dimension=0, tiled=False)  116 us
    ppermute x10, waiting for transfers between devices, flipped(): lax.ppermute(value, 'seq', [(index, index ^ bits) for index in range(coun...  97 us
    all_gather x1, waiting for transfers between devices, on_device(): attn_all = lax.all_gather(attn_shard, both, axis=0, tiled=False)  52.4 us
    all_gather x1, waiting for transfers between devices, on_device(): down_all = lax.all_gather(down_weight, 'dp', axis=0, tiled=True)  48.3 us
    all_gather x1, waiting for transfers between devices, on_device(): up_all = lax.all_gather(up_weight.T, 'dp', axis=0, tiled=True)  42.8 us
    psum x1, blocking collectives, on_device(): lax.psum(jnp.concatenate([grad_input_gain, grad_attention_gain, grad_feed...  42.8 us
    unnamed x260, local copies, waits for them, and re-layouts  28.3 us
  transfers between devices with their start and end apart: 24, of which 13 were waited for; matrix products, arithmetic and copies ran while one was open for 35% of the time, Pallas kernels for 0%

profile of v1, /device:TPU:0, one launch (start us, length us, event | category | flops | bytes accessed | tf_op | source)
XLA Modules:
  0.0 775.7 jit_solution(16463207885961873748)
XLA Ops:
  9.8 4.9 collective-permute-start
  29.6 52.4 %all-gather.12.cloned.1.call-done = bf16[2560,1152]{1,0:T(8,128)(2,1)} async-done(((bf16[80,1152]{1,0:T(8,128)(2,1)}), bf16[2560,1152]{1,0:T(8,128)(2,1)}) %all-gather.12.cloned.1.call-update) | async-done | bytes 5898256 | tf_op jit(solution)/shard_map/all_gather | solution.py:115
  83.4 4.7 fusion.79
  97.6 3.0 collective-permute-start.3
  100.6 3.6 collective-permute-start.2
  111.5 4.4 collective-permute-done.2
  119.2 2.8 fusion.22
  129.7 3.7 multiply_reduce_fusion.8
  137.3 2.7 collective-permute-start.4
  140.0 21.9 %collective-permute-done.5 = bf16[512,1152]{1,0:T(8,128)(2,1)} collective-permute-done((bf16[512,1152]{1,0:T(8,128)(2,1)S(1)}, bf16[512,1152]{1,0:T(8,128)(2,1)}, u32[]{:S(2)}, u32[]{:S(2)}) %collective-permute-start.5) | collective-permute-done | bytes 1179680 | tf_op jit(solution)/shard_map/ppermute | solution.py:17
  164.0 2.8 collective-permute-done.6
  166.8 15.5 %fusion.74 = f32[2048,1728]{0,1:T(8,128)} fusion(bf16[1728,1152]{1,0:T(8,128)(2,1)} %all-gather.6.cloned.1.call-done, bf16[512,1152]{1,0:T(8,128)(2,1)} %collective-permute-done.5, bf16[512,1152]{1,0:T(8,128)(2,1)S(1)} %multiply_convert_fusion.5, bf16[512,1152]{1,0:T(8,128)(2,1)} %collective-permute-done.6, bf16[512,1152]{1,0:T(8,128)(2,1)} %collective-permute-done.4), kind=kOutput, calls=%fused_computation.216 | convolution fusion | flops 8172601344 | bytes 22855680 | tf_op jit(solution)/shard_map/dot_general | solution.py:71
  182.3 42.8 %all-gather.8.cloned.1.call-done = bf16[1728,1152]{1,0:T(8,128)(2,1)} async-done(((bf16[216,1152]{1,0:T(8,128)(2,1)}), bf16[1728,1152]{1,0:T(8,128)(2,1)}) %all-gather.8.cloned.1.call-update) | async-done | bytes 3981328 | tf_op jit(solution)/shard_map/all_gather | solution.py:127
  225.2 22.8 %multiply_convert_fusion.1 = (bf16[2048,1728]{0,1:T(8,128)(2,1)}, f32[2048,1728]{0,1:T(8,128)}) fusion(f32[2048,1728]{0,1:T(8,128)} %fusion.74, bf16[1728,1152]{1,0:T(8,128)(2,1)} %all-gather.8.cloned.1.call-done, bf16[512,1152]{1,0:T(8,128)(2,1)} %collective-permute-done.5, bf16[512,1152]{1,0:T(8,128)(2,1)S(1)} %multiply_convert_fusion.5, ...), kind=kOutput, calls=%fused_computation.10 | convolution fusion | flops 8207990784 | bytes 44089344 | tf_op jit(solution)/shard_map/dot_general | solution.py:71
  248.0 48.3 %all-gather.10.cloned.1.call-done = bf16[1728,1152]{1,0:T(8,128)(2,1)} async-done(((bf16[216,1152]{1,0:T(8,128)(2,1)}), bf16[1728,1152]{1,0:T(8,128)(2,1)}) %all-gather.10.cloned.1.call-update) | async-done | bytes 3981328 | tf_op jit(solution)/shard_map/all_gather | solution.py:128
  296.3 8.3 %convolution_convert_fusion.5 = bf16[1024,1152]{1,0:T(8,128)(2,1)S(1)} fusion(bf16[1728,1152]{1,0:T(8,128)(2,1)} %all-gather.10.cloned.1.call-done, bf16[2048,1728]{0,1:T(8,128)(2,1)} %get-tuple-element.86), kind=kOutput, calls=%fused_computation.23 | convolution fusion | flops 4078043136 | bytes 9879552 | tf_op jit(solution)/shard_map/dot_general | solution.py:71
  304.8 4.5 collective-permute-done.7
  309.3 5.1 convert_add_fusion.1
  316.1 26.5 %collective-permute-done.8 = bf16[512,1152]{1,0:T(8,128)(2,1)S(1)} collective-permute-done((bf16[512,1152]{1,0:T(8,128)(2,1)S(1)}, bf16[512,1152]{1,0:T(8,128)(2,1)S(1)}, u32[]{:S(2)}, u32[]{:S(2)}) %collective-permute-start.8) | collective-permute-done | bytes 1179680 | tf_op jit(solution)/shard_map/ppermute | solution.py:17
  348.4 25.7 %collective-permute-done.10 = bf16[512,1152]{1,0:T(8,128)(2,1)S(1)} collective-permute-done((bf16[512,1152]{1,0:T(8,128)(2,1)S(1)}, bf16[512,1152]{1,0:T(8,128)(2,1)S(1)}, u32[]{:S(2)}, u32[]{:S(2)}) %collective-permute-start.10) | collective-permute-done | bytes 1179680 | tf_op jit(solution)/shard_map/ppermute | solution.py:17
  374.1 2.8 collective-permute-done.11
  378.0 10.8 %convolution_convert_fusion.1 = bf16[1728,1152]{1,0:T(8,128)(2,1)} fusion(bf16[2048,1728]{0,1:T(8,128)(2,1)S(1)} %copy-done.119, bf16[512,1152]{1,0:T(8,128)(2,1)S(1)} %collective-permute-done.10, bf16[512,1152]{1,0:T(8,128)(2,1)S(1)} %get-tuple-element.41, bf16[512,1152]{1,0:T(8,128)(2,1)S(1)} %collective-permute-done.11, ...), kind=kOutput, calls=%fused_computation.13 | convolution fusion | flops 8174592000 | bytes 15777792 | tf_op jit(solution)/shard_map/dot_general | solution.py:71
  388.9 26.4 %multiply_convert_fusion = (bf16[2048,1728]{0,1:T(8,128)(2,1)}, bf16[2048,1728]{0,1:T(8,128)(2,1)S(1)}) fusion(f32[2048,1728]{0,1:T(8,128)} %fusion.74, f32[2048,1728]{0,1:T(8,128)} %get-tuple-element.87, bf16[1728,1152]{1,0:T(8,128)(2,1)} %all-gather.10.cloned.1.call-done, bf16[512,1152]{1,0:T(8,128)(2,1)} %copy-done.116, bf16[512,1152]{1,0:T(8,128)(2,1)} %copy-done.46, ...), kind=kOutput, calls=%fused_computation.9 | convolution fusion | flops 8253997056 | bytes 51167232 | tf_op jit(solution)/shard_map/dot_general | solution.py:71
  415.2 2.9 copy-done.120
  418.1 12.8 %convolution_convert_fusion.3 = bf16[1728,1152]{1,0:T(8,128)(2,1)} fusion(bf16[2048,1728]{0,1:T(8,128)(2,1)S(1)} %get-tuple-element.38, bf16[512,1152]{1,0:T(8,128)(2,1)} %collective-permute-done.5, bf16[512,1152]{1,0:T(8,128)(2,1)S(1)} %copy-done.48, bf16[512,1152]{1,0:T(8,128)(2,1)} %collective-permute-done.6, bf16[512,1152]{1,0:T(8,128)(2,1)} %collective-permute-done.4), kind=kOutput, calls=%fused_computation.15 | convolution fusion | flops 8174592000 | bytes 15777792 | tf_op jit(solution)/shard_map/dot_general | solution.py:71
  431.1 8.5 %fusion.8 = f32[1024,1152]{1,0:T(8,128)S(1)} fusion(bf16[1728,1152]{1,0:T(8,128)(2,1)} %all-gather.6.cloned.1.call-done, bf16[2048,1728]{0,1:T(8,128)(2,1)} %copy-done.120), kind=kOutput, calls=%fused_computation.28 | convolution fusion | flops 4076863488 | bytes 12238848 | tf_op jit(solution)/shard_map/dot_general | solution.py:71
  439.7 7.4 add_convert_fusion
  451.6 5.4 fusion.11
  457.0 7.5 convert_add_fusion
  469.5 14.3 %convolution_convert_fusion.2 = bf16[1728,1152]{1,0:T(8,128)(2,1)} fusion(bf16[2048,1728]{0,1:T(8,128)(2,1)} %get-tuple-element.37, bf16[512,1152]{1,0:T(8,128)(2,1)} %collective-permute-done.5, bf16[512,1152]{1,0:T(8,128)(2,1)S(1)} %copy-done.49, bf16[512,1152]{1,0:T(8,128)(2,1)} %collective-permute-done.6, bf16[512,1152]{1,0:T(8,128)(2,1)} %collective-permute-done.4), kind=kOutput, calls=%fused_computation.14 | convolution fusion | flops 8174592000 | bytes 15777792 | tf_op jit(solution)/shard_map/dot_general | solution.py:71
  483.9 12.6 %collective-permute-done.13 = bf16[512,1152]{1,0:T(8,128)(2,1)} collective-permute-done((bf16[512,1152]{1,0:T(8,128)(2,1)}, bf16[512,1152]{1,0:T(8,128)(2,1)}, u32[]{:S(2)}, u32[]{:S(2)}) %collective-permute-start.13) | collective-permute-done | bytes 1179680 | tf_op jit(solution)/shard_map/ppermute | solution.py:17
  496.6 3.4 multiply_reduce_fusion.2
  500.0 3.9 multiply_reduce_fusion.3
  510.1 3.3 fusion.60
  513.4 5.1 fusion.43
  520.7 6.2 multiply_reduce_fusion
  527.0 3.9 multiply_convert_fusion.2
  539.3 2.7 convolution_multiply_fusion.1
  542.0 2.5 stack.30
  544.5 2.6 convolution_multiply_fusion
  552.5 3.0 convolution_convert_fusion.4
  567.2 3.6 convolution_convert_fusion
  572.5 3.1 pad_maximum_fusion
  576.9 7.0 fusion.37
  591.7 42.8 %psum.7 = f32[5120]{0:T(1024)} all-reduce(f32[5120]{0:T(1024)} %constant_dynamic-update-slice_fusion.6), channel_id=1, replica_groups=mesh['dp'=8,'seq'=4] {'dp','seq'}, use_global_device_ids=true, to_apply=%region_29.30 | all-reduce | flops 5120 | bytes 40960 | tf_op jit(solution)/shard_map/psum | solution.py:271
  637.9 3.7 fusion.36
  645.7 2.6 reduce-scatter.15.cloned.1.call-done
  650.4 115.9 %reduce-scatter.11.cloned.1.call-done = bf16[1,80,1152]{2,1,0:T(8,128)(2,1)} async-done(((bf16[32,80,1152]{2,1,0:T(8,128)(2,1)}), bf16[1,80,1152]{2,1,0:T(8,128)(2,1)}) %reduce-scatter.11.cloned.1.call-update) | async-done | bytes 184336 | tf_op jit(solution)/shard_map/reduce_scatter | solution.py:270
  (415 shorter events, 126.5 us)
Async XLA Ops:
  7.2 16.4 %copy-start.6 = (bf16[2,256,1152]{2,1,0:T(8,128)(2,1)S(1)}, bf16[2,256,1152]{2,1,0:T(8,128)(2,1)}, u32[]{:S(2)}) copy-start(bf16[2,256,1152]{2,1,0:T(8,128)(2,1)} %param.16) | copy-start | bytes 3538948
  7.2 15.8 %copy-start.112 = (f32[256]{0:T(256)S(1)}, f32[256]{0:T(256)}, u32[]{:S(2)}) copy-start(f32[256]{0:T(256)} %param.30) | copy-start | bytes 3076
  7.2 16.4 %copy-start.102 = (f32[1152]{0:T(1024)S(1)}, f32[1152]{0:T(1024)}, u32[]{:S(2)}) copy-start(f32[1152]{0:T(1024)} %param.27) | copy-start | bytes 13828
  7.2 74.7 %all-gather.12.cloned.1.call-start = ((), (), s32[]{:S(2)}) async-start(), calls=%async_computation.8 | async-start | bytes 6082560 | tf_op jit(solution)/shard_map/all_gather | solution.py:115
  9.0 155.0 %all-gather.6.cloned.1.call-start = ((), (), s32[]{:S(2)}) async-start(), calls=%async_computation.4 | async-start | bytes 4478976 | tf_op jit(solution)/shard_map/all_gather | solution.py:126
  9.8 215.4 %all-gather.8.cloned.1.call-start = ((), (), s32[]{:S(2)}) async-start(), calls=%async_computation.5 | async-start | bytes 4478976 | tf_op jit(solution)/shard_map/all_gather | solution.py:127
  9.8 19.1 %collective-permute-start = (s32[2,256]{1,0:T(2,128)}, s32[2,256]{1,0:T(2,128)S(1)}, u32[]{:S(2)}, u32[]{:S(2)}) collective-permute-start(s32[2,256]{1,0:T(2,128)} %param.17), channel_id=1, source_target_pairs={{0,2},{1,3},{4,6},{5,7},{8,10},{9,11},{12,14},{13,15},{16,18},{17,... | collective-permute-start | bytes 6152 | tf_op jit(solution)/shard_map/ppermute | solution.py:23
  14.7 14.3 %collective-permute-start.1 = (s32[2,256]{1,0:T(2,128)}, s32[2,256]{1,0:T(2,128)S(1)}, u32[]{:S(2)}, u32[]{:S(2)}) collective-permute-start(s32[2,256]{1,0:T(2,128)} %param.17), channel_id=1, source_target_pairs={{0,1},{1,2},{2,3},{4,5},{5,6},{6,7},{8,9},{9,10},{10,11},{12,13},{... | collective-permute-start | bytes 6152 | tf_op jit(solution)/shard_map/ppermute | solution.py:23
  16.2 280.1 %all-gather.10.cloned.1.call-start = ((), (), s32[]{:S(2)}) async-start(), calls=%async_computation.6 | async-start | bytes 4478976 | tf_op jit(solution)/shard_map/all_gather | solution.py:128
  17.7 115.8 %copy-start.62 = (f32[1152]{0:T(1024)}, f32[1152]{0:T(1024)S(1)}, u32[]{:S(2)}) copy-start(f32[1152]{0:T(1024)S(1)} %broadcast_add_fusion.2) | copy-start | bytes 13828
  19.0 64.3 %copy-start.66 = (f32[1152]{0:T(1024)}, f32[1152]{0:T(1024)S(1)}, u32[]{:S(2)}) copy-start(f32[1152]{0:T(1024)S(1)} %broadcast_add_fusion.3) | copy-start | bytes 13828
  20.6 62.7 %copy-start.89 = (f32[1,2,2,128]{3,1,2,0:T(2,128)}, f32[1,2,2,128]{3,1,2,0:T(2,128)S(1)}, u32[]{:S(2)}) copy-start(f32[1,2,2,128]{3,1,2,0:T(2,128)S(1)} %copy.55) | copy-start | bytes 6148
  23.0 72.9 %copy-start.25 = (f32[256,256]{0,1:T(8,128)}, f32[256,256]{0,1:T(8,128)S(1)}, u32[]{:S(2)}) copy-start(f32[256,256]{0,1:T(8,128)S(1)} %get-tuple-element.70) | copy-start | bytes 786436
  23.0 72.9 %copy-start.27 = (f32[256,256]{0,1:T(8,128)}, f32[256,256]{0,1:T(8,128)S(1)}, u32[]{:S(2)}) copy-start(f32[256,256]{0,1:T(8,128)S(1)} %get-tuple-element.69) | copy-start | bytes 786436
  23.6 110.6 %copy-start.64 = (f32[1152]{0:T(1024)}, f32[1152]{0:T(1024)S(1)}, u32[]{:S(2)}) copy-start(f32[1152]{0:T(1024)S(1)} %broadcast_add_fusion.1) | copy-start | bytes 13828
  28.1 80.9 %copy-start.30 = (f32[256,256]{1,0:T(8,128)}, f32[256,256]{1,0:T(8,128)S(1)}, u32[]{:S(2)}) copy-start(f32[256,256]{1,0:T(8,128)S(1)} %copy.49) | copy-start | bytes 786436
  97.6 13.9 %collective-permute-start.3 = (bf16[2,256,512]{1,2,0:T(8,128)(2,1)}, bf16[2,256,512]{1,2,0:T(8,128)(2,1)}, u32[]{:S(2)}, u32[]{:S(2)}) collective-permute-start(bf16[2,256,512]{1,2,0:T(8,128)(2,1)} %pad_maximum_fusion.13), channel_id=1, source_target_pairs={{0,1},{1,2},{2,3},{4,5},{5,6},{6,7},{8,9},{9,10},{10,11},{12,13},{... | collective-permute-start | bytes 1572872 | tf_op jit(solution)/shard_map/ppermute | solution.py:23
  100.6 15.3 %collective-permute-start.2 = (bf16[2,256,512]{1,2,0:T(8,128)(2,1)}, bf16[2,256,512]{1,2,0:T(8,128)(2,1)}, u32[]{:S(2)}, u32[]{:S(2)}) collective-permute-start(bf16[2,256,512]{1,2,0:T(8,128)(2,1)} %pad_maximum_fusion.13), channel_id=1, source_target_pairs={{0,2},{1,3},{4,6},{5,7},{8,10},{9,11},{12,14},{13,15},{16,18},{17,... | collective-permute-start | bytes 1572872 | tf_op jit(solution)/shard_map/ppermute | solution.py:23
  134.2 48.2 %copy-start.80 = (f32[512]{0:T(512)}, f32[512]{0:T(512)S(1)}, u32[]{:S(2)}) copy-start(f32[512]{0:T(512)S(1)} %add_rsqrt_fusion.2) | copy-start | bytes 6148
  134.9 90.3 %copy-start.47 = (bf16[512,1152]{1,0:T(8,128)(2,1)}, bf16[512,1152]{1,0:T(8,128)(2,1)S(1)}, u32[]{:S(2)}) copy-start(bf16[512,1152]{1,0:T(8,128)(2,1)S(1)} %multiply_convert_fusion.5) | copy-start | bytes 3538948
  134.9 27.1 %collective-permute-start.5 = (bf16[512,1152]{1,0:T(8,128)(2,1)S(1)}, bf16[512,1152]{1,0:T(8,128)(2,1)}, u32[]{:S(2)}, u32[]{:S(2)}) collective-permute-start(bf16[512,1152]{1,0:T(8,128)(2,1)S(1)} %multiply_convert_fusion.5), channel_id=1, source_target_pairs={{0,2},{1,3},{2,0},{3,1},{4,6},{5,7},{6,4},{7,5},{8,10},{9,11},{10,... | collective-permute-start | bytes 3538952 | tf_op jit(solution)/shard_map/ppermute | solution.py:17
  137.3 504.3 %reduce-scatter.17.cloned.1.call-start = ((), (), s32[]{:S(2)}) async-start(), calls=%async_computation.11 | async-start | bytes 4478976
  137.3 26.7 %collective-permute-start.4 = (bf16[512,1152]{1,0:T(8,128)(2,1)S(1)}, bf16[512,1152]{1,0:T(8,128)(2,1)}, u32[]{:S(2)}, u32[]{:S(2)}) collective-permute-start(bf16[512,1152]{1,0:T(8,128)(2,1)S(1)} %multiply_convert_fusion.5), channel_id=1, source_target_pairs={{0,1},{1,0},{2,3},{3,2},{4,5},{5,4},{6,7},{7,6},{8,9},{9,8},{10,11... | collective-permute-start | bytes 3538952 | tf_op jit(solution)/shard_map/ppermute | solution.py:17
  161.9 4.9 collective-permute-start.6
  296.3 13.0 %copy-start.115 = (bf16[1728,1152]{1,0:T(8,128)(2,1)S(1)}, bf16[1728,1152]{1,0:T(8,128)(2,1)}, u32[]{:S(2)}) copy-start(bf16[1728,1152]{1,0:T(8,128)(2,1)} %all-gather.10.cloned.1.call-done) | copy-start | bytes 11943940
  296.3 13.0 %copy-start.119 = (bf16[2048,1728]{0,1:T(8,128)(2,1)S(1)}, bf16[2048,1728]{0,1:T(8,128)(2,1)}, u32[]{:S(2)}) copy-start(bf16[2048,1728]{0,1:T(8,128)(2,1)} %get-tuple-element.86) | copy-start | bytes 21233668
  304.7 4.6 collective-permute-start.7
  314.4 28.6 %copy-start.16 = (bf16[2,256,1152]{2,1,0:T(8,128)(2,1)S(1)}, bf16[2,256,1152]{2,1,0:T(8,128)(2,1)}, u32[]{:S(2)}) copy-start(bf16[2,256,1152]{2,1,0:T(8,128)(2,1)} %param.31) | copy-start | bytes 3538948
  314.5 28.1 %collective-permute-start.8 = (bf16[512,1152]{1,0:T(8,128)(2,1)S(1)}, bf16[512,1152]{1,0:T(8,128)(2,1)S(1)}, u32[]{:S(2)}, u32[]{:S(2)}) collective-permute-start(bf16[512,1152]{1,0:T(8,128)(2,1)S(1)} %slice.396), channel_id=1, source_target_pairs={{0,2},{1,3},{2,0},{3,1},{4,6},{5,7},{6,4},{7,5},{8,10},{9,11},{10,... | collective-permute-start | bytes 3538952 | tf_op jit(solution)/shard_map/ppermute | solution.py:17
  346.9 30.0 %copy-start.46 = (bf16[512,1152]{1,0:T(8,128)(2,1)}, bf16[512,1152]{1,0:T(8,128)(2,1)S(1)}, u32[]{:S(2)}) copy-start(bf16[512,1152]{1,0:T(8,128)(2,1)S(1)} %get-tuple-element.41) | copy-start | bytes 3538948
  346.9 27.2 %collective-permute-start.10 = (bf16[512,1152]{1,0:T(8,128)(2,1)S(1)}, bf16[512,1152]{1,0:T(8,128)(2,1)S(1)}, u32[]{:S(2)}, u32[]{:S(2)}) collective-permute-start(bf16[512,1152]{1,0:T(8,128)(2,1)S(1)} %get-tuple-element.41), channel_id=1, source_target_pairs={{0,2},{1,3},{2,0},{3,1},{4,6},{5,7},{6,4},{7,5},{8,10},{9,11},{10,... | collective-permute-start | bytes 3538952 | tf_op jit(solution)/shard_map/ppermute | solution.py:17
  348.4 25.7 %collective-permute-start.9 = (bf16[512,1152]{1,0:T(8,128)(2,1)S(1)}, bf16[512,1152]{1,0:T(8,128)(2,1)S(1)}, u32[]{:S(2)}, u32[]{:S(2)}) collective-permute-start(bf16[512,1152]{1,0:T(8,128)(2,1)S(1)} %get-tuple-element.41), channel_id=1, source_target_pairs={{0,1},{1,0},{2,3},{3,2},{4,5},{5,4},{6,7},{7,6},{8,9},{9,8},{10,11... | collective-permute-start | bytes 3538952 | tf_op jit(solution)/shard_map/ppermute | solution.py:17
  374.1 2.8 collective-permute-start.11
  388.8 254.9 %reduce-scatter.13.cloned.1.call-start = ((), (), s32[]{:S(2)}) async-start(), calls=%async_computation.9 | async-start | bytes 4478976
  388.8 29.2 %copy-start.48 = (bf16[512,1152]{1,0:T(8,128)(2,1)S(1)}, bf16[512,1152]{1,0:T(8,128)(2,1)}, u32[]{:S(2)}) copy-start(bf16[512,1152]{1,0:T(8,128)(2,1)} %copy-done.47) | copy-start | bytes 3538948
  430.9 217.5 %reduce-scatter.15.cloned.1.call-start = ((), (), s32[]{:S(2)}) async-start(), calls=%async_computation.10 | async-start | bytes 4478976
  431.1 20.5 %slice-start = ((s8[7077888]{0:T(1024)(128)(4,1)}), s8[4194304]{0:T(1024)(128)(4,1)S(1)}, s32[]{:S(2)}) async-start(s8[7077888]{0:T(1024)(128)(4,1)} %bitcast.186), calls=%async_computation.12 | async-start | bytes 8388608
  447.1 9.9 %collective-permute-start.12 = (bf16[1024,1152]{1,0:T(8,128)(2,1)S(1)}, bf16[1024,1152]{1,0:T(8,128)(2,1)S(1)}, u32[]{:S(2)}, u32[]{:S(2)}) collective-permute-start(bf16[1024,1152]{1,0:T(8,128)(2,1)S(1)} %add_convert_fusion), channel_id=1, source_target_pairs={{0,1},{1,0},{2,3},{3,2},{4,5},{5,4},{6,7},{7,6},{8,9},{9,8},{10,11... | collective-permute-start | bytes 7077896 | tf_op jit(solution)/shard_map/ppermute | solution.py:17
  468.0 28.5 %collective-permute-start.13 = (bf16[512,1152]{1,0:T(8,128)(2,1)}, bf16[512,1152]{1,0:T(8,128)(2,1)}, u32[]{:S(2)}, u32[]{:S(2)}) collective-permute-start(bf16[512,1152]{1,0:T(8,128)(2,1)} %slice.395), channel_id=1, source_target_pairs={{0,2},{1,3},{2,0},{3,1},{4,6},{5,7},{6,4},{7,5},{8,10},{9,11},{10,... | collective-permute-start | bytes 3538952 | tf_op jit(solution)/shard_map/ppermute | solution.py:17
  483.8 12.8 %copy-start.65 = (f32[1152]{0:T(1024)S(1)}, f32[1152]{0:T(1024)}, u32[]{:S(2)}) copy-start(f32[1152]{0:T(1024)} %copy-done.64) | copy-start | bytes 13828
  483.8 16.1 %copy-start.63 = (f32[1152]{0:T(1024)S(1)}, f32[1152]{0:T(1024)}, u32[]{:S(2)}) copy-start(f32[1152]{0:T(1024)} %copy-done.62) | copy-start | bytes 13828
  483.8 282.4 %reduce-scatter.11.cloned.1.call-start = ((), (), s32[]{:S(2)}) async-start(), calls=%async_computation.7 | async-start | bytes 6082560 | tf_op jit(solution)/shard_map/reduce_scatter | solution.py:270
  483.9 16.1 %copy-start.3 = (f32[512,1152]{1,0:T(8,128)S(1)}, f32[512,1152]{1,0:T(8,128)}, u32[]{:S(2)}) copy-start(f32[512,1152]{1,0:T(8,128)} %copy-done.2) | copy-start | bytes 7077892
  483.9 16.1 %copy-start.79 = (f32[512]{0:T(512)S(1)}, f32[512]{0:T(512)}, u32[]{:S(2)}) copy-start(f32[512]{0:T(512)} %copy-done.78) | copy-start | bytes 6148
  483.9 16.1 %copy-start.81 = (f32[512]{0:T(512)S(1)}, f32[512]{0:T(512)}, u32[]{:S(2)}) copy-start(f32[512]{0:T(512)} %copy-done.80) | copy-start | bytes 6148
  536.7 26.4 %collective-permute-start.15 = (bf16[2,256,512]{1,2,0:T(8,128)(2,1)}, bf16[2,256,512]{1,2,0:T(8,128)(2,1)}, u32[]{:S(2)}, u32[]{:S(2)}) collective-permute-start(bf16[2,256,512]{1,2,0:T(8,128)(2,1)} %get-tuple-element.56), channel_id=1, source_target_pairs={{2,0},{3,1},{6,4},{7,5},{10,8},{11,9},{14,12},{15,13},{18,16},{19,... | collective-permute-start | bytes 1572872 | tf_op jit(solution)/shard_map/ppermute | solution.py:23
  538.0 25.2 %collective-permute-start.14 = (bf16[2,256,512]{1,2,0:T(8,128)(2,1)}, bf16[2,256,512]{1,2,0:T(8,128)(2,1)}, u32[]{:S(2)}, u32[]{:S(2)}) collective-permute-start(bf16[2,256,512]{1,2,0:T(8,128)(2,1)} %get-tuple-element.55), channel_id=1, source_target_pairs={{1,0},{2,1},{3,2},{5,4},{6,5},{7,6},{9,8},{10,9},{11,10},{13,12},{... | collective-permute-start | bytes 1572872 | tf_op jit(solution)/shard_map/ppermute | solution.py:23
  576.9 61.0 %copy-start.5 = (f32[512,1152]{1,0:T(8,128)S(1)}, f32[512,1152]{1,0:T(8,128)}, u32[]{:S(2)}) copy-start(f32[512,1152]{1,0:T(8,128)} %copy-done.4) | copy-start | bytes 7077892
  (99 other events, 437.6 us)
Sparse Core Ops, SparseCore 0:
  11.5 70.3 all-gather.11
  84.2 69.6 all-gather.5
  156.1 69.0 all-gather.7
  227.2 69.0 all-gather.9
  388.9 82.9 reduce-scatter.16
  475.4 84.3 reduce-scatter.12
  563.5 84.8 reduce-scatter.14
  654.0 112.2 reduce-scatter.10

commit v2 on v1

v2 whole, which is shorter than its diff:
```python
import functools

import jax
import jax.numpy as jnp
from jax import lax
from jax.experimental import pallas as pl
from jax.experimental.pallas import tpu as pltpu
from jax.sharding import PartitionSpec as P

HEADS = 4
WINDOW = 512

epsilon = 1e-06
both = ("dp", "seq")
low = jnp.bfloat16
wide = jnp.float32


def flipped(value, bits):
    count = lax.axis_size("seq")
    return lax.ppermute(value, "seq", [(index, index ^ bits) for index in range(count)])


def passed_along(value, axis, steps):
    count = lax.axis_size(axis)
    leading, last = (max(0, -steps), min(count, count - steps))
    return lax.ppermute(value, axis, [(source, source + steps) for source in range(leading, last)])


def by_steps():
    return lax.axis_size("dp") == 8 and lax.axis_size("seq") == 4


def along_z(value, steps):
    return lax.ppermute(value, "dp", [(index, (index + 2 * steps) % 8) for index in range(8)])


def along_x(value):
    return lax.ppermute(value, "dp", [(index, index ^ 1) for index in range(8)])


def column_groups():
    return [[2 * z + x for z in range(4)] for x in range(2)] if by_steps() else None


def hidden_gather(shard):
    return lax.all_gather(shard, "dp", axis=0, axis_index_groups=column_groups(), tiled=True)


def hidden_reduce(terms):
    return lax.psum_scatter(
        terms.astype(low), "dp", scatter_dimension=0, axis_index_groups=column_groups(), tiled=True
    ).astype(wide)


def tied(*values):
    return lax.optimization_barrier(values)


def group_gather(rows):
    across_y = flipped(rows, 2)
    if by_steps():
        half = rows.shape[0] // 2
        across_x = along_x(rows)
        diagonal = jnp.concatenate([along_x(across_y[:half]), flipped(across_x[half:], 2)], axis=0)
        own = [diagonal, across_x, across_y, rows]
    else:
        own = [across_y, rows]
    return [flipped(block, 1) for block in own], own


def group_reduce(sent, kept, beside=lambda ready: None, last=lambda ready: None):
    got = flipped(sent, 1)
    rows = kept[0].shape[0]
    half = rows // 2
    part = lambda start, end: got[start:end].astype(wide)
    if not by_steps():
        crossing = (kept[0] + part(0, rows)).astype(low)
        return (kept[1], got[rows:], flipped(crossing, 2)), beside(sent), last(sent)
    diagonal = (kept[0] + part(0, rows)).astype(low)
    diagonal, got, *kept = tied(diagonal, got, *kept[1:])
    aside = beside(kept[0])
    for_y, for_x = along_x(diagonal[:half]), flipped(diagonal[half:], 2)
    for_y, for_x, aside, *kept = tied(for_y, for_x, aside, *kept)
    nothing = jnp.zeros_like(for_x, dtype=wide)
    x_part = kept[0] + part(rows, 2 * rows) + jnp.concatenate([nothing, for_x.astype(wide)], axis=0)
    y_part = kept[1] + part(2 * rows, 3 * rows) + jnp.concatenate([for_y.astype(wide), nothing], axis=0)
    x_part, y_part, *kept = tied(x_part.astype(low), y_part.astype(low), *kept)
    after = last(kept[-1])
    x_part, y_part, after = tied(along_x(x_part), flipped(y_part, 2), after)
    return (kept[-1], got[3 * rows :], x_part, y_part), aside, after


def reduce_step(terms, names, name):
    dp, seq = lax.axis_index("dp"), lax.axis_index("seq")
    own = {"x": dp % 2, "y": seq // 2, "core": seq % 2}[name]
    send = {"x": along_x, "y": lambda v: flipped(v, 2), "core": lambda v: flipped(v, 1)}[name]
    at = names.index(name)
    names.pop(at)
    kept = lax.dynamic_index_in_dim(terms, own, at, keepdims=False)
    sent = lax.dynamic_index_in_dim(terms, 1 - own, at, keepdims=False)
    return kept.astype(wide) + send(sent.astype(low)).astype(wide)


def reduce_first(terms):
    if not by_steps():
        return terms
    return reduce_step(terms.reshape(4, 2, 2, 2, *terms.shape[1:]), ["z", "x", "y", "core"], "core")


def reduce_rest(terms, order):
    if not by_steps():
        return lax.psum_scatter(terms.astype(low), both, scatter_dimension=0, tiled=False).astype(wide)
    z = lax.axis_index("dp") // 2
    names = ["z", "x", "y"]
    for name in order:
        terms = reduce_step(terms, names, name)
    total = lax.dynamic_index_in_dim(terms, z, 0, keepdims=False)
    for steps in (2, 1, 3):
        sent = lax.dynamic_index_in_dim(terms, (z - steps) % 4, 0, keepdims=False)
        total = total + along_z(sent.astype(low), -steps).astype(wide)
    return total


def sum_everywhere(values):
    if not by_steps():
        return lax.psum(values, both)
    values = values + flipped(values, 1)
    values = values + flipped(values, 2)
    values = values + along_x(values)
    values = values + along_z(values, 2)
    return values + along_z(values, 1)


def rms_parts(values):
    scale = lax.rsqrt(jnp.mean(values * values, axis=-1, keepdims=True) + epsilon)
    return values * scale, scale


def rms_back(unit, scale, gain, grad):
    weighted = grad * (1.0 + gain)
    inner = jnp.mean(unit * weighted, axis=-1, keepdims=True)
    axes = tuple(range(grad.ndim - 1))
    return scale * (weighted - unit * inner), jnp.sum(unit * grad, axis=axes)


def rope_tables(positions, width):
    steps = jnp.arange(width // 2, dtype=wide)
    inverse = 10000.0 ** (-2.0 * steps / width)
    angles = positions.astype(wide)[:, None] * inverse[None, :]
    doubled = jnp.concatenate([angles, angles], axis=-1)
    return (jnp.cos(doubled), jnp.sin(doubled))


def rotate(values, cosine, sine):
    half = values.shape[-1] // 2
    turned = jnp.concatenate([-values[..., half:], values[..., :half]], axis=-1)
    return values * cosine + turned * sine


def rotate_back(grad, cosine, sine):
    half = grad.shape[-1] // 2
    swung = grad * sine
    turned = jnp.concatenate([swung[..., half:], -swung[..., :half]], axis=-1)
    return grad * cosine + turned


def product_of(left, right, left_axis, right_axis):
    return lax.dot_general(
        left, right, (((left_axis,), (right_axis,)), ((), ())), preferred_element_type=wide
    )


def gelu_parts(gate):
    inner = 0.7978845608028654 * (gate + 0.044715 * gate * gate * gate)
    bend = jnp.tanh(inner)
    value = 0.5 * gate * (1.0 + bend)
    slope = 0.5 * (1.0 + bend) + 0.5 * gate * (1.0 - bend * bend) * 0.7978845608028654 * (
        1.0 + 3.0 * 0.044715 * gate * gate
    )
    return value, slope


def rms_back_rows(values, gain, grad):
    unit, scale = rms_parts(values)
    weighted = grad * (1.0 + gain)
    inner = jnp.mean(unit * weighted, axis=-1, keepdims=True)
    return unit, scale * (weighted - unit * inner), jnp.sum(unit * grad, axis=0, keepdims=True)


def total_of(terms):
    return functools.reduce(jnp.add, [term[...].astype(wide) for term in terms])


def turn_kernel(*refs):
    *terms, hidden, cotangent, gain, output, grad_down, grad_gain = refs
    down = total_of(terms)
    unit, grad, grad_gain[0] = rms_back_rows(down, gain[...], cotangent[...].astype(wide))
    output[...] = (hidden[...] + unit * (1.0 + gain[...])).astype(low)
    grad_down[...] = grad.astype(low)


def hidden_kernel(*refs):
    *terms, hidden, attended, cotangent, feed, attention, grad_hidden, grad_attended, gains = refs
    grad_prenorm = total_of(terms)
    _, grad, gains[0, 0:1] = rms_back_rows(hidden[...], feed[...], grad_prenorm)
    grad = grad + cotangent[...].astype(wide)
    grad_hidden[...] = grad
    _, grad, gains[0, 1:2] = rms_back_rows(attended[...], attention[...], grad)
    grad_attended[...] = grad.astype(low)


def by_rows(kernel, arrays, gains, kinds, gain_rows, tile=128):
    rows, width = arrays[-1].shape
    tiles = rows // tile
    block = pl.BlockSpec((tile, width), lambda item: (item, 0))
    gain_spec = pl.BlockSpec((1, width), lambda item: (0, 0))
    *results, grads = pl.pallas_call(
        kernel,
        grid=(tiles,),
        in_specs=[block] * len(arrays) + [gain_spec] * len(gains),
        out_specs=[block] * len(kinds) + [pl.BlockSpec((1, gain_rows, width), lambda item: (item, 0, 0))],
        out_shape=[jax.ShapeDtypeStruct((rows, width), kind) for kind in kinds]
        + [jax.ShapeDtypeStruct((tiles, gain_rows, width), wide)],
        compiler_params=pltpu.CompilerParams(vmem_limit_bytes=24 * 2**20),
        cost_estimate=pl.CostEstimate(
            flops=40 * rows * width, bytes_accessed=18 * rows * width, transcendentals=rows
        ),
    )(*arrays, *[gain.reshape(1, width) for gain in gains])
    return *results, jnp.sum(grads, axis=0)


def row_specs(blocks, tile):
    specs, starts, start = [], [], 0
    for block in blocks:
        count = block.shape[0] // tile
        specs.append(
            pl.BlockSpec(
                (tile, block.shape[1]),
                lambda item, start=start, count=count: (jnp.clip(item - start, 0, count - 1), 0),
            )
        )
        starts.append(start)
        start += count
    return specs, starts, start


def picked(refs, starts):
    item = pl.program_id(0)
    value = refs[0][...]
    for ref, start in zip(refs[1:], starts[1:]):
        value = jnp.where(item >= start, ref[...], value)
    return value


def put(refs, starts, value):
    item = pl.program_id(0)
    ends = [*starts[1:], pl.num_programs(0)]
    for ref, start, end in zip(refs, starts, ends):

        @pl.when((item >= start) & (item < end))
        def _():
            ref[...] = value.astype(ref.dtype)


def feed_kernel(counts, starts, *refs):
    ins, outs = counts
    blocks, (gate_all, up_all, down_all) = refs[:ins], refs[ins : ins + 3]
    rows, product, value, slope = refs[ins + 3 : ins + 7]
    rows[...] = picked(blocks, starts)
    gate = product_of(rows[...], gate_all[...], 1, 1)
    upward = product_of(rows[...], up_all[...], 1, 1)
    bent, bend_slope = gelu_parts(gate)
    mixed = (bent * upward).astype(low)
    product[...] = mixed
    value[...] = bent.astype(low)
    slope[...] = (bend_slope * upward).astype(low)
    put(refs[-outs:], starts if outs > 1 else [0], product_of(mixed, down_all[...], 1, 0))


def feed_back_kernel(counts, starts, *refs):
    ins, outs = counts
    blocks, (value, slope, gate_all, up_all, down_all) = refs[:ins], refs[ins : ins + 5]
    rows, grad_gate, grad_up = refs[ins + 5 : ins + 8]
    rows[...] = picked(blocks, starts)
    grad = product_of(rows[...], down_all[...], 1, 1)
    gate = (grad * slope[...].astype(wide)).astype(low)
    upward = (grad * value[...].astype(wide)).astype(low)
    grad_gate[...] = gate
    grad_up[...] = upward
    terms = product_of(gate, gate_all[...], 1, 0) + product_of(upward, up_all[...], 1, 0)
    put(refs[-outs:], starts if outs > 1 else [0], terms)


def feed(back, blocks, kept, weights, split):
    hidden, width = weights[0].shape
    tile = 512 if hidden <= 1024 else 256
    specs, starts, tiles = row_specs(blocks, tile)
    rows = tiles * tile
    inner = pl.BlockSpec((tile, hidden), lambda item: (item, 0))
    outer = pl.BlockSpec((tile, width), lambda item: (item, 0))
    full = pl.BlockSpec((hidden, width), lambda item: (0, 0), pipeline_mode=pl.Buffered(1))
    count = 2 if back else 3
    shape = jax.ShapeDtypeStruct
    if split:
        last_specs = specs
        last = [shape(block.shape, low) for block in blocks[:-1]] + [shape(blocks[-1].shape, wide)]
    else:
        last_specs, last = [outer], [shape((rows, width), low)]
    group, *results = pl.pallas_call(
        functools.partial(feed_back_kernel if back else feed_kernel, (len(blocks), len(last)), starts),
        grid=(tiles,),
        in_specs=specs + [inner] * len(kept) + [full] * 3,
        out_specs=[outer] + [inner] * count + last_specs,
        out_shape=[shape((rows, width), low)] + [shape((rows, hidden), low)] * count + last,
        compiler_params=pltpu.CompilerParams(vmem_limit_bytes=56 * 2**20),
        cost_estimate=pl.CostEstimate(
            flops=6 * rows * hidden * width,
            bytes_accessed=rows * (10 * hidden + 8 * width) + 6 * hidden * width,
            transcendentals=0 if back else rows * hidden,
        ),
    )(*blocks, *kept, *weights)
    return group, results[:count], results[count:] if split else results[count]


def weight_grad(lefts, rights):
    terms = [product_of(left, right, 0, 0) for left, right in zip(lefts, rights)]
    return (terms[0] + terms[1]).astype(low)


def weights_kernel(rows, place, *refs):
    blocks, outs = refs[:8], refs[8:]
    relative = pl.program_id(0) ^ place[0]
    for number, block in enumerate(blocks):

        @pl.when(relative == number)
        def _():
            for z in range(4):
                source = lax.rem(place[1] + 4 - z, 4)
                start = 0
                for out, count in zip(outs, rows):
                    out[z, 0] = block[source, start : start + count]
                    start += count


def attention_weights(shards):
    rows = [shard.shape[0] for shard in shards]
    width = shards[0].shape[1]
    shard = jnp.concatenate(shards, axis=0)
    if not by_steps():
        whole = lax.all_gather(shard, both, axis=0, tiled=False)
        starts = [sum(rows[:at]) for at in range(len(rows))]
        return [
            whole[:, start : start + count].reshape(-1, width) for start, count in zip(starts, rows)
        ]
    first, third, second = along_z(shard, 1), along_z(shard, 3), along_z(shard, 2)
    column = jnp.concatenate([shard, first, second, third], axis=0)
    far, near = group_gather(column)
    blocks = [block.reshape(4, -1, width) for at in (3, 2, 1, 0) for block in (near[at], far[at])]
    dp, seq = lax.axis_index("dp"), lax.axis_index("seq")
    place = jnp.stack([(dp % 2) * 4 + seq, dp // 2]).astype(jnp.int32)
    results = pl.pallas_call(
        functools.partial(weights_kernel, rows),
        grid=(8,),
        in_specs=[pl.BlockSpec(memory_space=pltpu.SMEM)]
        + [pl.BlockSpec((4, sum(rows), width), lambda item: (0, 0, 0), pipeline_mode=pl.Buffered(1))] * 8,
        out_specs=[pl.BlockSpec((4, 1, count, width), lambda item: (0, item, 0, 0)) for count in rows],
        out_shape=[jax.ShapeDtypeStruct((4, 8, count, width), shard.dtype) for count in rows],
        compiler_params=pltpu.CompilerParams(vmem_limit_bytes=24 * 2**20),
        cost_estimate=pl.CostEstimate(
            flops=0, bytes_accessed=64 * sum(rows) * width * 2, transcendentals=0
        ),
    )(place, *blocks)
    return [result.reshape(-1, width) for result in results]


def allowed_pairs(base, row_seg, column_seg, length, before):
    shape = (before + length, length)
    key = lax.broadcasted_iota(jnp.int32, shape, 0)
    distance = lax.broadcasted_iota(jnp.int32, shape, 1) + before - key
    allowed = (distance >= 0) & (distance < WINDOW) & (key >= before - base)
    return allowed & (column_seg == row_seg)


def shaped_query(projected, gain, cosine, sine):
    unit, scale = rms_parts(projected)
    return unit, scale, rotate(unit * (1.0 + gain), cosine, sine).astype(low)


def attend_kernel(heads, base, proj, cosine, sine, gain, own_seg, key_seg, *refs):
    *blocks, mixed, logs = refs
    length, size = cosine.shape
    keys = jnp.concatenate([block[0] for block in blocks], axis=0)
    only, values = keys[:, :size], keys[:, size:]
    before = keys.shape[0] - length
    allowed = allowed_pairs(base[0], own_seg[0], key_seg[0], length, before)
    for head in range(heads):
        at = slice(head * size, (head + 1) * size)
        _, _, query = shaped_query(proj[:, at], gain[...], cosine[...], sine[...])
        scores = product_of(only, query, 1, 1) * size**-0.5
        scores = jnp.where(allowed, scores, -1e30)
        highest = jnp.max(scores, axis=0, keepdims=True)
        expo = jnp.exp(scores - highest)
        total = jnp.sum(expo, axis=0, keepdims=True)
        probs = (expo * (1.0 / total)).astype(low)
        mixed[:, at] = product_of(probs.T, values, 1, 0).astype(low)
        logs[0, head : head + 1, :] = highest + jnp.log(total)


def attend_back_kernel(heads, base, proj, cosine, sine, gain, own_seg, key_seg, logs, grad, *refs):
    hops = (len(refs) - 3) // 2
    blocks, outs = refs[: hops + 1], refs[hops + 1 :]
    grad_proj, grad_gain = outs[0], outs[1]
    length, size = cosine.shape
    keys = jnp.concatenate([block[0] for block in blocks], axis=0)
    only, values = keys[:, :size], keys[:, size:]
    before = hops * length
    allowed = allowed_pairs(base[0], own_seg[0], key_seg[0], length, before)
    grad_keys = jnp.zeros((before + length, size), wide)
    grad_values = jnp.zeros((before + length, size), wide)
    gains = jnp.zeros((1, size), wide)
    for head in range(heads):
        at = slice(head * size, (head + 1) * size)
        unit, scale, query = shaped_query(proj[:, at], gain[...], cosine[...], sine[...])
        mixed_grad = grad[:, at]
        scores = product_of(only, query, 1, 1) * size**-0.5
        probs = jnp.where(allowed, jnp.exp(scores - logs[0, head : head + 1, :]), 0.0)
        grad_probs = product_of(values, mixed_grad, 1, 1)
        delta = jnp.sum(probs * grad_probs, axis=0, keepdims=True)
        grad_scores = (probs * (grad_probs - delta)).astype(low)
        grad_values += product_of(probs.astype(low), mixed_grad, 1, 0)
        grad_keys += product_of(grad_scores, query, 1, 0)
        grad_query = product_of(grad_scores.T, only, 1, 0) * size**-0.5
        turned = rotate_back(grad_query, cosine[...], sine[...])
        weighted = turned * (1.0 + gain[...])
        inner = jnp.mean(unit * weighted, axis=-1, keepdims=True)
        grad_proj[:, at] = (scale * (weighted - unit * inner)).astype(low)
        gains += jnp.sum(unit * turned, axis=0, keepdims=True)
    grad_gain[0] = gains
    for hop in range(hops + 1):
        rows = slice(hop * length, (hop + 1) * length)
        target = outs[2 + hop]
        target[0, :, :size] = (grad_keys[rows] * size**-0.5).astype(target.dtype)
        target[0, :, size:] = grad_values[rows].astype(target.dtype)


def attention(back, micro, length, base, projected, tables, gain, segments, key_seg, blocks, extra=()):
    size = gain.shape[-1]
    hops = len(blocks) - 1
    whole = lambda *shape: pl.BlockSpec(shape, lambda item: (0,) * len(shape))
    each = lambda *shape: pl.BlockSpec((1, *shape), lambda item: (item, 0, 0))
    flat = pl.BlockSpec((length, HEADS * size), lambda item: (item, 0))
    key_count = (hops + 1) * length
    in_specs = [
        pl.BlockSpec(memory_space=pltpu.SMEM),
        flat,
        whole(length, size),
        whole(length, size),
        whole(1, size),
        each(1, length),
        each(key_count, 1),
    ]
    logs_spec, block_spec = each(HEADS, length), each(length, 2 * size)
    shape = jax.ShapeDtypeStruct
    rows = (micro * length, HEADS * size)
    if back:
        in_specs += [logs_spec, flat]
        out_specs = [flat, each(1, size)] + [block_spec] * (hops + 1)
        out_shape = [shape(rows, low), shape((micro, 1, size), wide)]
        out_shape += [shape((micro, length, 2 * size), low)] * hops
        out_shape += [shape((micro, length, 2 * size), wide)]
    else:
        out_specs = [flat, logs_spec]
        out_shape = [shape(rows, low), shape((micro, HEADS, length), wide)]
    flops = micro * HEADS * key_count * length * size * 2 * (5 if back else 2)
    return pl.pallas_call(
        functools.partial(attend_back_kernel if back else attend_kernel, HEADS),
        grid=(micro,),
        in_specs=in_specs + [block_spec] * (hops + 1),
        out_specs=out_specs,
        out_shape=out_shape,
        compiler_params=pltpu.CompilerParams(vmem_limit_bytes=40 * 2**20),
        cost_estimate=pl.CostEstimate(
            flops=flops, bytes_accessed=10 * 2**20, transcendentals=micro * HEADS * key_count * length
        ),
    )(
        base.reshape(1),
        projected,
        *tables,
        gain.reshape(1, size),
        segments.reshape(micro, 1, length),
        key_seg.reshape(micro, key_count, 1),
        *extra,
        *blocks,
    )


def on_device(
    inputs,
    segments,
    query_weight,
    key_weight,
    value_weight,
    out_weight,
    gate_weight,
    up_weight,
    down_weight,
    input_gain,
    attention_gain,
    feed_gain,
    output_gain,
    query_gain,
    key_gain,
    cotangent,
):
    micro, length, width = inputs.shape
    rows = micro * length
    size = query_gain.shape[0]
    seq_count = lax.axis_size("seq")
    dp_count = lax.axis_size("dp")
    hops = min((WINDOW + length - 2) // length, seq_count - 1)
    seq_index = lax.axis_index("seq")
    nq, nk, nv = query_weight.shape[1], key_weight.shape[1], value_weight.shape[1]

    full_query, full_key, full_value, full_out = attention_weights(
        [query_weight.T, key_weight.T, value_weight.T, out_weight]
    )
    units = gate_weight.shape[1]
    shards = 4 if by_steps() else dp_count
    padding = next(extra for extra in range(129) if (units + extra) * shards % 128 == 0)
    padded = lambda shard: jnp.pad(shard, ((0, padding), (0, 0)))
    gate_all = hidden_gather(padded(gate_weight.T))
    up_all = hidden_gather(padded(up_weight.T))
    down_all = hidden_gather(padded(down_weight))

    positions = seq_index * length + jnp.arange(length, dtype=jnp.int32)
    cosine, sine = rope_tables(positions, size)
    source = inputs.reshape(rows, width).astype(wide)
    source_unit, source_scale = rms_parts(source)
    normed = (source_unit * (1.0 + input_gain)).astype(low)
    key_proj = product_of(normed, full_key, 1, 1).reshape(micro, length, size)
    value_low = product_of(normed, full_value, 1, 1).astype(low).reshape(micro, length, size)
    key_unit, key_scale = rms_parts(key_proj)
    key_low = rotate(key_unit * (1.0 + key_gain), cosine, sine).astype(low)
    own_block = jnp.concatenate([key_low, value_low], axis=-1)
    blocks = [own_block]
    seg_blocks = [segments]
    for hop in range(1, hops + 1):
        blocks.insert(0, passed_along(own_block, "seq", hop))
        seg_blocks.insert(0, passed_along(segments, "seq", hop))
    key_seg = jnp.concatenate(seg_blocks, axis=1)
    query_proj = product_of(normed, full_query, 1, 1)
    base = seq_index * length
    attend = functools.partial(
        attention,
        micro=micro,
        length=length,
        base=base,
        projected=query_proj,
        tables=(cosine, sine),
        gain=query_gain,
        segments=segments,
        key_seg=key_seg,
        blocks=blocks,
    )
    mixed_flat, logs = attend(back=False)
    attended = product_of(mixed_flat, full_out, 1, 0)
    attended_unit, attended_scale = rms_parts(attended)
    hidden = source + attended_unit * (1.0 + attention_gain)
    hidden_unit, hidden_scale = rms_parts(hidden)
    prenorm = (hidden_unit * (1.0 + feed_gain)).astype(low)

    weights = (gate_all, up_all, down_all)
    far, near = group_gather(prenorm)
    far, far_kept, sent = feed(False, far, (), weights, False)
    near, near_kept, kept = feed(False, near, (), weights, True)
    down, _, _ = group_reduce(sent, kept)
    flat_cotangent = cotangent.reshape(rows, width)
    output, grad_down, grad_output_gain = by_rows(
        turn_kernel, (*down, hidden, flat_cotangent), (output_gain,), (low, low), 1
    )

    grad_far, grad_near = group_gather(grad_down)
    grad_far, (far_gate, far_up), sent = feed(True, grad_far, far_kept[1:], weights, False)
    grad_near, (near_gate, near_up), kept = feed(True, grad_near, near_kept[1:], weights, True)

    def down_weight_grad(ready):
        left, _ = tied(near_kept[0], ready)
        return weight_grad((far_kept[0], left), (grad_far, grad_near))

    def gate_weight_grad(ready):
        left, _ = tied(near_gate, ready)
        return weight_grad((far_gate, left), (far, near))

    grad_prenorm, grad_down_weight, grad_gate_weight = group_reduce(
        sent, kept, down_weight_grad, gate_weight_grad
    )
    shard_down = hidden_reduce(grad_down_weight)[:units]
    shard_gate = hidden_reduce(grad_gate_weight)[:units]

    grad_hidden, grad_attended, gains = by_rows(
        hidden_kernel,
        (*grad_prenorm, hidden, attended, flat_cotangent),
        (feed_gain, attention_gain),
        (wide, low),
        2,
    )
    grad_feed_gain, grad_attention_gain = gains[0], gains[1]
    grad_out = product_of(mixed_flat, grad_attended, 0, 0).astype(low)
    grad_mixed = product_of(grad_attended, full_out, 1, 1).astype(low)
    grad_query_proj, query_gains, *key_grads = attend(back=True, extra=(logs, grad_mixed))
    grad_query_gain = jnp.sum(query_gains, axis=(0, 1))
    count = dp_count * seq_count
    grad_out = reduce_first(grad_out.reshape(count, -1, width))
    grad_query = product_of(grad_query_proj, normed, 0, 0).astype(low)
    grad_query = reduce_first(grad_query.reshape(count, nq, width))
    left, _ = tied(near_up, key_grads[hops])
    grad_up_weight = weight_grad((far_up, left), (far, near))
    shard_up = hidden_reduce(grad_up_weight)[:units]
    returning = key_grads[hops]
    for hop in range(1, hops + 1):
        returning = returning + passed_along(key_grads[hops - hop], "seq", -hop).astype(wide)
    returning, grad_out, grad_query, _ = tied(returning, grad_out, grad_query, grad_up_weight)
    shard_out = reduce_rest(grad_out, ("x", "y"))
    shard_query = reduce_rest(grad_query, ("y", "x"))
    grad_key_proj, grad_key_gain = rms_back(
        key_unit, key_scale, key_gain, rotate_back(returning[..., :size], cosine, sine)
    )
    grad_key = grad_key_proj.astype(low).reshape(rows, size)
    grad_value = returning[..., size:].astype(low).reshape(rows, size)
    grad_kv = [
        product_of(grad, normed, 0, 0).astype(low).reshape(count, -1, width)
        for grad in (grad_key, grad_value)
    ]
    grad_normed = product_of(grad_query_proj, full_query, 1, 0) + product_of(grad_key, full_key, 1, 0)
    grad_normed = grad_normed + product_of(grad_value, full_value, 1, 0)
    grad_source, grad_input_gain = rms_back(source_unit, source_scale, input_gain, grad_normed)
    grad_inputs = grad_hidden + grad_source

    shard_second = reduce_rest(reduce_first(jnp.concatenate(grad_kv, axis=1)), ("y", "x"))
    gains = sum_everywhere(
        jnp.concatenate(
            [
                grad_input_gain,
                grad_attention_gain,
                grad_feed_gain,
                grad_output_gain[0],
                grad_query_gain,
                grad_key_gain,
            ]
        )
    )
    return (
        output.reshape(micro, length, width),
        grad_inputs.reshape(micro, length, width),
        shard_query.T,
        shard_second[:nk].T,
        shard_second[nk:].T,
        shard_out,
        shard_gate.T,
        shard_up.T,
        shard_down,
        gains[:width],
        gains[width : 2 * width],
        gains[2 * width : 3 * width],
        gains[3 * width : 4 * width],
        gains[4 * width : 4 * width + size],
        gains[4 * width + size :],
    )


def solution(mesh):
    in_specs = (
        P("dp", "seq", None),
        P("dp", "seq"),
        P(None, ("dp", "seq")),
        P(None, ("dp", "seq")),
        P(None, ("dp", "seq")),
        P(("dp", "seq"), None),
        P(None, ("dp", "seq")),
        P(None, ("dp", "seq")),
        P(("dp", "seq"), None),
        P(),
        P(),
        P(),
        P(),
        P(),
        P(),
        P("dp", "seq", None),
    )
    out_specs = (
        P("dp", "seq", None),
        P("dp", "seq", None),
        P(None, ("dp", "seq")),
        P(None, ("dp", "seq")),
        P(None, ("dp", "seq")),
        P(("dp", "seq"), None),
        P(None, ("dp", "seq")),
        P(None, ("dp", "seq")),
        P(("dp", "seq"), None),
        P(),
        P(),
        P(),
        P(),
        P(),
        P(),
    )
    return jax.shard_map(
        on_device, mesh=mesh, in_specs=in_specs, out_specs=out_specs, check_vma=False
    )
```

time: 782 us -> 575 us (0.74)
  matrix products: 198 us -> 61.6 us
  waiting for transfers between devices: 364 us -> 233 us
  Pallas kernels: 0 us -> 123 us
  blocking collectives: 42.8 us -> 0 us
  starting transfers between devices: 27.9 us -> 69.1 us
  other arithmetic: 63.8 us -> 30.1 us
  local copies, waits for them, and re-layouts: 62.7 us -> 32.4 us
    dot_general x30 -> x18, matrix products: 198 us -> 61.6 us  [product_of(): lax.dot_general(left, right, (((left_axis,), (right_axis,)), ((), ())), p...]
    all_gather x4 -> x3, waiting for transfers between devices: 143 us -> 15.8 us  [hidden_gather(): lax.all_gather(shard, 'dp', axis=0, axis_index_groups=column_groups(), ti...]
    pallas_call x0 -> x9, Pallas kernels: none -> 123 us  [the longest x4 102 us: feed(): pl.pallas_call(functools.partial(feed_back_kernel if back else feed_kerne...]
    ppermute x0 -> x28, waiting for transfers between devices: none -> 119 us  [the longest x14 84.1 us: along_x(): return lax.ppermute(value, 'dp', [(index, index ^ 1) for index in range(8)])]
    reduce_scatter x1 -> x3, waiting for transfers between devices: 116 us -> 0.01 us  [hidden_reduce(): lax.psum_scatter(terms.astype(low), 'dp', scatter_dimension=0, axis_index...]
    psum x1 -> x0, blocking collectives: 42.8 us -> none  [on_device(): lax.psum(jnp.concatenate([grad_input_gain, grad_attention_gain, grad_feed...]
    ppermute x0 -> x28, starting transfers between devices: none -> 32.2 us  [the longest x14 18.1 us: along_z(): lax.ppermute(value, 'dp', [(index, (index + 2 * steps) % 8) for index in...]
    ppermute x10 -> x32, waiting for transfers between devices: 97 us -> 79.1 us  [flipped(): lax.ppermute(value, 'seq', [(index, index ^ bits) for index in range(coun...]
  transfers between devices with their start and end apart: 24 -> 72, of which waited for: 13 -> 32; matrix products, arithmetic and copies ran while one was open for 35% -> 17% of each run, Pallas kernels for 0% -> 13%
where the time goes in v2:
time: 575 us; the launch traced here: 566 us
  waiting for transfers between devices  233 us (41%)
  Pallas kernels  123 us (21%)
  starting transfers between devices  69.1 us (12%)
  matrix products  61.6 us (11%)
  local copies, waits for them, and re-layouts  32.4 us (6%)
  other arithmetic  30.1 us (5%)
  between operations  16.4 us (3%)
    pallas_call x4, Pallas kernels, feed(): pl.pallas_call(functools.partial(feed_back_kernel if back else feed_kerne...  102 us
    ppermute x14, waiting for transfers between devices, along_x(): return lax.ppermute(value, 'dp', [(index, index ^ 1) for index in range(8)])  84.1 us
    ppermute x32, waiting for transfers between devices, flipped(): lax.ppermute(value, 'seq', [(index, index ^ bits) for index in range(coun...  79.1 us
    dot_general x18, matrix products, product_of(): lax.dot_general(left, right, (((left_axis,), (right_axis,)), ((), ())), p...  61.6 us
    ppermute x14, waiting for transfers between devices, along_z(): lax.ppermute(value, 'dp', [(index, (index + 2 * steps) % 8) for index in...  34.6 us
    ppermute x32, starting transfers between devices, flipped(): lax.ppermute(value, 'seq', [(index, index ^ bits) for index in range(coun...  23.5 us
    ppermute x6, waiting for transfers between devices, passed_along(): lax.ppermute(value, axis, [(source, source + steps) for source in range(l...  19.2 us
    ppermute x14, starting transfers between devices, along_z(): lax.ppermute(value, 'dp', [(index, (index + 2 * steps) % 8) for index in...  18.1 us
  transfers between devices with their start and end apart: 72, of which 32 were waited for; matrix products, arithmetic and copies ran while one was open for 17% of the time, Pallas kernels for 13%

profile of v2, /device:TPU:0, one launch (start us, length us, event | category | flops | bytes accessed | tf_op | source)
XLA Modules:
  0.0 565.7 jit_solution(6363802009685737760)
XLA Ops:
  10.3 3.1 collective-permute-start
  13.4 2.6 collective-permute-start.1
  17.3 3.4 collective-permute-start.11
  22.9 12.7 %collective-permute-done.1 = bf16[80,1152]{1,0:T(8,128)(2,1)S(1)} collective-permute-done((bf16[80,1152]{1,0:T(8,128)(2,1)S(1)}, bf16[80,1152]{1,0:T(8,128)(2,1)S(1)}, u32[]{:S(2)}, u32[]{:S(2)}) %collective-permute-start.1) | collective-permute-done | bytes 184352 | tf_op jit(solution)/shard_map/ppermute | solution.py:35
  39.0 14.9 %collective-permute-done.4 = bf16[320,1152]{1,0:T(8,128)(2,1)S(1)} collective-permute-done((bf16[320,1152]{1,0:T(8,128)(2,1)S(1)}, bf16[320,1152]{1,0:T(8,128)(2,1)S(1)}, u32[]{:S(2)}, u32[]{:S(2)}) %collective-permute-start.4) | collective-permute-done | bytes 737312 | tf_op jit(solution)/shard_map/ppermute | solution.py:21
  54.4 2.7 collective-permute-start.9
  58.7 4.9 collective-permute-done.8
  71.7 3.5 collective-permute-start.13
  76.9 3.9 fusion.53.proj
  80.8 6.7 %collective-permute-done.13.refs_0_ = bf16[2,256,512]{2,1,0:T(8,128)(2,1)S(1)} collective-permute-done((bf16[2,256,512]{2,1,0:T(8,128)(2,1)S(1)}, bf16[2,256,512]{2,1,0:T(8,128)(2,1)S(1)}, u32[]{:S(2)}, u32[]{:S(2)}) %collective-permute-start.13) | collective-permute-done | bytes 524320 | tf_op jit(solution)/shard_map/ppermute | solution.py:27
  87.6 4.8 shard_map.272
  96.3 6.6 %collective-permute-start.15 = (bf16[512,1152]{1,0:T(8,128)(2,1)S(1)}, bf16[512,1152]{1,0:T(8,128)(2,1)}, u32[]{:S(2)}, u32[]{:S(2)}) collective-permute-start(bf16[512,1152]{1,0:T(8,128)(2,1)S(1)} %multiply_convert_fusion.refs_3_), channel_id=1, source_target_pairs={{0,2},{1,3},{2,0},{3,1},{4,6},{5,7},{6,4},{7,5},{8,10},{9,11},{10,... | collective-permute-start | bytes 3538952 | tf_op jit(solution)/shard_map/ppermute | solution.py:21
  104.2 24.3 %collective-permute-done.15.refs_2_ = bf16[512,1152]{1,0:T(8,128)(2,1)} collective-permute-done((bf16[512,1152]{1,0:T(8,128)(2,1)S(1)}, bf16[512,1152]{1,0:T(8,128)(2,1)}, u32[]{:S(2)}, u32[]{:S(2)}) %collective-permute-start.15) | collective-permute-done | bytes 1179680 | tf_op jit(solution)/shard_map/ppermute | solution.py:21
  132.0 11.7 %collective-permute-done.16 = bf16[256,1152]{1,0:T(8,128)(2,1)S(1)} collective-permute-done((bf16[256,1152]{1,0:T(8,128)(2,1)S(1)}, bf16[256,1152]{1,0:T(8,128)(2,1)S(1)}, u32[]{:S(2)}, u32[]{:S(2)}) %collective-permute-start.16) | collective-permute-done | bytes 589856 | tf_op jit(solution)/shard_map/ppermute | solution.py:39
  145.8 15.8 %all-gather.8.cloned.1.call-done.refs_6_.refs_8_ = bf16[896,1152]{1,0:T(8,128)(2,1)} async-done(((bf16[224,1152]{1,0:T(8,128)(2,1)}), bf16[896,1152]{1,0:T(8,128)(2,1)}) %all-gather.8.cloned.1.call-update) | async-done | bytes 2064400 | tf_op jit(solution)/shard_map/all_gather | solution.py:47
  161.6 24.7 %shard_map.274 = (bf16[2048,1152]{1,0:T(8,128)(2,1)}, bf16[2048,896]{1,0:T(8,128)(2,1)}, bf16[2048,896]{1,0:T(8,128)(2,1)}, bf16[2048,896]{1,0:T(8,128)(2,1)}, bf16[2048,1152]{1,0:T(8,128)(2,1)}) custom-call(bf16[512,1152]{1,0:T(8,128)(2,1)} %collective-permute-done.19.refs_0_, bf16[512,1152]{1,0:T(8,128)(2,1)} %collective-permute-done.20.refs_1_, ...), custom_call_target="tpu_custom_call" | custom-call | flops 12683575296 | bytes 43417600 | tf_op jit(solution)/shard_map/pallas_call | solution.py:310
  186.3 26.1 %shard_map.273 = (bf16[2048,1152]{1,0:T(8,128)(2,1)}, bf16[2048,896]{1,0:T(8,128)(2,1)}, bf16[2048,896]{1,0:T(8,128)(2,1)}, bf16[2048,896]{1,0:T(8,128)(2,1)}, b...) custom-call(bf16[512,1152]{1,0:T(8,128)(2,1)} %constant_dynamic-update-sl, ...), custom_call_target="tpu_custom_call" | custom-call | flops 12683575296 | bytes 43417600 | tf_op jit(solution)/shard_map/pallas_call | solution.py:310
  217.2 12.8 %collective-permute-done.24 = bf16[256,1152]{1,0:T(8,128)(2,1)S(1)} collective-permute-done((bf16[256,1152]{1,0:T(8,128)(2,1)S(1)}, bf16[256,1152]{1,0:T(8,128)(2,1)S(1)}, u32[]{:S(2)}, u32[]{:S(2)}) %collective-permute-start.24) | collective-permute-done | bytes 589856 | tf_op jit(solution)/shard_map/ppermute | solution.py:39
  234.2 25.1 %collective-permute-done.26.refs_2_ = bf16[512,1152]{1,0:T(8,128)(2,1)S(1)} collective-permute-done((bf16[512,1152]{1,0:T(8,128)(2,1)S(1)}, bf16[512,1152]{1,0:T(8,128)(2,1)S(1)}, u32[]{:S(2)}, u32[]{:S(2)}) %collective-permute-start.26) | collective-permute-done | bytes 1179680 | tf_op jit(solution)/shard_map/ppermute | solution.py:39
  259.6 2.7 shard_map.275
  265.2 23.2 %collective-permute-done.28.refs_2_ = bf16[512,1152]{1,0:T(8,128)(2,1)S(1)} collective-permute-done((bf16[512,1152]{1,0:T(8,128)(2,1)S(1)}, bf16[512,1152]{1,0:T(8,128)(2,1)S(1)}, u32[]{:S(2)}, u32[]{:S(2)}) %collective-permute-start.28) | collective-permute-done | bytes 1179680 | tf_op jit(solution)/shard_map/ppermute | solution.py:21
  292.0 10.3 %collective-permute-done.29 = bf16[256,1152]{1,0:T(8,128)(2,1)S(1)} collective-permute-done((bf16[256,1152]{1,0:T(8,128)(2,1)S(1)}, bf16[256,1152]{1,0:T(8,128)(2,1)S(1)}, u32[]{:S(2)}, u32[]{:S(2)}) %collective-permute-start.29) | collective-permute-done | bytes 589856 | tf_op jit(solution)/shard_map/ppermute | solution.py:39
  302.6 2.8 collective-permute-done.32.refs_0_
  306.3 24.4 %shard_map.277 = (bf16[2048,1152]{1,0:T(8,128)(2,1)}, bf16[2048,896]{1,0:T(8,128)(2,1)}, bf16[2048,896]{1,0:T(8,128)(2,1)}, bf16[2048,1152]{1,0:T(8,128)(2,1)}) custom-call(bf16[512,1152]{1,0:T(8,128)(2,1)} %copy-done.90, bf16[512,1152]{1,0:T(8,128)(2,1)} %copy-done.88, bf16[512,1152]{1,0:T(8,128)(2,1)} %copy-done.89, bf16[512,1152]{1,0:T(8,128)(2,1)} %copy-done.87, ...), custom_call_target="tpu_custom_call" | custom-call | flops 12683575296 | bytes 43417600 | tf_op jit(solution)/shard_map/pallas_call | solution.py:310
  331.0 26.5 %shard_map.276 = (bf16[2048,1152]{1,0:T(8,128)(2,1)}, bf16[2048,896]{1,0:T(8,128)(2,1)}, bf16[2048,896]{1,0:T(8,128)(2,1)}, bf16[512,1152]{1,0:T(8,128)(2,1)}, b...) custom-call(bf16[512,1152]{1,0:T(8,128)(2,1)} %copy-done.67, ...), custom_call_target="tpu_custom_call" | custom-call | flops 12683575296 | bytes 43417600 | tf_op jit(solution)/shard_map/pallas_call | solution.py:310
  357.5 2.6 add_convert_fusion.2
  363.4 7.4 %fusion.54 = f32[896,1152]{1,0:T(8,128)S(1)} fusion(bf16[2048,896]{1,0:T(8,128)(2,1)} %get-tuple-element.135, bf16[2048,1152]{1,0:T(8,128)(2,1)S(1)} %copy-done.94), kind=kOutput, calls=%fused_computation.175 | convolution fusion | flops 4227858432 | bytes 12517376 | tf_op jit(solution)/shard_map/dot_general | solution.py:169
  370.8 6.5 %fusion = bf16[896,1152]{1,0:T(8,128)(2,1)} fusion(f32[896,1152]{1,0:T(8,128)S(1)} %fusion.54, bf16[2048,896]{1,0:T(8,128)(2,1)S(1)} %copy-done.91, bf16[2048,1152]{1,0:T(8,128)(2,1)S(1)} %bitcast.248), kind=kOutput, calls=%fused_computation.5 | convolution fusion | flops 4229922816 | bytes 14581760 | tf_op jit(solution)/shard_map/dot_general | solution.py:169
  377.3 2.6 slice.136.refs_1_
  379.9 4.2 add_convert_fusion
  386.2 8.7 %fusion.55 = f32[896,1152]{1,0:T(8,128)S(1)} fusion(bf16[2048,896]{1,0:T(8,128)(2,1)} %get-tuple-element.151, bf16[2048,1152]{1,0:T(8,128)(2,1)} %get-tuple-element.152), kind=kOutput, calls=%fused_computation.176 | convolution fusion | flops 4227858432 | bytes 12517376 | tf_op jit(solution)/shard_map/dot_general | solution.py:169
  394.9 8.8 %fusion.1 = bf16[896,1152]{1,0:T(8,128)(2,1)} fusion(f32[896,1152]{1,0:T(8,128)S(1)} %fusion.55, bf16[2048,896]{1,0:T(8,128)(2,1)S(1)} %copy-done.93, bf16[2048,1152]{1,0:T(8,128)(2,1)} %get-tuple-element.149), kind=kOutput, calls=%fused_computation.6 | convolution fusion | flops 4229922816 | bytes 14581760 | tf_op jit(solution)/shard_map/dot_general | solution.py:169
  403.8 8.2 %collective-permute-done.39.refs_2_ = bf16[512,1152]{1,0:T(8,128)(2,1)} collective-permute-done((bf16[512,1152]{1,0:T(8,128)(2,1)}, bf16[512,1152]{1,0:T(8,128)(2,1)}, u32[]{:S(2)}, u32[]{:S(2)}) %collective-permute-start.39) | collective-permute-done | bytes 1179680 | tf_op jit(solution)/shard_map/ppermute | solution.py:39
  417.6 4.9 shard_map.278
  426.4 7.0 %shard_map.279 = (bf16[512,1024]{1,0:T(8,128)(2,1)S(1)}, f32[2,1,256]{2,1,0:T(1,128)S(1)}, bf16[2,256,512]{2,1,0:T(8,128)(2,1)S(1)}, bf16[2,256,512]{2,1,0:T(8,128)(2,1)S(1)}, f32[2,256,512]{2,1,0:T(8,128)S(1)}) custom-call(s32[1]{0:T(128)} %bitcast.1.base, f32[512,1024]{1,0:T(8,128)S(1)} %copy-done.41, f32[256,256]{1,0:T(8,128)S(1)} %copy-done.11, ...), custom_call_target="tpu_custom_call" | custom-call | flops 4026531840 | bytes 10485760 | tf_op jit(solution)/shard_map/pallas_call | solution.py:476
  433.5 5.2 fusion.57
  438.8 6.5 %fusion.2 = bf16[896,1152]{1,0:T(8,128)(2,1)} fusion(f32[896,1152]{1,0:T(8,128)S(1)} %fusion.57, bf16[2048,896]{1,0:T(8,128)(2,1)S(1)} %copy-done.92, bf16[2048,1152]{1,0:T(8,128)(2,1)S(1)} %bitcast.246), kind=kOutput, calls=%fused_computation.7 | convolution fusion | flops 4229922816 | bytes 14581760 | tf_op jit(solution)/shard_map/dot_general | solution.py:169
  445.7 3.2 convolution_convert_fusion
  459.8 2.9 fusion.56
  462.9 12.5 %collective-permute-done.42 = bf16[2,256,512]{2,1,0:T(8,128)(2,1)} collective-permute-done((bf16[2,256,512]{2,1,0:T(8,128)(2,1)S(1)}, bf16[2,256,512]{2,1,0:T(8,128)(2,1)}, u32[]{:S(2)}, u32[]{:S(2)}) %collective-permute-start.42) | collective-permute-done | bytes 524320 | tf_op jit(solution)/shard_map/ppermute | solution.py:27
  487.2 3.4 collective-permute-done.62
  491.8 10.1 %collective-permute-done.63 = f32[5120]{0:T(1024)S(1)} collective-permute-done((f32[5120]{0:T(1024)S(1)}, f32[5120]{0:T(1024)S(1)}, u32[]{:S(2)}, u32[]{:S(2)}) %collective-permute-start.63) | collective-permute-done | bytes 20512 | tf_op jit(solution)/shard_map/ppermute | solution.py:39
  503.1 5.7 %collective-permute-done.64 = f32[5120]{0:T(1024)S(1)} collective-permute-done((f32[5120]{0:T(1024)S(1)}, f32[5120]{0:T(1024)S(1)}, u32[]{:S(2)}, u32[]{:S(2)}) %collective-permute-start.64) | collective-permute-done | bytes 20512 | tf_op jit(solution)/shard_map/ppermute | solution.py:35
  510.8 4.1 collective-permute-done.65
  518.9 6.2 %collective-permute-done.57 = bf16[4,32,1152]{2,1,0:T(8,128)(2,1)S(1)} collective-permute-done((bf16[4,32,1152]{2,1,0:T(8,128)(2,1)S(1)}, bf16[4,32,1152]{2,1,0:T(8,128)(2,1)S(1)}, u32[]{:S(2)}, u32[]{:S(2)}) %collective-permute-start.57) | collective-permute-done | bytes 294944 | tf_op jit(solution)/shard_map/ppermute | solution.py:21
  531.3 7.1 %collective-permute-done.58 = bf16[32,1152]{1,0:T(8,128)(2,1)S(1)} collective-permute-done((bf16[32,1152]{1,0:T(8,128)(2,1)S(1)}, bf16[32,1152]{1,0:T(8,128)(2,1)S(1)}, u32[]{:S(2)}, u32[]{:S(2)}) %collective-permute-start.58) | collective-permute-done | bytes 73760 | tf_op jit(solution)/shard_map/ppermute | solution.py:35
  539.4 3.4 collective-permute-start.49
  548.6 3.3 collective-permute-done.55
  (452 shorter events, 114.9 us)
Async XLA Ops:
  7.2 138.6 %all-gather.4.cloned.1.call-start = ((), (), s32[]{:S(2)}) async-start(), calls=%async_computation.3 | async-start | bytes 2580480 | tf_op jit(solution)/shard_map/all_gather | solution.py:47
  9.3 136.5 %all-gather.6.cloned.1.call-start = ((), (), s32[]{:S(2)}) async-start(), calls=%async_computation.4 | async-start | bytes 2580480 | tf_op jit(solution)/shard_map/all_gather | solution.py:47
  10.3 12.6 %collective-permute-start = (bf16[80,1152]{1,0:T(8,128)(2,1)S(1)}, bf16[80,1152]{1,0:T(8,128)(2,1)S(1)}, u32[]{:S(2)}, u32[]{:S(2)}) collective-permute-start(bf16[80,1152]{1,0:T(8,128)(2,1)S(1)} %pad_maximum_fusion.2), channel_id=1, source_target_pairs={{0,8},{4,12},{8,16},{12,20},{16,24},{20,28},{24,0},{28,4},{1,9},{5... | collective-permute-start | bytes 552968 | tf_op jit(solution)/shard_map/ppermute | solution.py:35
  13.4 22.2 %collective-permute-start.1 = (bf16[80,1152]{1,0:T(8,128)(2,1)S(1)}, bf16[80,1152]{1,0:T(8,128)(2,1)S(1)}, u32[]{:S(2)}, u32[]{:S(2)}) collective-permute-start(bf16[80,1152]{1,0:T(8,128)(2,1)S(1)} %pad_maximum_fusion.2), channel_id=1, source_target_pairs={{0,16},{4,20},{8,24},{12,28},{16,0},{20,4},{24,8},{28,12},{1,17},{... | collective-permute-start | bytes 552968 | tf_op jit(solution)/shard_map/ppermute | solution.py:35
  16.0 19.6 %collective-permute-start.2 = (bf16[80,1152]{1,0:T(8,128)(2,1)S(1)}, bf16[80,1152]{1,0:T(8,128)(2,1)S(1)}, u32[]{:S(2)}, u32[]{:S(2)}) collective-permute-start(bf16[80,1152]{1,0:T(8,128)(2,1)S(1)} %pad_maximum_fusion.2), channel_id=1, source_target_pairs={{0,24},{4,28},{8,0},{12,4},{16,8},{20,12},{24,16},{28,20},{1,25},{... | collective-permute-start | bytes 552968 | tf_op jit(solution)/shard_map/ppermute | solution.py:35
  17.3 59.2 %collective-permute-start.11 = (s32[2,256]{1,0:T(2,128)}, s32[2,256]{1,0:T(2,128)S(1)}, u32[]{:S(2)}, u32[]{:S(2)}) collective-permute-start(s32[2,256]{1,0:T(2,128)} %param.17), channel_id=1, source_target_pairs={{0,2},{1,3},{4,6},{5,7},{8,10},{9,11},{12,14},{13,15},{16,18},{17,... | collective-permute-start | bytes 6152 | tf_op jit(solution)/shard_map/ppermute | solution.py:27
  22.7 138.9 %all-gather.8.cloned.1.call-start = ((), (), s32[]{:S(2)}) async-start(), calls=%async_computation.5 | async-start | bytes 2580480 | tf_op jit(solution)/shard_map/all_gather | solution.py:47
  35.7 18.3 %collective-permute-start.4 = (bf16[320,1152]{1,0:T(8,128)(2,1)S(1)}, bf16[320,1152]{1,0:T(8,128)(2,1)S(1)}, u32[]{:S(2)}, u32[]{:S(2)}) collective-permute-start(bf16[320,1152]{1,0:T(8,128)(2,1)S(1)} %constant_dynamic-update-slice_fusion), channel_id=1, source_target_pairs={{0,2},{1,3},{2,0},{3,1},{4,6},{5,7},{6,4},{7,5},{8,10},{9,11},{10,... | collective-permute-start | bytes 2211848 | tf_op jit(solution)/shard_map/ppermute | solution.py:21
  37.3 17.0 %collective-permute-start.6 = (bf16[320,1152]{1,0:T(8,128)(2,1)S(1)}, bf16[320,1152]{1,0:T(8,128)(2,1)S(1)}, u32[]{:S(2)}, u32[]{:S(2)}) collective-permute-start(bf16[320,1152]{1,0:T(8,128)(2,1)S(1)} %constant_dynamic-update-slice_fusion), channel_id=1, source_target_pairs={{0,4},{4,0},{8,12},{12,8},{16,20},{20,16},{24,28},{28,24},{1,5},{5... | collective-permute-start | bytes 2211848 | tf_op jit(solution)/shard_map/ppermute | solution.py:39
  64.6 12.0 %collective-permute-start.12 = (s32[2,256]{1,0:T(2,128)S(1)}, s32[2,256]{1,0:T(2,128)S(1)}, u32[]{:S(2)}, u32[]{:S(2)}) collective-permute-start(s32[2,256]{1,0:T(2,128)S(1)} %copy-done.84), channel_id=1, source_target_pairs={{0,1},{1,2},{2,3},{4,5},{5,6},{6,7},{8,9},{9,10},{10,11},{12,13},{... | collective-permute-start | bytes 6152 | tf_op jit(solution)/shard_map/ppermute | solution.py:27
  71.7 15.8 %collective-permute-start.13 = (bf16[2,256,512]{2,1,0:T(8,128)(2,1)S(1)}, bf16[2,256,512]{2,1,0:T(8,128)(2,1)S(1)}, u32[]{:S(2)}, u32[]{:S(2)}) collective-permute-start(bf16[2,256,512]{2,1,0:T(8,128)(2,1)S(1)} %pad_maximum_fusion.refs_2_), channel_id=1, source_target_pairs={{0,2},{1,3},{4,6},{5,7},{8,10},{9,11},{12,14},{13,15},{16,18},{17,... | collective-permute-start | bytes 1572872 | tf_op jit(solution)/shard_map/ppermute | solution.py:27
  75.1 12.3 %collective-permute-start.14 = (bf16[2,256,512]{2,1,0:T(8,128)(2,1)S(1)}, bf16[2,256,512]{2,1,0:T(8,128)(2,1)S(1)}, u32[]{:S(2)}, u32[]{:S(2)}) collective-permute-start(bf16[2,256,512]{2,1,0:T(8,128)(2,1)S(1)} %pad_maximum_fusion.refs_2_), channel_id=1, source_target_pairs={{0,1},{1,2},{2,3},{4,5},{5,6},{6,7},{8,9},{9,10},{10,11},{12,13},{... | collective-permute-start | bytes 1572872 | tf_op jit(solution)/shard_map/ppermute | solution.py:27
  96.3 32.2 %collective-permute-start.15 = (bf16[512,1152]{1,0:T(8,128)(2,1)S(1)}, bf16[512,1152]{1,0:T(8,128)(2,1)}, u32[]{:S(2)}, u32[]{:S(2)}) collective-permute-start(bf16[512,1152]{1,0:T(8,128)(2,1)S(1)} %multiply_convert_fusion.refs_3_), channel_id=1, source_target_pairs={{0,2},{1,3},{2,0},{3,1},{4,6},{5,7},{6,4},{7,5},{8,10},{9,11},{10,... | collective-permute-start | bytes 3538952 | tf_op jit(solution)/shard_map/ppermute | solution.py:21
  102.9 27.1 %collective-permute-start.17 = (bf16[512,1152]{1,0:T(8,128)(2,1)S(1)}, bf16[512,1152]{1,0:T(8,128)(2,1)}, u32[]{:S(2)}, u32[]{:S(2)}) collective-permute-start(bf16[512,1152]{1,0:T(8,128)(2,1)S(1)} %multiply_convert_fusion.refs_3_), channel_id=1, source_target_pairs={{0,4},{4,0},{8,12},{12,8},{16,20},{20,16},{24,28},{28,24},{1,5},{5... | collective-permute-start | bytes 3538952 | tf_op jit(solution)/shard_map/ppermute | solution.py:39
  104.1 448.4 %reduce-scatter.8.cloned.1.call-start = ((), (), s32[]{:S(2)}) async-start(), calls=%async_computation.8 | async-start | bytes 2580480 | tf_op jit(solution)/shard_map/reduce_scatter | solution.py:51
  129.6 14.0 %collective-permute-start.16 = (bf16[256,1152]{1,0:T(8,128)(2,1)S(1)}, bf16[256,1152]{1,0:T(8,128)(2,1)S(1)}, u32[]{:S(2)}, u32[]{:S(2)}) collective-permute-start(bf16[256,1152]{1,0:T(8,128)(2,1)S(1)} %slice.159), channel_id=1, source_target_pairs={{0,4},{4,0},{8,12},{12,8},{16,20},{20,16},{24,28},{28,24},{1,5},{5... | collective-permute-start | bytes 1769480 | tf_op jit(solution)/shard_map/ppermute | solution.py:39
  131.2 13.8 %collective-permute-start.18 = (bf16[256,1152]{1,0:T(8,128)(2,1)S(1)}, bf16[256,1152]{1,0:T(8,128)(2,1)S(1)}, u32[]{:S(2)}, u32[]{:S(2)}) collective-permute-start(bf16[256,1152]{1,0:T(8,128)(2,1)S(1)} %slice.160), channel_id=1, source_target_pairs={{0,2},{1,3},{2,0},{3,1},{4,6},{5,7},{6,4},{7,5},{8,10},{9,11},{10,... | collective-permute-start | bytes 1769480 | tf_op jit(solution)/shard_map/ppermute | solution.py:21
  131.5 30.1 %collective-permute-start.22 = (bf16[512,1152]{1,0:T(8,128)(2,1)S(1)}, bf16[512,1152]{1,0:T(8,128)(2,1)}, u32[]{:S(2)}, u32[]{:S(2)}) collective-permute-start(bf16[512,1152]{1,0:T(8,128)(2,1)S(1)} %multiply_convert_fusion.refs_3_), channel_id=1, source_target_pairs={{0,1},{1,0},{2,3},{3,2},{4,5},{5,4},{6,7},{7,6},{8,9},{9,8},{10,11... | collective-permute-start | bytes 3538952 | tf_op jit(solution)/shard_map/ppermute | solution.py:21
  131.5 30.1 %collective-permute-start.20 = (bf16[512,1152]{1,0:T(8,128)(2,1)}, bf16[512,1152]{1,0:T(8,128)(2,1)}, u32[]{:S(2)}, u32[]{:S(2)}) collective-permute-start(bf16[512,1152]{1,0:T(8,128)(2,1)} %collective-permute-done.17.refs_1_), channel_id=1, source_target_pairs={{0,1},{1,0},{2,3},{3,2},{4,5},{5,4},{6,7},{7,6},{8,9},{9,8},{10,11... | collective-permute-start | bytes 3538952 | tf_op jit(solution)/shard_map/ppermute | solution.py:21
  132.0 29.6 %collective-permute-start.21 = (bf16[512,1152]{1,0:T(8,128)(2,1)}, bf16[512,1152]{1,0:T(8,128)(2,1)}, u32[]{:S(2)}, u32[]{:S(2)}) collective-permute-start(bf16[512,1152]{1,0:T(8,128)(2,1)} %collective-permute-done.15.refs_2_), channel_id=1, source_target_pairs={{0,1},{1,0},{2,3},{3,2},{4,5},{5,4},{6,7},{7,6},{8,9},{9,8},{10,11... | collective-permute-start | bytes 3538952 | tf_op jit(solution)/shard_map/ppermute | solution.py:21
  145.8 15.8 %collective-permute-start.19 = (bf16[512,1152]{1,0:T(8,128)(2,1)}, bf16[512,1152]{1,0:T(8,128)(2,1)}, u32[]{:S(2)}, u32[]{:S(2)}) collective-permute-start(bf16[512,1152]{1,0:T(8,128)(2,1)} %constant_dynamic-update-slice_fusion.9.refs_0_), channel_id=1, source_target_pairs={{0,1},{1,0},{2,3},{3,2},{4,5},{5,4},{6,7},{7,6},{8,9},{9,8},{10,11... | collective-permute-start | bytes 3538952 | tf_op jit(solution)/shard_map/ppermute | solution.py:21
  186.3 26.1 %collective-permute-start.23 = (bf16[2048,1152]{1,0:T(8,128)(2,1)}, bf16[2048,1152]{1,0:T(8,128)(2,1)S(1)}, u32[]{:S(2)}, u32[]{:S(2)}) collective-permute-start(bf16[2048,1152]{1,0:T(8,128)(2,1)} %get-tuple-element.100), channel_id=1, source_target_pairs={{0,1},{1,0},{2,3},{3,2},{4,5},{5,4},{6,7},{7,6},{8,9},{9,8},{10,11... | collective-permute-start | bytes 14155784 | tf_op jit(solution)/shard_map/ppermute | solution.py:21
  214.2 15.8 %collective-permute-start.24 = (bf16[256,1152]{1,0:T(8,128)(2,1)S(1)}, bf16[256,1152]{1,0:T(8,128)(2,1)S(1)}, u32[]{:S(2)}, u32[]{:S(2)}) collective-permute-start(bf16[256,1152]{1,0:T(8,128)(2,1)S(1)} %get-tuple-element.196), channel_id=1, source_target_pairs={{0,4},{4,0},{8,12},{12,8},{16,20},{20,16},{24,28},{28,24},{1,5},{5... | collective-permute-start | bytes 1769480 | tf_op jit(solution)/shard_map/ppermute | solution.py:39
  215.8 15.4 %collective-permute-start.25 = (bf16[256,1152]{1,0:T(8,128)(2,1)S(1)}, bf16[256,1152]{1,0:T(8,128)(2,1)S(1)}, u32[]{:S(2)}, u32[]{:S(2)}) collective-permute-start(bf16[256,1152]{1,0:T(8,128)(2,1)S(1)} %get-tuple-element.195), channel_id=1, source_target_pairs={{0,2},{1,3},{2,0},{3,1},{4,6},{5,7},{6,4},{7,5},{8,10},{9,11},{10,... | collective-permute-start | bytes 1769480 | tf_op jit(solution)/shard_map/ppermute | solution.py:21
  232.0 27.3 %collective-permute-start.26 = (bf16[512,1152]{1,0:T(8,128)(2,1)S(1)}, bf16[512,1152]{1,0:T(8,128)(2,1)S(1)}, u32[]{:S(2)}, u32[]{:S(2)}) collective-permute-start(bf16[512,1152]{1,0:T(8,128)(2,1)S(1)} %get-tuple-element.115), channel_id=1, source_target_pairs={{0,4},{4,0},{8,12},{12,8},{16,20},{20,16},{24,28},{28,24},{1,5},{5... | collective-permute-start | bytes 3538952 | tf_op jit(solution)/shard_map/ppermute | solution.py:39
  232.6 27.0 %collective-permute-start.27 = (bf16[512,1152]{1,0:T(8,128)(2,1)S(1)}, bf16[512,1152]{1,0:T(8,128)(2,1)S(1)}, u32[]{:S(2)}, u32[]{:S(2)}) collective-permute-start(bf16[512,1152]{1,0:T(8,128)(2,1)S(1)} %get-tuple-element.116), channel_id=1, source_target_pairs={{0,2},{1,3},{2,0},{3,1},{4,6},{5,7},{6,4},{7,5},{8,10},{9,11},{10,... | collective-permute-start | bytes 3538952 | tf_op jit(solution)/shard_map/ppermute | solution.py:21
  262.3 26.1 %collective-permute-start.28 = (bf16[512,1152]{1,0:T(8,128)(2,1)S(1)}, bf16[512,1152]{1,0:T(8,128)(2,1)S(1)}, u32[]{:S(2)}, u32[]{:S(2)}) collective-permute-start(bf16[512,1152]{1,0:T(8,128)(2,1)S(1)} %get-tuple-element.120.refs_3_), channel_id=1, source_target_pairs={{0,2},{1,3},{2,0},{3,1},{4,6},{5,7},{6,4},{7,5},{8,10},{9,11},{10,... | collective-permute-start | bytes 3538952 | tf_op jit(solution)/shard_map/ppermute | solution.py:21
  263.8 26.9 %collective-permute-start.30 = (bf16[512,1152]{1,0:T(8,128)(2,1)S(1)}, bf16[512,1152]{1,0:T(8,128)(2,1)S(1)}, u32[]{:S(2)}, u32[]{:S(2)}) collective-permute-start(bf16[512,1152]{1,0:T(8,128)(2,1)S(1)} %get-tuple-element.120.refs_3_), channel_id=1, source_target_pairs={{0,4},{4,0},{8,12},{12,8},{16,20},{20,16},{24,28},{28,24},{1,5},{5... | collective-permute-start | bytes 3538952 | tf_op jit(solution)/shard_map/ppermute | solution.py:39
  288.5 13.8 %collective-permute-start.29 = (bf16[256,1152]{1,0:T(8,128)(2,1)S(1)}, bf16[256,1152]{1,0:T(8,128)(2,1)S(1)}, u32[]{:S(2)}, u32[]{:S(2)}) collective-permute-start(bf16[256,1152]{1,0:T(8,128)(2,1)S(1)} %slice.162), channel_id=1, source_target_pairs={{0,4},{4,0},{8,12},{12,8},{16,20},{20,16},{24,28},{28,24},{1,5},{5... | collective-permute-start | bytes 1769480 | tf_op jit(solution)/shard_map/ppermute | solution.py:39
  330.8 26.7 %collective-permute-start.36 = (bf16[2048,1152]{1,0:T(8,128)(2,1)}, bf16[2048,1152]{1,0:T(8,128)(2,1)S(1)}, u32[]{:S(2)}, u32[]{:S(2)}) collective-permute-start(bf16[2048,1152]{1,0:T(8,128)(2,1)} %get-tuple-element.126), channel_id=1, source_target_pairs={{0,1},{1,0},{2,3},{3,2},{4,5},{5,4},{6,7},{7,6},{8,9},{9,8},{10,11... | collective-permute-start | bytes 14155784 | tf_op jit(solution)/shard_map/ppermute | solution.py:21
  361.2 18.6 %collective-permute-start.37 = (bf16[256,1152]{1,0:T(8,128)(2,1)}, bf16[256,1152]{1,0:T(8,128)(2,1)}, u32[]{:S(2)}, u32[]{:S(2)}) collective-permute-start(bf16[256,1152]{1,0:T(8,128)(2,1)} %get-tuple-element.194), channel_id=1, source_target_pairs={{0,4},{4,0},{8,12},{12,8},{16,20},{20,16},{24,28},{28,24},{1,5},{5... | collective-permute-start | bytes 1769480 | tf_op jit(solution)/shard_map/ppermute | solution.py:39
  362.6 17.2 %collective-permute-start.38 = (bf16[256,1152]{1,0:T(8,128)(2,1)}, bf16[256,1152]{1,0:T(8,128)(2,1)}, u32[]{:S(2)}, u32[]{:S(2)}) collective-permute-start(bf16[256,1152]{1,0:T(8,128)(2,1)} %get-tuple-element.193), channel_id=1, source_target_pairs={{0,2},{1,3},{2,0},{3,1},{4,6},{5,7},{6,4},{7,5},{8,10},{9,11},{10,... | collective-permute-start | bytes 1769480 | tf_op jit(solution)/shard_map/ppermute | solution.py:21
  384.0 28.0 %collective-permute-start.39 = (bf16[512,1152]{1,0:T(8,128)(2,1)}, bf16[512,1152]{1,0:T(8,128)(2,1)}, u32[]{:S(2)}, u32[]{:S(2)}) collective-permute-start(bf16[512,1152]{1,0:T(8,128)(2,1)} %get-tuple-element.146), channel_id=1, source_target_pairs={{0,4},{4,0},{8,12},{12,8},{16,20},{20,16},{24,28},{28,24},{1,5},{5... | collective-permute-start | bytes 3538952 | tf_op jit(solution)/shard_map/ppermute | solution.py:39
  385.3 27.7 %collective-permute-start.40 = (bf16[512,1152]{1,0:T(8,128)(2,1)}, bf16[512,1152]{1,0:T(8,128)(2,1)}, u32[]{:S(2)}, u32[]{:S(2)}) collective-permute-start(bf16[512,1152]{1,0:T(8,128)(2,1)} %get-tuple-element.147), channel_id=1, source_target_pairs={{0,2},{1,3},{2,0},{3,1},{4,6},{5,7},{6,4},{7,5},{8,10},{9,11},{10,... | collective-permute-start | bytes 3538952 | tf_op jit(solution)/shard_map/ppermute | solution.py:21
  386.0 168.5 %reduce-scatter.6.cloned.1.call-start = ((), (), s32[]{:S(2)}) async-start(), calls=%async_computation.7 | async-start | bytes 2580480 | tf_op jit(solution)/shard_map/reduce_scatter | solution.py:51
  445.3 111.3 %reduce-scatter.4.cloned.1.call-start = ((), (), s32[]{:S(2)}) async-start(), calls=%async_computation.6 | async-start | bytes 2580480 | tf_op jit(solution)/shard_map/reduce_scatter | solution.py:51
  451.3 25.4 %collective-permute-start.44 = (bf16[4,2,2,32,1152]{4,3,0,1,2:T(8,128)(2,1)}, bf16[4,2,2,32,1152]{4,3,0,1,2:T(8,128)(2,1)}, u32[]{:S(2)}, u32[]{:S(2)}) collective-permute-start(bf16[4,2,2,32,1152]{4,3,0,1,2:T(8,128)(2,1)} %bitcast.202), channel_id=1, source_target_pairs={{0,1},{1,0},{2,3},{3,2},{4,5},{5,4},{6,7},{7,6},{8,9},{9,8},{10,11... | collective-permute-start | bytes 3538952 | tf_op jit(solution)/shard_map/ppermute | solution.py:21
  455.0 20.4 %collective-permute-start.42 = (bf16[2,256,512]{2,1,0:T(8,128)(2,1)S(1)}, bf16[2,256,512]{2,1,0:T(8,128)(2,1)}, u32[]{:S(2)}, u32[]{:S(2)}) collective-permute-start(bf16[2,256,512]{2,1,0:T(8,128)(2,1)S(1)} %get-tuple-element.161), channel_id=1, source_target_pairs={{2,0},{3,1},{6,4},{7,5},{10,8},{11,9},{14,12},{15,13},{18,16},{19,... | collective-permute-start | bytes 1572872 | tf_op jit(solution)/shard_map/ppermute | solution.py:27
  458.7 19.7 %collective-permute-start.43 = (bf16[4,2,2,32,1152]{4,3,0,2,1:T(8,128)(2,1)}, bf16[4,2,2,32,1152]{4,3,0,2,1:T(8,128)(2,1)}, u32[]{:S(2)}, u32[]{:S(2)}) collective-permute-start(bf16[4,2,2,32,1152]{4,3,0,2,1:T(8,128)(2,1)} %bitcast.203), channel_id=1, source_target_pairs={{0,1},{1,0},{2,3},{3,2},{4,5},{5,4},{6,7},{7,6},{8,9},{9,8},{10,11... | collective-permute-start | bytes 3538952 | tf_op jit(solution)/shard_map/ppermute | solution.py:21
  485.7 30.5 %collective-permute-start.56 = (bf16[4,2,32,1152]{3,2,0,1:T(8,128)(2,1)S(1)}, bf16[4,2,32,1152]{3,2,0,1:T(8,128)(2,1)S(1)}, u32[]{:S(2)}, u32[]{:S(2)}) collective-permute-start(bf16[4,2,32,1152]{3,2,0,1:T(8,128)(2,1)S(1)} %fusion.19), channel_id=1, source_target_pairs={{0,4},{4,0},{8,12},{12,8},{16,20},{20,16},{24,28},{28,24},{1,5},{5... | collective-permute-start | bytes 1769480 | tf_op jit(solution)/shard_map/ppermute | solution.py:39
  487.0 29.4 %collective-permute-start.50 = (bf16[4,2,2,16,1152]{4,3,0,1,2:T(8,128)(2,1)S(1)}, bf16[4,2,2,16,1152]{4,3,0,1,2:T(8,128)(2,1)S(1)}, u32[]{:S(2)}, u32[]{:S(2)}) collective-permute-start(bf16[4,2,2,16,1152]{4,3,0,1,2:T(8,128)(2,1)S(1)} %bitcast.234), channel_id=1, source_target_pairs={{0,1},{1,0},{2,3},{3,2},{4,5},{5,4},{6,7},{7,6},{8,9},{9,8},{10,11... | collective-permute-start | bytes 1769480 | tf_op jit(solution)/shard_map/ppermute | solution.py:21
  491.7 26.9 %collective-permute-start.45 = (bf16[4,2,32,1152]{3,2,0,1:T(8,128)(2,1)S(1)}, bf16[4,2,32,1152]{3,2,0,1:T(8,128)(2,1)S(1)}, u32[]{:S(2)}, u32[]{:S(2)}) collective-permute-start(bf16[4,2,32,1152]{3,2,0,1:T(8,128)(2,1)S(1)} %fusion.18), channel_id=1, source_target_pairs={{0,2},{1,3},{2,0},{3,1},{4,6},{5,7},{6,4},{7,5},{8,10},{9,11},{10,... | collective-permute-start | bytes 1769480 | tf_op jit(solution)/shard_map/ppermute | solution.py:21
  516.6 11.6 %collective-permute-start.51 = (bf16[4,2,16,1152]{3,2,0,1:T(8,128)(2,1)S(1)}, bf16[4,2,16,1152]{3,2,0,1:T(8,128)(2,1)S(1)}, u32[]{:S(2)}, u32[]{:S(2)}) collective-permute-start(bf16[4,2,16,1152]{3,2,0,1:T(8,128)(2,1)S(1)} %fusion.25), channel_id=1, source_target_pairs={{0,2},{1,3},{2,0},{3,1},{4,6},{5,7},{6,4},{7,5},{8,10},{9,11},{10,... | collective-permute-start | bytes 884744 | tf_op jit(solution)/shard_map/ppermute | solution.py:21
  525.2 13.2 %collective-permute-start.58 = (bf16[32,1152]{1,0:T(8,128)(2,1)S(1)}, bf16[32,1152]{1,0:T(8,128)(2,1)S(1)}, u32[]{:S(2)}, u32[]{:S(2)}) collective-permute-start(bf16[32,1152]{1,0:T(8,128)(2,1)S(1)} %get-tuple-element.197), channel_id=1, source_target_pairs={{0,16},{4,20},{8,24},{12,28},{16,0},{20,4},{24,8},{28,12},{1,17},{... | collective-permute-start | bytes 221192 | tf_op jit(solution)/shard_map/ppermute | solution.py:35
  525.3 14.2 %collective-permute-start.59 = (bf16[32,1152]{1,0:T(8,128)(2,1)S(1)}, bf16[32,1152]{1,0:T(8,128)(2,1)S(1)}, u32[]{:S(2)}, u32[]{:S(2)}) collective-permute-start(bf16[32,1152]{1,0:T(8,128)(2,1)S(1)} %get-tuple-element.199), channel_id=1, source_target_pairs={{0,24},{4,28},{8,0},{12,4},{16,8},{20,12},{24,16},{28,20},{1,25},{... | collective-permute-start | bytes 221192 | tf_op jit(solution)/shard_map/ppermute | solution.py:35
  527.1 15.7 %collective-permute-start.60 = (bf16[32,1152]{1,0:T(8,128)(2,1)S(1)}, bf16[32,1152]{1,0:T(8,128)(2,1)S(1)}, u32[]{:S(2)}, u32[]{:S(2)}) collective-permute-start(bf16[32,1152]{1,0:T(8,128)(2,1)S(1)} %get-tuple-element.198), channel_id=1, source_target_pairs={{0,8},{4,12},{8,16},{12,20},{16,24},{20,28},{24,0},{28,4},{1,9},{5... | collective-permute-start | bytes 221192 | tf_op jit(solution)/shard_map/ppermute | solution.py:35
  528.3 15.2 %collective-permute-start.52 = (bf16[4,16,1152]{2,1,0:T(8,128)(2,1)S(1)}, bf16[4,16,1152]{2,1,0:T(8,128)(2,1)S(1)}, u32[]{:S(2)}, u32[]{:S(2)}) collective-permute-start(bf16[4,16,1152]{2,1,0:T(8,128)(2,1)S(1)} %fusion.29), channel_id=1, source_target_pairs={{0,4},{4,0},{8,12},{12,8},{16,20},{20,16},{24,28},{28,24},{1,5},{5... | collective-permute-start | bytes 442376 | tf_op jit(solution)/shard_map/ppermute | solution.py:39
  530.5 15.6 %collective-permute-start.47 = (bf16[32,1152]{1,0:T(8,128)(2,1)S(1)}, bf16[32,1152]{1,0:T(8,128)(2,1)S(1)}, u32[]{:S(2)}, u32[]{:S(2)}) collective-permute-start(bf16[32,1152]{1,0:T(8,128)(2,1)S(1)} %get-tuple-element.200), channel_id=1, source_target_pairs={{0,16},{4,20},{8,24},{12,28},{16,0},{20,4},{24,8},{28,12},{1,17},{... | collective-permute-start | bytes 221192 | tf_op jit(solution)/shard_map/ppermute | solution.py:35
  (126 other events, 1138.2 us)
Sparse Core Ops, SparseCore 0:
  10.2 55.2 all-gather.3
  67.6 44.8 all-gather.5
  114.1 47.4 all-gather.7
  386.1 42.1 reduce-scatter.7
  445.4 41.6 reduce-scatter.5
  489.4 50.3 reduce-scatter.3

commit v3 on v2

--- a/solution.py
+++ b/solution.py
@@ -69,14 +69,14 @@
     return [flipped(block, 1) for block in own], own
 
 
-def group_reduce(sent, kept, beside=lambda ready: None, last=lambda ready: None):
+def group_reduce(sent, kept, beside=lambda ready: None, last=()):
     got = flipped(sent, 1)
     rows = kept[0].shape[0]
     half = rows // 2
     part = lambda start, end: got[start:end].astype(wide)
     if not by_steps():
         crossing = (kept[0] + part(0, rows)).astype(low)
-        return (kept[1], got[rows:], flipped(crossing, 2)), beside(sent), last(sent)
+        return (kept[1], got[rows:], flipped(crossing, 2)), beside(sent), [step(sent) for step in last]
     diagonal = (kept[0] + part(0, rows)).astype(low)
     diagonal, got, *kept = tied(diagonal, got, *kept[1:])
     aside = beside(kept[0])
@@ -86,9 +86,17 @@
     x_part = kept[0] + part(rows, 2 * rows) + jnp.concatenate([nothing, for_x.astype(wide)], axis=0)
     y_part = kept[1] + part(2 * rows, 3 * rows) + jnp.concatenate([for_y.astype(wide), nothing], axis=0)
     x_part, y_part, *kept = tied(x_part.astype(low), y_part.astype(low), *kept)
-    after = last(kept[-1])
-    x_part, y_part, after = tied(along_x(x_part), flipped(y_part, 2), after)
-    return (kept[-1], got[3 * rows :], x_part, y_part), aside, after
+    if not last:
+        return (kept[-1], got[3 * rows :], along_x(x_part), flipped(y_part, 2)), aside, ()
+    first, second = last
+    early = (along_x(x_part[:half]), flipped(y_part[:half], 2))
+    first = first(kept[-1])
+    early, first = tied(early, first)
+    late = (along_x(x_part[half:]), flipped(y_part[half:], 2))
+    second = second(early[0])
+    late, second = tied(late, second)
+    x_part, y_part = (jnp.concatenate(halves, axis=0) for halves in zip(early, late))
+    return (kept[-1], got[3 * rows :], x_part, y_part), aside, (first, second)
 
 
 def reduce_step(terms, names, name):
@@ -102,19 +110,8 @@
     return kept.astype(wide) + send(sent.astype(low)).astype(wide)
 
 
-def reduce_first(terms):
-    if not by_steps():
-        return terms
-    return reduce_step(terms.reshape(4, 2, 2, 2, *terms.shape[1:]), ["z", "x", "y", "core"], "core")
-
-
-def reduce_rest(terms, order):
-    if not by_steps():
-        return lax.psum_scatter(terms.astype(low), both, scatter_dimension=0, tiled=False).astype(wide)
+def reduce_z(terms):
     z = lax.axis_index("dp") // 2
-    names = ["z", "x", "y"]
-    for name in order:
-        terms = reduce_step(terms, names, name)
     total = lax.dynamic_index_in_dim(terms, z, 0, keepdims=False)
     for steps in (2, 1, 3):
         sent = lax.dynamic_index_in_dim(terms, (z - steps) % 4, 0, keepdims=False)
@@ -125,11 +122,9 @@
 def sum_everywhere(values):
     if not by_steps():
         return lax.psum(values, both)
-    values = values + flipped(values, 1)
-    values = values + flipped(values, 2)
+    values = (values + flipped(values, 1)) + (flipped(values, 2) + flipped(values, 3))
     values = values + along_x(values)
-    values = values + along_z(values, 2)
-    return values + along_z(values, 1)
+    return (values + along_z(values, 2)) + (along_z(values, 1) + along_z(values, 3))
 
 
 def rms_parts(values):
@@ -592,11 +587,16 @@
         left, _ = tied(near_gate, ready)
         return weight_grad((far_gate, left), (far, near))
 
-    grad_prenorm, grad_down_weight, grad_gate_weight = group_reduce(
-        sent, kept, down_weight_grad, gate_weight_grad
+    def up_weight_grad(ready):
+        left, _ = tied(near_up, ready)
+        return weight_grad((far_up, left), (far, near))
+
+    grad_prenorm, grad_down_weight, (grad_gate_weight, grad_up_weight) = group_reduce(
+        sent, kept, down_weight_grad, (gate_weight_grad, up_weight_grad)
     )
     shard_down = hidden_reduce(grad_down_weight)[:units]
     shard_gate = hidden_reduce(grad_gate_weight)[:units]
+    shard_up = hidden_reduce(grad_up_weight)[:units]
 
     grad_hidden, grad_attended, gains = by_rows(
         hidden_kernel,
@@ -608,28 +608,34 @@
     grad_feed_gain, grad_attention_gain = gains[0], gains[1]
     grad_out = product_of(mixed_flat, grad_attended, 0, 0).astype(low)
     grad_mixed = product_of(grad_attended, full_out, 1, 1).astype(low)
+    grad_mixed, grad_out = tied(grad_mixed, grad_out)
+    count = dp_count * seq_count
+    places = (4, 2, 2, 2) if by_steps() else (count,)
+    grad_out = grad_out.reshape(*places, -1, width)
+    if by_steps():
+        grad_out = reduce_step(grad_out, ["z", "x", "y", "core"], "core")
     grad_query_proj, query_gains, *key_grads = attend(back=True, extra=(logs, grad_mixed))
+    key_grads[hops], grad_out = tied(key_grads[hops], grad_out)
     grad_query_gain = jnp.sum(query_gains, axis=(0, 1))
-    count = dp_count * seq_count
-    grad_out = reduce_first(grad_out.reshape(count, -1, width))
-    grad_query = product_of(grad_query_proj, normed, 0, 0).astype(low)
-    grad_query = reduce_first(grad_query.reshape(count, nq, width))
-    left, _ = tied(near_up, key_grads[hops])
-    grad_up_weight = weight_grad((far_up, left), (far, near))
-    shard_up = hidden_reduce(grad_up_weight)[:units]
+    grad_query = product_of(grad_query_proj, normed, 0, 0).astype(low).reshape(*places, nq, width)
+    if by_steps():
+        grad_out = reduce_step(grad_out, ["z", "x", "y"], "x")
+        grad_query = reduce_step(grad_query, ["z", "x", "y", "core"], "core")
     returning = key_grads[hops]
     for hop in range(1, hops + 1):
         returning = returning + passed_along(key_grads[hops - hop], "seq", -hop).astype(wide)
-    returning, grad_out, grad_query, _ = tied(returning, grad_out, grad_query, grad_up_weight)
-    shard_out = reduce_rest(grad_out, ("x", "y"))
-    shard_query = reduce_rest(grad_query, ("y", "x"))
+    if by_steps():
+        grad_query = reduce_step(grad_query, ["z", "x", "y"], "x")
+    returning, grad_out, grad_query = tied(returning, grad_out, grad_query)
+    if by_steps():
+        grad_out = reduce_step(grad_out, ["z", "y"], "y")
     grad_key_proj, grad_key_gain = rms_back(
         key_unit, key_scale, key_gain, rotate_back(returning[..., :size], cosine, sine)
     )
     grad_key = grad_key_proj.astype(low).reshape(rows, size)
     grad_value = returning[..., size:].astype(low).reshape(rows, size)
     grad_kv = [
-        product_of(grad, normed, 0, 0).astype(low).reshape(count, -1, width)
+        product_of(grad, normed, 0, 0).astype(low).reshape(*places, -1, width)
         for grad in (grad_key, grad_value)
     ]
     grad_normed = product_of(grad_query_proj, full_query, 1, 0) + product_of(grad_key, full_key, 1, 0)
@@ -637,27 +643,38 @@
     grad_source, grad_input_gain = rms_back(source_unit, source_scale, input_gain, grad_normed)
     grad_inputs = grad_hidden + grad_source
 
-    shard_second = reduce_rest(reduce_first(jnp.concatenate(grad_kv, axis=1)), ("y", "x"))
-    gains = sum_everywhere(
-        jnp.concatenate(
-            [
-                grad_input_gain,
-                grad_attention_gain,
-                grad_feed_gain,
-                grad_output_gain[0],
-                grad_query_gain,
-                grad_key_gain,
-            ]
-        )
-    )
+    grad_kv = jnp.concatenate(grad_kv, axis=-2)
+    gains = jnp.concatenate(
+        [
+            grad_input_gain,
+            grad_attention_gain,
+            grad_feed_gain,
+            grad_output_gain[0],
+            grad_query_gain,
+            grad_key_gain,
+        ]
+    )
+    shard_gate = shard_gate.T
+    if by_steps():
+        grad_kv = reduce_step(grad_kv, ["z", "x", "y", "core"], "core")
+        grad_kv, gains = tied(grad_kv, gains)
+        grad_kv = reduce_step(grad_kv, ["z", "x", "y"], "x")
+        joined = reduce_step(jnp.concatenate([grad_query, grad_kv], axis=-2), ["z", "y"], "y")
+        joined, shard_down, shard_gate = tied(joined, shard_down, shard_gate)
+        shard = reduce_z(jnp.concatenate([joined, grad_out], axis=-2))
+    else:
+        shard = jnp.concatenate([grad_query, grad_kv, grad_out], axis=-2)
+        shard = lax.psum_scatter(shard, both, scatter_dimension=0, tiled=False).astype(wide)
+    gains = sum_everywhere(gains)
+    ends = (nq, nq + nk, nq + nk + nv)
     return (
         output.reshape(micro, length, width),
         grad_inputs.reshape(micro, length, width),
-        shard_query.T,
-        shard_second[:nk].T,
-        shard_second[nk:].T,
-        shard_out,
-        shard_gate.T,
+        shard[: ends[0]].T,
+        shard[ends[0] : ends[1]].T,
+        shard[ends[1] : ends[2]].T,
+        shard[ends[2] :],
+        shard_gate,
         shard_up.T,
         shard_down,
         gains[:width],

time: 575 us -> 567 us (0.986)
  waiting for transfers between devices: 233 us -> 215 us
  matrix products: 61.6 us -> 67.5 us
    ppermute x14 -> x9, waiting for transfers between devices: 34.6 us -> 23.5 us  [along_z(): lax.ppermute(value, 'dp', [(index, (index + 2 * steps) % 8) for index in...]
    ppermute x32 -> x33, starting transfers between devices: 23.5 us -> 29.7 us  [flipped(): lax.ppermute(value, 'seq', [(index, index ^ bits) for index in range(coun...]
    dot_general x18, matrix products: 61.6 us -> 67.5 us  [product_of(): lax.dot_general(left, right, (((left_axis,), (right_axis,)), ((), ())), p...]
    unnamed x220 -> x206, local copies, waits for them, and re-layouts: 13.2 us -> 7.49 us
    ppermute x14 -> x15, waiting for transfers between devices: 84.1 us -> 81.4 us  [along_x(): return lax.ppermute(value, 'dp', [(index, index ^ 1) for index in range(8)])]
    ppermute x14 -> x9, starting transfers between devices: 18.1 us -> 16.4 us  [along_z(): lax.ppermute(value, 'dp', [(index, (index + 2 * steps) % 8) for index in...]
    ppermute x32 -> x33, waiting for transfers between devices: 79.1 us -> 77.8 us  [flipped(): lax.ppermute(value, 'seq', [(index, index ^ bits) for index in range(coun...]
    ppermute x14 -> x15, starting transfers between devices: 14.1 us -> 14.5 us  [along_x(): return lax.ppermute(value, 'dp', [(index, index ^ 1) for index in range(8)])]
  transfers between devices with their start and end apart: 72 -> 69, of which waited for: 32 -> 30; matrix products, arithmetic and copies ran while one was open for 17% -> 20% of each run, Pallas kernels for 13% -> 12%
where the time goes in v3:
time: 567 us; the launch traced here: 558 us
  waiting for transfers between devices  215 us (38%)
  Pallas kernels  121 us (21%)
  starting transfers between devices  74.3 us (13%)
  matrix products  67.5 us (12%)
  local copies, waits for them, and re-layouts  32.6 us (6%)
  other arithmetic  31.1 us (5%)
  between operations  16.5 us (3%)
    pallas_call x4, Pallas kernels, feed(): pl.pallas_call(functools.partial(feed_back_kernel if back else feed_kerne...  102 us
    ppermute x15, waiting for transfers between devices, along_x(): return lax.ppermute(value, 'dp', [(index, index ^ 1) for index in range(8)])  81.4 us
    ppermute x33, waiting for transfers between devices, flipped(): lax.ppermute(value, 'seq', [(index, index ^ bits) for index in range(coun...  77.8 us
    dot_general x18, matrix products, product_of(): lax.dot_general(left, right, (((left_axis,), (right_axis,)), ((), ())), p...  67.5 us
    ppermute x33, starting transfers between devices, flipped(): lax.ppermute(value, 'seq', [(index, index ^ bits) for index in range(coun...  29.7 us
    ppermute x9, waiting for transfers between devices, along_z(): lax.ppermute(value, 'dp', [(index, (index + 2 * steps) % 8) for index in...  23.5 us
    ppermute x6, waiting for transfers between devices, passed_along(): lax.ppermute(value, axis, [(source, source + steps) for source in range(l...  16.5 us
    ppermute x9, starting transfers between devices, along_z(): lax.ppermute(value, 'dp', [(index, (index + 2 * steps) % 8) for index in...  16.4 us
  transfers between devices with their start and end apart: 69, of which 30 were waited for; matrix products, arithmetic and copies ran while one was open for 20% of the time, Pallas kernels for 12%

profile of v3, /device:TPU:0, one launch (start us, length us, event | category | flops | bytes accessed | tf_op | source)
XLA Modules:
  0.0 558.3 jit_solution(18412340469738086582)
XLA Ops:
  10.3 3.1 collective-permute-start
  13.4 2.6 collective-permute-start.1
  17.3 3.4 collective-permute-start.11
  22.9 12.7 %collective-permute-done.1 = bf16[80,1152]{1,0:T(8,128)(2,1)S(1)} collective-permute-done((bf16[80,1152]{1,0:T(8,128)(2,1)S(1)}, bf16[80,1152]{1,0:T(8,128)(2,1)S(1)}, u32[]{:S(2)}, u32[]{:S(2)}) %collective-permute-start.1) | collective-permute-done | bytes 184352 | tf_op jit(solution)/shard_map/ppermute | solution.py:35
  39.0 14.9 %collective-permute-done.4 = bf16[320,1152]{1,0:T(8,128)(2,1)S(1)} collective-permute-done((bf16[320,1152]{1,0:T(8,128)(2,1)S(1)}, bf16[320,1152]{1,0:T(8,128)(2,1)S(1)}, u32[]{:S(2)}, u32[]{:S(2)}) %collective-permute-start.4) | collective-permute-done | bytes 737312 | tf_op jit(solution)/shard_map/ppermute | solution.py:21
  54.4 2.7 collective-permute-start.9
  58.7 4.9 collective-permute-done.8
  66.8 2.1 shard_map.271
  71.7 3.5 collective-permute-start.13
  76.9 3.9 fusion.58.proj
  80.8 6.7 %collective-permute-done.13.refs_0_ = bf16[2,256,512]{2,1,0:T(8,128)(2,1)S(1)} collective-permute-done((bf16[2,256,512]{2,1,0:T(8,128)(2,1)S(1)}, bf16[2,256,512]{2,1,0:T(8,128)(2,1)S(1)}, u32[]{:S(2)}, u32[]{:S(2)}) %collective-permute-start.13) | collective-permute-done | bytes 524320 | tf_op jit(solution)/shard_map/ppermute | solution.py:27
  87.6 4.8 shard_map.272
  96.3 6.6 %collective-permute-start.15 = (bf16[512,1152]{1,0:T(8,128)(2,1)S(1)}, bf16[512,1152]{1,0:T(8,128)(2,1)}, u32[]{:S(2)}, u32[]{:S(2)}) collective-permute-start(bf16[512,1152]{1,0:T(8,128)(2,1)S(1)} %multiply_convert_fusion.refs_3_), channel_id=1, source_target_pairs={{0,2},{1,3},{2,0},{3,1},{4,6},{5,7},{6,4},{7,5},{8,10},{9,11},{10,... | collective-permute-start | bytes 3538952 | tf_op jit(solution)/shard_map/ppermute | solution.py:21
  104.2 24.3 %collective-permute-done.15.refs_2_ = bf16[512,1152]{1,0:T(8,128)(2,1)} collective-permute-done((bf16[512,1152]{1,0:T(8,128)(2,1)S(1)}, bf16[512,1152]{1,0:T(8,128)(2,1)}, u32[]{:S(2)}, u32[]{:S(2)}) %collective-permute-start.15) | collective-permute-done | bytes 1179680 | tf_op jit(solution)/shard_map/ppermute | solution.py:21
  132.0 11.6 %collective-permute-done.16 = bf16[256,1152]{1,0:T(8,128)(2,1)S(1)} collective-permute-done((bf16[256,1152]{1,0:T(8,128)(2,1)S(1)}, bf16[256,1152]{1,0:T(8,128)(2,1)S(1)}, u32[]{:S(2)}, u32[]{:S(2)}) %collective-permute-start.16) | collective-permute-done | bytes 589856 | tf_op jit(solution)/shard_map/ppermute | solution.py:39
  145.8 15.8 %all-gather.8.cloned.1.call-done.refs_6_.refs_8_ = bf16[896,1152]{1,0:T(8,128)(2,1)} async-done(((bf16[224,1152]{1,0:T(8,128)(2,1)}), bf16[896,1152]{1,0:T(8,128)(2,1)}) %all-gather.8.cloned.1.call-update) | async-done | bytes 2064400 | tf_op jit(solution)/shard_map/all_gather | solution.py:47
  161.6 25.0 %shard_map.274 = (bf16[2048,1152]{1,0:T(8,128)(2,1)}, bf16[2048,896]{1,0:T(8,128)(2,1)}, bf16[2048,896]{1,0:T(8,128)(2,1)}, bf16[2048,896]{1,0:T(8,128)(2,1)}, bf16[2048,1152]{1,0:T(8,128)(2,1)}) custom-call(bf16[512,1152]{1,0:T(8,128)(2,1)} %collective-permute-done.19.refs_0_, bf16[512,1152]{1,0:T(8,128)(2,1)} %collective-permute-done.20.refs_1_, ...), custom_call_target="tpu_custom_call" | custom-call | flops 12683575296 | bytes 43417600 | tf_op jit(solution)/shard_map/pallas_call | solution.py:305
  186.6 26.0 %shard_map.273 = (bf16[2048,1152]{1,0:T(8,128)(2,1)}, bf16[2048,896]{1,0:T(8,128)(2,1)}, bf16[2048,896]{1,0:T(8,128)(2,1)}, bf16[2048,896]{1,0:T(8,128)(2,1)}, b...) custom-call(bf16[512,1152]{1,0:T(8,128)(2,1)} %constant_dynamic-update-sl, ...), custom_call_target="tpu_custom_call" | custom-call | flops 12683575296 | bytes 43417600 | tf_op jit(solution)/shard_map/pallas_call | solution.py:305
  217.5 12.8 %collective-permute-done.24 = bf16[256,1152]{1,0:T(8,128)(2,1)S(1)} collective-permute-done((bf16[256,1152]{1,0:T(8,128)(2,1)S(1)}, bf16[256,1152]{1,0:T(8,128)(2,1)S(1)}, u32[]{:S(2)}, u32[]{:S(2)}) %collective-permute-start.24) | collective-permute-done | bytes 589856 | tf_op jit(solution)/shard_map/ppermute | solution.py:39
  234.5 25.1 %collective-permute-done.26.refs_2_ = bf16[512,1152]{1,0:T(8,128)(2,1)S(1)} collective-permute-done((bf16[512,1152]{1,0:T(8,128)(2,1)S(1)}, bf16[512,1152]{1,0:T(8,128)(2,1)S(1)}, u32[]{:S(2)}, u32[]{:S(2)}) %collective-permute-start.26) | collective-permute-done | bytes 1179680 | tf_op jit(solution)/shard_map/ppermute | solution.py:39
  259.9 2.6 shard_map.275
  265.4 23.2 %collective-permute-done.28.refs_2_ = bf16[512,1152]{1,0:T(8,128)(2,1)S(1)} collective-permute-done((bf16[512,1152]{1,0:T(8,128)(2,1)S(1)}, bf16[512,1152]{1,0:T(8,128)(2,1)S(1)}, u32[]{:S(2)}, u32[]{:S(2)}) %collective-permute-start.28) | collective-permute-done | bytes 1179680 | tf_op jit(solution)/shard_map/ppermute | solution.py:21
  292.2 10.2 %collective-permute-done.29 = bf16[256,1152]{1,0:T(8,128)(2,1)S(1)} collective-permute-done((bf16[256,1152]{1,0:T(8,128)(2,1)S(1)}, bf16[256,1152]{1,0:T(8,128)(2,1)S(1)}, u32[]{:S(2)}, u32[]{:S(2)}) %collective-permute-start.29) | collective-permute-done | bytes 589856 | tf_op jit(solution)/shard_map/ppermute | solution.py:39
  302.8 2.8 collective-permute-done.32.refs_0_
  306.6 24.6 %shard_map.277 = (bf16[2048,1152]{1,0:T(8,128)(2,1)}, bf16[2048,896]{1,0:T(8,128)(2,1)}, bf16[2048,896]{1,0:T(8,128)(2,1)}, bf16[2048,1152]{1,0:T(8,128)(2,1)}) custom-call(bf16[512,1152]{1,0:T(8,128)(2,1)} %copy-done.86, bf16[512,1152]{1,0:T(8,128)(2,1)} %copy-done.84, bf16[512,1152]{1,0:T(8,128)(2,1)} %copy-done.85, bf16[512,1152]{1,0:T(8,128)(2,1)} %copy-done.83, ...), custom_call_target="tpu_custom_call" | custom-call | flops 12683575296 | bytes 43417600 | tf_op jit(solution)/shard_map/pallas_call | solution.py:305
  331.4 26.2 %shard_map.276 = (bf16[2048,1152]{1,0:T(8,128)(2,1)}, bf16[2048,896]{1,0:T(8,128)(2,1)}, bf16[2048,896]{1,0:T(8,128)(2,1)}, bf16[512,1152]{1,0:T(8,128)(2,1)}, b...) custom-call(bf16[512,1152]{1,0:T(8,128)(2,1)} %copy-done.63, ...), custom_call_target="tpu_custom_call" | custom-call | flops 12683575296 | bytes 43417600 | tf_op jit(solution)/shard_map/pallas_call | solution.py:305
  362.9 5.2 fusion.59
  368.2 6.5 %fusion = bf16[896,1152]{1,0:T(8,128)(2,1)} fusion(f32[896,1152]{1,0:T(8,128)S(1)} %fusion.59, bf16[2048,896]{1,0:T(8,128)(2,1)S(1)} %copy-done.87, bf16[2048,1152]{1,0:T(8,128)(2,1)S(1)} %bitcast.222), kind=kOutput, calls=%fused_computation.5 | convolution fusion | flops 4229922816 | bytes 14581760 | tf_op jit(solution)/shard_map/dot_general | solution.py:164
  374.7 2.5 slice.154.refs_1_
  377.8 4.2 add_convert_fusion
  382.5 2.5 fusion.50
  390.2 8.7 %fusion.60 = f32[896,1152]{1,0:T(8,128)S(1)} fusion(bf16[2048,896]{1,0:T(8,128)(2,1)} %get-tuple-element.159, bf16[2048,1152]{1,0:T(8,128)(2,1)} %get-tuple-element.160), kind=kOutput, calls=%fused_computation.182 | convolution fusion | flops 4227858432 | bytes 12517376 | tf_op jit(solution)/shard_map/dot_general | solution.py:164
  398.9 6.5 %fusion.1 = bf16[896,1152]{1,0:T(8,128)(2,1)} fusion(f32[896,1152]{1,0:T(8,128)S(1)} %fusion.60, bf16[2048,896]{1,0:T(8,128)(2,1)S(1)} %copy-done.88, bf16[2048,1152]{1,0:T(8,128)(2,1)S(1)} %bitcast.220), kind=kOutput, calls=%fused_computation.6 | convolution fusion | flops 4229922816 | bytes 14581760 | tf_op jit(solution)/shard_map/dot_general | solution.py:164
  405.4 10.6 %fusion.61 = f32[896,1152]{1,0:T(8,128)} fusion(bf16[2048,896]{1,0:T(8,128)(2,1)} %get-tuple-element.164, bf16[2048,1152]{1,0:T(8,128)(2,1)} %get-tuple-element.160), kind=kOutput, calls=%fused_computation.183 | convolution fusion | flops 4227858432 | bytes 12517376 | tf_op jit(solution)/shard_map/dot_general | solution.py:164
  416.1 11.0 %fusion.2 = bf16[896,1152]{1,0:T(8,128)(2,1)} fusion(f32[896,1152]{1,0:T(8,128)} %fusion.61, bf16[2048,896]{1,0:T(8,128)(2,1)} %get-tuple-element.162, bf16[2048,1152]{1,0:T(8,128)(2,1)} %get-tuple-element.157), kind=kOutput, calls=%fused_computation.7 | convolution fusion | flops 4229922816 | bytes 14581760 | tf_op jit(solution)/shard_map/dot_general | solution.py:164
  431.8 3.0 shard_map.278
  434.9 3.0 convolution_convert_fusion.1
  440.5 7.0 %shard_map.279 = (bf16[512,1024]{1,0:T(8,128)(2,1)S(1)}, f32[2,1,256]{2,1,0:T(1,128)S(1)}, bf16[2,256,512]{2,1,0:T(8,128)(2,1)S(1)}, bf16[2,256,512]{2,1,0:T(8,128)(2,1)S(1)}, f32[2,256,512]{2,1,0:T(8,128)S(1)}) custom-call(s32[1]{0:T(128)} %bitcast.1.base, f32[512,1024]{1,0:T(8,128)S(1)} %copy-done.38, f32[256,256]{1,0:T(8,128)S(1)} %copy-done.11, ...), custom_call_target="tpu_custom_call" | custom-call | flops 4026531840 | bytes 10485760 | tf_op jit(solution)/shard_map/pallas_call | solution.py:471
  451.5 2.9 constant_dynamic-slice_fusion.3
  459.1 3.6 fusion.62
  468.4 9.7 %collective-permute-done.45 = bf16[2,256,512]{2,1,0:T(8,128)(2,1)} collective-permute-done((bf16[2,256,512]{2,1,0:T(8,128)(2,1)S(1)}, bf16[2,256,512]{2,1,0:T(8,128)(2,1)}, u32[]{:S(2)}, u32[]{:S(2)}) %collective-permute-start.45) | collective-permute-done | bytes 524320 | tf_op jit(solution)/shard_map/ppermute | solution.py:27
  480.8 12.5 %collective-permute-done.46 = bf16[4,2,32,1152]{3,2,0,1:T(8,128)(2,1)S(1)} collective-permute-done((bf16[4,2,32,1152]{3,2,0,1:T(8,128)(2,1)S(1)}, bf16[4,2,32,1152]{3,2,0,1:T(8,128)(2,1)S(1)}, u32[]{:S(2)}, u32[]{:S(2)}) %collective-permute-start.46) | collective-permute-done | bytes 589856 | tf_op jit(solution)/shard_map/ppermute | solution.py:39
  496.2 3.3 collective-permute-start.52
  514.0 2.6 collective-permute-start.62
  521.4 8.1 %collective-permute-done.51 = bf16[4,48,1152]{2,1,0:T(8,128)(2,1)S(1)} collective-permute-done((bf16[4,48,1152]{2,1,0:T(8,128)(2,1)S(1)}, bf16[4,48,1152]{2,1,0:T(8,128)(2,1)S(1)}, u32[]{:S(2)}, u32[]{:S(2)}) %collective-permute-start.51) | collective-permute-done | bytes 442400 | tf_op jit(solution)/shard_map/ppermute | solution.py:21
  535.0 3.4 collective-permute-start.54
  540.4 6.9 %collective-permute-done.53 = bf16[80,1152]{1,0:T(8,128)(2,1)S(1)} collective-permute-done((bf16[80,1152]{1,0:T(8,128)(2,1)S(1)}, bf16[80,1152]{1,0:T(8,128)(2,1)S(1)}, u32[]{:S(2)}, u32[]{:S(2)}) %collective-permute-start.53) | collective-permute-done | bytes 184352 | tf_op jit(solution)/shard_map/ppermute | solution.py:35
  547.3 2.2 collective-permute-done.55
  (428 shorter events, 113.8 us)
Async XLA Ops:
  7.2 138.6 %all-gather.4.cloned.1.call-start = ((), (), s32[]{:S(2)}) async-start(), calls=%async_computation.3 | async-start | bytes 2580480 | tf_op jit(solution)/shard_map/all_gather | solution.py:47
  9.3 136.5 %all-gather.6.cloned.1.call-start = ((), (), s32[]{:S(2)}) async-start(), calls=%async_computation.4 | async-start | bytes 2580480 | tf_op jit(solution)/shard_map/all_gather | solution.py:47
  10.3 12.6 %collective-permute-start = (bf16[80,1152]{1,0:T(8,128)(2,1)S(1)}, bf16[80,1152]{1,0:T(8,128)(2,1)S(1)}, u32[]{:S(2)}, u32[]{:S(2)}) collective-permute-start(bf16[80,1152]{1,0:T(8,128)(2,1)S(1)} %pad_maximum_fusion.4), channel_id=1, source_target_pairs={{0,8},{4,12},{8,16},{12,20},{16,24},{20,28},{24,0},{28,4},{1,9},{5... | collective-permute-start | bytes 552968 | tf_op jit(solution)/shard_map/ppermute | solution.py:35
  13.4 22.2 %collective-permute-start.1 = (bf16[80,1152]{1,0:T(8,128)(2,1)S(1)}, bf16[80,1152]{1,0:T(8,128)(2,1)S(1)}, u32[]{:S(2)}, u32[]{:S(2)}) collective-permute-start(bf16[80,1152]{1,0:T(8,128)(2,1)S(1)} %pad_maximum_fusion.4), channel_id=1, source_target_pairs={{0,16},{4,20},{8,24},{12,28},{16,0},{20,4},{24,8},{28,12},{1,17},{... | collective-permute-start | bytes 552968 | tf_op jit(solution)/shard_map/ppermute | solution.py:35
  16.0 19.6 %collective-permute-start.2 = (bf16[80,1152]{1,0:T(8,128)(2,1)S(1)}, bf16[80,1152]{1,0:T(8,128)(2,1)S(1)}, u32[]{:S(2)}, u32[]{:S(2)}) collective-permute-start(bf16[80,1152]{1,0:T(8,128)(2,1)S(1)} %pad_maximum_fusion.4), channel_id=1, source_target_pairs={{0,24},{4,28},{8,0},{12,4},{16,8},{20,12},{24,16},{28,20},{1,25},{... | collective-permute-start | bytes 552968 | tf_op jit(solution)/shard_map/ppermute | solution.py:35
  17.3 59.2 %collective-permute-start.11 = (s32[2,256]{1,0:T(2,128)}, s32[2,256]{1,0:T(2,128)S(1)}, u32[]{:S(2)}, u32[]{:S(2)}) collective-permute-start(s32[2,256]{1,0:T(2,128)} %param.17), channel_id=1, source_target_pairs={{0,2},{1,3},{4,6},{5,7},{8,10},{9,11},{12,14},{13,15},{16,18},{17,... | collective-permute-start | bytes 6152 | tf_op jit(solution)/shard_map/ppermute | solution.py:27
  22.7 138.9 %all-gather.8.cloned.1.call-start = ((), (), s32[]{:S(2)}) async-start(), calls=%async_computation.5 | async-start | bytes 2580480 | tf_op jit(solution)/shard_map/all_gather | solution.py:47
  35.7 18.3 %collective-permute-start.4 = (bf16[320,1152]{1,0:T(8,128)(2,1)S(1)}, bf16[320,1152]{1,0:T(8,128)(2,1)S(1)}, u32[]{:S(2)}, u32[]{:S(2)}) collective-permute-start(bf16[320,1152]{1,0:T(8,128)(2,1)S(1)} %constant_dynamic-update-slice_fusion), channel_id=1, source_target_pairs={{0,2},{1,3},{2,0},{3,1},{4,6},{5,7},{6,4},{7,5},{8,10},{9,11},{10,... | collective-permute-start | bytes 2211848 | tf_op jit(solution)/shard_map/ppermute | solution.py:21
  37.3 17.0 %collective-permute-start.6 = (bf16[320,1152]{1,0:T(8,128)(2,1)S(1)}, bf16[320,1152]{1,0:T(8,128)(2,1)S(1)}, u32[]{:S(2)}, u32[]{:S(2)}) collective-permute-start(bf16[320,1152]{1,0:T(8,128)(2,1)S(1)} %constant_dynamic-update-slice_fusion), channel_id=1, source_target_pairs={{0,4},{4,0},{8,12},{12,8},{16,20},{20,16},{24,28},{28,24},{1,5},{5... | collective-permute-start | bytes 2211848 | tf_op jit(solution)/shard_map/ppermute | solution.py:39
  64.6 12.0 %collective-permute-start.12 = (s32[2,256]{1,0:T(2,128)S(1)}, s32[2,256]{1,0:T(2,128)S(1)}, u32[]{:S(2)}, u32[]{:S(2)}) collective-permute-start(s32[2,256]{1,0:T(2,128)S(1)} %copy-done.80), channel_id=1, source_target_pairs={{0,1},{1,2},{2,3},{4,5},{5,6},{6,7},{8,9},{9,10},{10,11},{12,13},{... | collective-permute-start | bytes 6152 | tf_op jit(solution)/shard_map/ppermute | solution.py:27
  71.7 15.8 %collective-permute-start.13 = (bf16[2,256,512]{2,1,0:T(8,128)(2,1)S(1)}, bf16[2,256,512]{2,1,0:T(8,128)(2,1)S(1)}, u32[]{:S(2)}, u32[]{:S(2)}) collective-permute-start(bf16[2,256,512]{2,1,0:T(8,128)(2,1)S(1)} %pad_maximum_fusion.2.refs_2_), channel_id=1, source_target_pairs={{0,2},{1,3},{4,6},{5,7},{8,10},{9,11},{12,14},{13,15},{16,18},{17,... | collective-permute-start | bytes 1572872 | tf_op jit(solution)/shard_map/ppermute | solution.py:27
  75.2 12.3 %collective-permute-start.14 = (bf16[2,256,512]{2,1,0:T(8,128)(2,1)S(1)}, bf16[2,256,512]{2,1,0:T(8,128)(2,1)S(1)}, u32[]{:S(2)}, u32[]{:S(2)}) collective-permute-start(bf16[2,256,512]{2,1,0:T(8,128)(2,1)S(1)} %pad_maximum_fusion.2.refs_2_), channel_id=1, source_target_pairs={{0,1},{1,2},{2,3},{4,5},{5,6},{6,7},{8,9},{9,10},{10,11},{12,13},{... | collective-permute-start | bytes 1572872 | tf_op jit(solution)/shard_map/ppermute | solution.py:27
  96.3 32.2 %collective-permute-start.15 = (bf16[512,1152]{1,0:T(8,128)(2,1)S(1)}, bf16[512,1152]{1,0:T(8,128)(2,1)}, u32[]{:S(2)}, u32[]{:S(2)}) collective-permute-start(bf16[512,1152]{1,0:T(8,128)(2,1)S(1)} %multiply_convert_fusion.refs_3_), channel_id=1, source_target_pairs={{0,2},{1,3},{2,0},{3,1},{4,6},{5,7},{6,4},{7,5},{8,10},{9,11},{10,... | collective-permute-start | bytes 3538952 | tf_op jit(solution)/shard_map/ppermute | solution.py:21
  102.9 27.1 %collective-permute-start.17 = (bf16[512,1152]{1,0:T(8,128)(2,1)S(1)}, bf16[512,1152]{1,0:T(8,128)(2,1)}, u32[]{:S(2)}, u32[]{:S(2)}) collective-permute-start(bf16[512,1152]{1,0:T(8,128)(2,1)S(1)} %multiply_convert_fusion.refs_3_), channel_id=1, source_target_pairs={{0,4},{4,0},{8,12},{12,8},{16,20},{20,16},{24,28},{28,24},{1,5},{5... | collective-permute-start | bytes 3538952 | tf_op jit(solution)/shard_map/ppermute | solution.py:39
  104.1 425.5 %reduce-scatter.4.cloned.1.call-start = ((), (), s32[]{:S(2)}) async-start(), calls=%async_computation.6 | async-start | bytes 2580480 | tf_op jit(solution)/shard_map/reduce_scatter | solution.py:51
  129.6 14.0 %collective-permute-start.16 = (bf16[256,1152]{1,0:T(8,128)(2,1)S(1)}, bf16[256,1152]{1,0:T(8,128)(2,1)S(1)}, u32[]{:S(2)}, u32[]{:S(2)}) collective-permute-start(bf16[256,1152]{1,0:T(8,128)(2,1)S(1)} %slice.183), channel_id=1, source_target_pairs={{0,4},{4,0},{8,12},{12,8},{16,20},{20,16},{24,28},{28,24},{1,5},{5... | collective-permute-start | bytes 1769480 | tf_op jit(solution)/shard_map/ppermute | solution.py:39
  131.1 13.8 %collective-permute-start.18 = (bf16[256,1152]{1,0:T(8,128)(2,1)S(1)}, bf16[256,1152]{1,0:T(8,128)(2,1)S(1)}, u32[]{:S(2)}, u32[]{:S(2)}) collective-permute-start(bf16[256,1152]{1,0:T(8,128)(2,1)S(1)} %slice.184), channel_id=1, source_target_pairs={{0,2},{1,3},{2,0},{3,1},{4,6},{5,7},{6,4},{7,5},{8,10},{9,11},{10,... | collective-permute-start | bytes 1769480 | tf_op jit(solution)/shard_map/ppermute | solution.py:21
  131.5 30.1 %collective-permute-start.22 = (bf16[512,1152]{1,0:T(8,128)(2,1)S(1)}, bf16[512,1152]{1,0:T(8,128)(2,1)}, u32[]{:S(2)}, u32[]{:S(2)}) collective-permute-start(bf16[512,1152]{1,0:T(8,128)(2,1)S(1)} %multiply_convert_fusion.refs_3_), channel_id=1, source_target_pairs={{0,1},{1,0},{2,3},{3,2},{4,5},{5,4},{6,7},{7,6},{8,9},{9,8},{10,11... | collective-permute-start | bytes 3538952 | tf_op jit(solution)/shard_map/ppermute | solution.py:21
  131.5 30.1 %collective-permute-start.20 = (bf16[512,1152]{1,0:T(8,128)(2,1)}, bf16[512,1152]{1,0:T(8,128)(2,1)}, u32[]{:S(2)}, u32[]{:S(2)}) collective-permute-start(bf16[512,1152]{1,0:T(8,128)(2,1)} %collective-permute-done.17.refs_1_), channel_id=1, source_target_pairs={{0,1},{1,0},{2,3},{3,2},{4,5},{5,4},{6,7},{7,6},{8,9},{9,8},{10,11... | collective-permute-start | bytes 3538952 | tf_op jit(solution)/shard_map/ppermute | solution.py:21
  132.0 29.6 %collective-permute-start.21 = (bf16[512,1152]{1,0:T(8,128)(2,1)}, bf16[512,1152]{1,0:T(8,128)(2,1)}, u32[]{:S(2)}, u32[]{:S(2)}) collective-permute-start(bf16[512,1152]{1,0:T(8,128)(2,1)} %collective-permute-done.15.refs_2_), channel_id=1, source_target_pairs={{0,1},{1,0},{2,3},{3,2},{4,5},{5,4},{6,7},{7,6},{8,9},{9,8},{10,11... | collective-permute-start | bytes 3538952 | tf_op jit(solution)/shard_map/ppermute | solution.py:21
  145.8 15.8 %collective-permute-start.19 = (bf16[512,1152]{1,0:T(8,128)(2,1)}, bf16[512,1152]{1,0:T(8,128)(2,1)}, u32[]{:S(2)}, u32[]{:S(2)}) collective-permute-start(bf16[512,1152]{1,0:T(8,128)(2,1)} %constant_dynamic-update-slice_fusion.9.refs_0_), channel_id=1, source_target_pairs={{0,1},{1,0},{2,3},{3,2},{4,5},{5,4},{6,7},{7,6},{8,9},{9,8},{10,11... | collective-permute-start | bytes 3538952 | tf_op jit(solution)/shard_map/ppermute | solution.py:21
  186.6 26.1 %collective-permute-start.23 = (bf16[2048,1152]{1,0:T(8,128)(2,1)}, bf16[2048,1152]{1,0:T(8,128)(2,1)S(1)}, u32[]{:S(2)}, u32[]{:S(2)}) collective-permute-start(bf16[2048,1152]{1,0:T(8,128)(2,1)} %get-tuple-element.110), channel_id=1, source_target_pairs={{0,1},{1,0},{2,3},{3,2},{4,5},{5,4},{6,7},{7,6},{8,9},{9,8},{10,11... | collective-permute-start | bytes 14155784 | tf_op jit(solution)/shard_map/ppermute | solution.py:21
  214.5 15.8 %collective-permute-start.24 = (bf16[256,1152]{1,0:T(8,128)(2,1)S(1)}, bf16[256,1152]{1,0:T(8,128)(2,1)S(1)}, u32[]{:S(2)}, u32[]{:S(2)}) collective-permute-start(bf16[256,1152]{1,0:T(8,128)(2,1)S(1)} %get-tuple-element.223), channel_id=1, source_target_pairs={{0,4},{4,0},{8,12},{12,8},{16,20},{20,16},{24,28},{28,24},{1,5},{5... | collective-permute-start | bytes 1769480 | tf_op jit(solution)/shard_map/ppermute | solution.py:39
  216.0 15.4 %collective-permute-start.25 = (bf16[256,1152]{1,0:T(8,128)(2,1)S(1)}, bf16[256,1152]{1,0:T(8,128)(2,1)S(1)}, u32[]{:S(2)}, u32[]{:S(2)}) collective-permute-start(bf16[256,1152]{1,0:T(8,128)(2,1)S(1)} %get-tuple-element.222), channel_id=1, source_target_pairs={{0,2},{1,3},{2,0},{3,1},{4,6},{5,7},{6,4},{7,5},{8,10},{9,11},{10,... | collective-permute-start | bytes 1769480 | tf_op jit(solution)/shard_map/ppermute | solution.py:21
  232.3 27.3 %collective-permute-start.26 = (bf16[512,1152]{1,0:T(8,128)(2,1)S(1)}, bf16[512,1152]{1,0:T(8,128)(2,1)S(1)}, u32[]{:S(2)}, u32[]{:S(2)}) collective-permute-start(bf16[512,1152]{1,0:T(8,128)(2,1)S(1)} %get-tuple-element.125), channel_id=1, source_target_pairs={{0,4},{4,0},{8,12},{12,8},{16,20},{20,16},{24,28},{28,24},{1,5},{5... | collective-permute-start | bytes 3538952 | tf_op jit(solution)/shard_map/ppermute | solution.py:39
  232.9 27.0 %collective-permute-start.27 = (bf16[512,1152]{1,0:T(8,128)(2,1)S(1)}, bf16[512,1152]{1,0:T(8,128)(2,1)S(1)}, u32[]{:S(2)}, u32[]{:S(2)}) collective-permute-start(bf16[512,1152]{1,0:T(8,128)(2,1)S(1)} %get-tuple-element.126), channel_id=1, source_target_pairs={{0,2},{1,3},{2,0},{3,1},{4,6},{5,7},{6,4},{7,5},{8,10},{9,11},{10,... | collective-permute-start | bytes 3538952 | tf_op jit(solution)/shard_map/ppermute | solution.py:21
  262.5 26.1 %collective-permute-start.28 = (bf16[512,1152]{1,0:T(8,128)(2,1)S(1)}, bf16[512,1152]{1,0:T(8,128)(2,1)S(1)}, u32[]{:S(2)}, u32[]{:S(2)}) collective-permute-start(bf16[512,1152]{1,0:T(8,128)(2,1)S(1)} %get-tuple-element.128.refs_3_), channel_id=1, source_target_pairs={{0,2},{1,3},{2,0},{3,1},{4,6},{5,7},{6,4},{7,5},{8,10},{9,11},{10,... | collective-permute-start | bytes 3538952 | tf_op jit(solution)/shard_map/ppermute | solution.py:21
  264.0 26.9 %collective-permute-start.30 = (bf16[512,1152]{1,0:T(8,128)(2,1)S(1)}, bf16[512,1152]{1,0:T(8,128)(2,1)S(1)}, u32[]{:S(2)}, u32[]{:S(2)}) collective-permute-start(bf16[512,1152]{1,0:T(8,128)(2,1)S(1)} %get-tuple-element.128.refs_3_), channel_id=1, source_target_pairs={{0,4},{4,0},{8,12},{12,8},{16,20},{20,16},{24,28},{28,24},{1,5},{5... | collective-permute-start | bytes 3538952 | tf_op jit(solution)/shard_map/ppermute | solution.py:39
  288.7 13.8 %collective-permute-start.29 = (bf16[256,1152]{1,0:T(8,128)(2,1)S(1)}, bf16[256,1152]{1,0:T(8,128)(2,1)S(1)}, u32[]{:S(2)}, u32[]{:S(2)}) collective-permute-start(bf16[256,1152]{1,0:T(8,128)(2,1)S(1)} %slice.186), channel_id=1, source_target_pairs={{0,4},{4,0},{8,12},{12,8},{16,20},{20,16},{24,28},{28,24},{1,5},{5... | collective-permute-start | bytes 1769480 | tf_op jit(solution)/shard_map/ppermute | solution.py:39
  291.0 11.6 %collective-permute-start.31 = (bf16[256,1152]{1,0:T(8,128)(2,1)S(1)}, bf16[256,1152]{1,0:T(8,128)(2,1)S(1)}, u32[]{:S(2)}, u32[]{:S(2)}) collective-permute-start(bf16[256,1152]{1,0:T(8,128)(2,1)S(1)} %slice.187), channel_id=1, source_target_pairs={{0,2},{1,3},{2,0},{3,1},{4,6},{5,7},{6,4},{7,5},{8,10},{9,11},{10,... | collective-permute-start | bytes 1769480 | tf_op jit(solution)/shard_map/ppermute | solution.py:21
  331.1 26.5 %collective-permute-start.36 = (bf16[2048,1152]{1,0:T(8,128)(2,1)}, bf16[2048,1152]{1,0:T(8,128)(2,1)}, u32[]{:S(2)}, u32[]{:S(2)}) collective-permute-start(bf16[2048,1152]{1,0:T(8,128)(2,1)} %get-tuple-element.134), channel_id=1, source_target_pairs={{0,1},{1,0},{2,3},{3,2},{4,5},{5,4},{6,7},{7,6},{8,9},{9,8},{10,11... | collective-permute-start | bytes 14155784 | tf_op jit(solution)/shard_map/ppermute | solution.py:21
  360.8 16.4 %collective-permute-start.37 = (bf16[256,1152]{1,0:T(8,128)(2,1)}, bf16[256,1152]{1,0:T(8,128)(2,1)}, u32[]{:S(2)}, u32[]{:S(2)}) collective-permute-start(bf16[256,1152]{1,0:T(8,128)(2,1)} %get-tuple-element.221), channel_id=1, source_target_pairs={{0,4},{4,0},{8,12},{12,8},{16,20},{20,16},{24,28},{28,24},{1,5},{5... | collective-permute-start | bytes 1769480 | tf_op jit(solution)/shard_map/ppermute | solution.py:39
  362.2 15.6 %collective-permute-start.38 = (bf16[256,1152]{1,0:T(8,128)(2,1)}, bf16[256,1152]{1,0:T(8,128)(2,1)}, u32[]{:S(2)}, u32[]{:S(2)}) collective-permute-start(bf16[256,1152]{1,0:T(8,128)(2,1)} %get-tuple-element.220), channel_id=1, source_target_pairs={{0,2},{1,3},{2,0},{3,1},{4,6},{5,7},{6,4},{7,5},{8,10},{9,11},{10,... | collective-permute-start | bytes 1769480 | tf_op jit(solution)/shard_map/ppermute | solution.py:21
  382.1 149.6 %reduce-scatter.6.cloned.1.call-start = ((), (), s32[]{:S(2)}) async-start(), calls=%async_computation.7 | async-start | bytes 2580480 | tf_op jit(solution)/shard_map/reduce_scatter | solution.py:51
  385.0 20.4 %collective-permute-start.39 = (bf16[256,1152]{1,0:T(8,128)(2,1)}, bf16[256,1152]{1,0:T(8,128)(2,1)}, u32[]{:S(2)}, u32[]{:S(2)}) collective-permute-start(bf16[256,1152]{1,0:T(8,128)(2,1)} %get-tuple-element.218), channel_id=1, source_target_pairs={{0,4},{4,0},{8,12},{12,8},{16,20},{20,16},{24,28},{28,24},{1,5},{5... | collective-permute-start | bytes 1769480 | tf_op jit(solution)/shard_map/ppermute | solution.py:39
  386.9 18.5 %collective-permute-start.40 = (bf16[256,1152]{1,0:T(8,128)(2,1)}, bf16[256,1152]{1,0:T(8,128)(2,1)}, u32[]{:S(2)}, u32[]{:S(2)}) collective-permute-start(bf16[256,1152]{1,0:T(8,128)(2,1)} %get-tuple-element.216), channel_id=1, source_target_pairs={{0,2},{1,3},{2,0},{3,1},{4,6},{5,7},{6,4},{7,5},{8,10},{9,11},{10,... | collective-permute-start | bytes 1769480 | tf_op jit(solution)/shard_map/ppermute | solution.py:21
  388.2 39.0 %collective-permute-start.41 = (bf16[256,1152]{1,0:T(8,128)(2,1)}, bf16[256,1152]{1,0:T(8,128)(2,1)}, u32[]{:S(2)}, u32[]{:S(2)}) collective-permute-start(bf16[256,1152]{1,0:T(8,128)(2,1)} %get-tuple-element.219), channel_id=1, source_target_pairs={{0,4},{4,0},{8,12},{12,8},{16,20},{20,16},{24,28},{28,24},{1,5},{5... | collective-permute-start | bytes 1769480 | tf_op jit(solution)/shard_map/ppermute | solution.py:39
  388.9 38.3 %collective-permute-start.42 = (bf16[256,1152]{1,0:T(8,128)(2,1)}, bf16[256,1152]{1,0:T(8,128)(2,1)}, u32[]{:S(2)}, u32[]{:S(2)}) collective-permute-start(bf16[256,1152]{1,0:T(8,128)(2,1)} %get-tuple-element.217), channel_id=1, source_target_pairs={{0,2},{1,3},{2,0},{3,1},{4,6},{5,7},{6,4},{7,5},{8,10},{9,11},{10,... | collective-permute-start | bytes 1769480 | tf_op jit(solution)/shard_map/ppermute | solution.py:21
  416.1 122.3 %reduce-scatter.8.cloned.1.call-start = ((), (), s32[]{:S(2)}) async-start(), calls=%async_computation.8 | async-start | bytes 2580480 | tf_op jit(solution)/shard_map/reduce_scatter | solution.py:51
  451.5 11.2 %collective-permute-start.47 = (bf16[4,2,2,32,1152]{4,3,0,2,1:T(8,128)(2,1)}, bf16[4,2,2,32,1152]{4,3,0,2,1:T(8,128)(2,1)}, u32[]{:S(2)}, u32[]{:S(2)}) collective-permute-start(bf16[4,2,2,32,1152]{4,3,0,2,1:T(8,128)(2,1)} %bitcast.176), channel_id=1, source_target_pairs={{0,1},{1,0},{2,3},{3,2},{4,5},{5,4},{6,7},{7,6},{8,9},{9,8},{10,11... | collective-permute-start | bytes 3538952 | tf_op jit(solution)/shard_map/ppermute | solution.py:21
  456.1 12.3 %collective-permute-start.44 = (bf16[2,256,512]{2,1,0:T(8,128)(2,1)S(1)}, bf16[2,256,512]{2,1,0:T(8,128)(2,1)S(1)}, u32[]{:S(2)}, u32[]{:S(2)}) collective-permute-start(bf16[2,256,512]{2,1,0:T(8,128)(2,1)S(1)} %get-tuple-element.176), channel_id=1, source_target_pairs={{1,0},{2,1},{3,2},{5,4},{6,5},{7,6},{9,8},{10,9},{11,10},{13,12},{... | collective-permute-start | bytes 1572872 | tf_op jit(solution)/shard_map/ppermute | solution.py:27
  457.4 20.8 %collective-permute-start.45 = (bf16[2,256,512]{2,1,0:T(8,128)(2,1)S(1)}, bf16[2,256,512]{2,1,0:T(8,128)(2,1)}, u32[]{:S(2)}, u32[]{:S(2)}) collective-permute-start(bf16[2,256,512]{2,1,0:T(8,128)(2,1)S(1)} %get-tuple-element.177), channel_id=1, source_target_pairs={{2,0},{3,1},{6,4},{7,5},{10,8},{11,9},{14,12},{15,13},{18,16},{19,... | collective-permute-start | bytes 1572872 | tf_op jit(solution)/shard_map/ppermute | solution.py:27
  464.5 16.2 %collective-permute-start.48 = (bf16[4,2,32,1152]{3,2,0,1:T(8,128)(2,1)S(1)}, bf16[4,2,32,1152]{3,2,0,1:T(8,128)(2,1)S(1)}, u32[]{:S(2)}, u32[]{:S(2)}) collective-permute-start(bf16[4,2,32,1152]{3,2,0,1:T(8,128)(2,1)S(1)} %fusion.24), channel_id=1, source_target_pairs={{0,4},{4,0},{8,12},{12,8},{16,20},{20,16},{24,28},{28,24},{1,5},{5... | collective-permute-start | bytes 1769480 | tf_op jit(solution)/shard_map/ppermute | solution.py:39
  466.9 26.5 %collective-permute-start.46 = (bf16[4,2,32,1152]{3,2,0,1:T(8,128)(2,1)S(1)}, bf16[4,2,32,1152]{3,2,0,1:T(8,128)(2,1)S(1)}, u32[]{:S(2)}, u32[]{:S(2)}) collective-permute-start(bf16[4,2,32,1152]{3,2,0,1:T(8,128)(2,1)S(1)} %fusion.23), channel_id=1, source_target_pairs={{0,4},{4,0},{8,12},{12,8},{16,20},{20,16},{24,28},{28,24},{1,5},{5... | collective-permute-start | bytes 1769480 | tf_op jit(solution)/shard_map/ppermute | solution.py:39
  496.2 20.4 %collective-permute-start.52 = (bf16[4,32,1152]{2,1,0:T(8,128)(2,1)S(1)}, bf16[4,32,1152]{2,1,0:T(8,128)(2,1)S(1)}, u32[]{:S(2)}, u32[]{:S(2)}) collective-permute-start(bf16[4,32,1152]{2,1,0:T(8,128)(2,1)S(1)} %fusion.42), channel_id=1, source_target_pairs={{0,2},{1,3},{2,0},{3,1},{4,6},{5,7},{6,4},{7,5},{8,10},{9,11},{10,... | collective-permute-start | bytes 884744 | tf_op jit(solution)/shard_map/ppermute | solution.py:21
  533.8 13.5 %collective-permute-start.53 = (bf16[80,1152]{1,0:T(8,128)(2,1)S(1)}, bf16[80,1152]{1,0:T(8,128)(2,1)S(1)}, u32[]{:S(2)}, u32[]{:S(2)}) collective-permute-start(bf16[80,1152]{1,0:T(8,128)(2,1)S(1)} %get-tuple-element.210), channel_id=1, source_target_pairs={{0,16},{4,20},{8,24},{12,28},{16,0},{20,4},{24,8},{28,12},{1,17},{... | collective-permute-start | bytes 552968 | tf_op jit(solution)/shard_map/ppermute | solution.py:35
  535.0 12.3 %collective-permute-start.54 = (bf16[80,1152]{1,0:T(8,128)(2,1)S(1)}, bf16[80,1152]{1,0:T(8,128)(2,1)S(1)}, u32[]{:S(2)}, u32[]{:S(2)}) collective-permute-start(bf16[80,1152]{1,0:T(8,128)(2,1)S(1)} %get-tuple-element.211), channel_id=1, source_target_pairs={{0,24},{4,28},{8,0},{12,4},{16,8},{20,12},{24,16},{28,20},{1,25},{... | collective-permute-start | bytes 552968 | tf_op jit(solution)/shard_map/ppermute | solution.py:35
  538.4 11.2 %collective-permute-start.55 = (bf16[80,1152]{1,0:T(8,128)(2,1)S(1)}, bf16[80,1152]{1,0:T(8,128)(2,1)S(1)}, u32[]{:S(2)}, u32[]{:S(2)}) collective-permute-start(bf16[80,1152]{1,0:T(8,128)(2,1)S(1)} %get-tuple-element.212), channel_id=1, source_target_pairs={{0,8},{4,12},{8,16},{12,20},{16,24},{20,28},{24,0},{28,4},{1,9},{5... | collective-permute-start | bytes 552968 | tf_op jit(solution)/shard_map/ppermute | solution.py:35
  (116 other events, 1077.7 us)
Sparse Core Ops, SparseCore 0:
  10.2 55.2 all-gather.3
  67.6 44.8 all-gather.5
  114.1 47.4 all-gather.7
  382.2 41.6 reduce-scatter.3
  426.2 42.4 reduce-scatter.5
  470.8 42.4 reduce-scatter.7
